TPU v7x, 32 devices: a whole 2x2x4 slice. The times are simulated.
32 devices in a mesh: seq: 8 (over y, x, core), fsdp: 4 (over z).
Axes of the slice: x: 2, y: 2, z: 4, core: 2. Of those that a mesh axis runs over, the one named last changes fastest.
Arguments:
- tokens_in: bfloat16 [8, 1024, 2048], P('fsdp', 'seq'), may hold values from -6 to 6
- segments: int32 [8, 1024], P('fsdp'), may hold values from 0 to 2, as said below
- routes: int32 [8, 1024, 6], P('fsdp', 'seq'), may hold values from 0 to 15, all different within a row; in each aligned block of 128 rows (0 to 127, 128 to 255, ..., all dimensions but the last counted through in order) at most 64 rows name the same one
- cotangent: bfloat16 [8, 1024, 2048], P('fsdp', 'seq'), may hold values from -6 to 6
- g_attn: bfloat16 [2048], P(('seq', 'fsdp')), may hold values from 0.5 to 1.5
- g_kv: bfloat16 [512], P(('seq', 'fsdp')), may hold values from 0.5 to 1.5
- g_moe: bfloat16 [2048], P(('seq', 'fsdp')), may hold values from 0.5 to 1.5
- w_query: bfloat16 [2048, 3072], P(('seq', 'fsdp')), may hold values from -0.125 to 0.125
- w_kv_down: bfloat16 [2048, 576], P(('seq', 'fsdp')), may hold values from -0.125 to 0.125
- w_kv_up: bfloat16 [512, 4096], P(None, ('seq', 'fsdp')), may hold values from -0.25 to 0.25
- w_out: bfloat16 [2048, 2048], P(None, ('seq', 'fsdp')), may hold values from -0.5 to 0.5
- w_router: bfloat16 [2048, 16], P(('seq', 'fsdp')), may hold values from -0.0625 to 0.0625
- w_shared_gate: bfloat16 [2048, 2816], P(('seq', 'fsdp')), may hold values from -0.125 to 0.125
- w_shared_up: bfloat16 [2048, 2816], P(('seq', 'fsdp')), may hold values from -0.125 to 0.125
- w_shared_down: bfloat16 [2816, 2048], P(None, ('seq', 'fsdp')), may hold values from -0.109375 to 0.109375
- w_expert_gate: bfloat16 [32, 2048, 704], P(('seq', 'fsdp')), may hold values from -0.125 to 0.125
- w_expert_up: bfloat16 [32, 2048, 704], P(('seq', 'fsdp')), may hold values from -0.125 to 0.125
- w_expert_down: bfloat16 [32, 704, 2048], P(('seq', 'fsdp')), may hold values from -6 to 6
Outputs:
- output: bfloat16 [8, 1024, 2048], P('fsdp', 'seq')
- input_grad: float32 [8, 1024, 2048], P('fsdp', 'seq')
- grad_g_attn: float32 [2048], P(('seq', 'fsdp'))
- grad_g_kv: float32 [512], P(('seq', 'fsdp'))
- grad_g_moe: float32 [2048], P(('seq', 'fsdp'))
- grad_query: float32 [2048, 3072], P(('seq', 'fsdp'))
- grad_kv_down: float32 [2048, 576], P(('seq', 'fsdp'))
- grad_kv_up: float32 [512, 4096], P(None, ('seq', 'fsdp'))
- grad_out: float32 [2048, 2048], P(None, ('seq', 'fsdp'))
- grad_router: float32 [2048, 16], P(('seq', 'fsdp'))
- grad_shared_gate: float32 [2048, 2816], P(('seq', 'fsdp'))
- grad_shared_up: float32 [2048, 2816], P(('seq', 'fsdp'))
- grad_shared_down: float32 [2816, 2048], P(None, ('seq', 'fsdp'))
- grad_expert_gate: float32 [32, 2048, 704], P(('seq', 'fsdp'))
- grad_expert_up: float32 [32, 2048, 704], P(('seq', 'fsdp'))
- grad_expert_down: float32 [32, 704, 2048], P(('seq', 'fsdp'))
Inputs may be any that keep to these rules, and one draw needn't show every extreme that they name: `segments`: along each sequence the numbers start at 0 and never fall; of the 2 sequences of each index of fsdp, one, drawn from the seed, is a single document numbered 0; each other sequence has three documents, numbered 0, 1 and 2, the first two of 33 to 400 tokens each and the third holding the rest. `routes`: a token's 6 experts differ; within the 128 tokens of one sequence on one device of seq, no expert is named more than 64 times, a bound that some block reaches.
All inputs are finite; a program needn't handle non-finite values.
Results may differ from a plain program's by a relative error of at most 0.023.
Values may be sent and summed in bfloat16 or wider, within the bound.
No kernel may reach another device: no remote copies, remote signals or barrier semaphores. Data moves between devices by JAX's collectives and lax.ppermute only.
A program may use at most 448 MiB of HBM per device.

v0:
```python
import jax
import jax.numpy as jnp
from jax import lax
from jax.sharding import PartitionSpec as P

HEADS = 16
NOPE = 128
ROPE = 64
VDIM = 128
KVR = 512


EPS = 1e-06
THETA = 10000.0
NEGATIVE = -1e30
HIGHEST = lax.Precision.HIGHEST


def product(left, right):
    return jnp.dot(left, right, preferred_element_type=jnp.float32)


def left_product_input(left, right):
    return lax.dot_general(
        left, right, (((0,), (0,)), ((), ())), preferred_element_type=jnp.float32
    )


def right_product_input(left, right):
    return lax.dot_general(
        left, right, (((1,), (1,)), ((), ())), preferred_element_type=jnp.float32
    )


def left_exact(left, right):
    return lax.dot_general(
        left, right, (((0,), (0,)), ((), ())), precision=HIGHEST, preferred_element_type=jnp.float32
    )


def right_exact(left, right):
    return lax.dot_general(
        left, right, (((1,), (1,)), ((), ())), precision=HIGHEST, preferred_element_type=jnp.float32
    )


def normed(value):
    factor = lax.rsqrt(jnp.mean(value * value, axis=-1, keepdims=True) + EPS)
    return (value * factor, factor)


def norm_back(grad_unit, unit, factor):
    return factor * (grad_unit - unit * jnp.mean(grad_unit * unit, axis=-1, keepdims=True))


def rotate(value, angles):
    middle = value.shape[-1] // 2
    cosine = jnp.cos(angles)
    sine = jnp.sin(angles)
    first = value[..., :middle]
    second = value[..., middle:]
    return jnp.concatenate(
        [first * cosine - second * sine, second * cosine + first * sine], axis=-1
    )


def silu_parts(value):
    logistic = jax.nn.sigmoid(value)
    return (value * logistic, logistic * (1.0 + value * (1.0 - logistic)))


def score_block(query, keys_nope, keys_rope, allowed, factor):
    plain = jnp.einsum(
        "qhd,khd->hqk", query[..., :NOPE], keys_nope, preferred_element_type=jnp.float32
    )
    turned = jnp.einsum(
        "qhd,kd->hqk", query[..., NOPE:], keys_rope, preferred_element_type=jnp.float32
    )
    return jnp.where(allowed[None], (plain + turned) * factor, NEGATIVE)


def per_device(
    tokens_in,
    segments,
    routes,
    cotangent,
    g_attn,
    g_kv,
    g_moe,
    w_query,
    w_kv_down,
    w_kv_up,
    w_out,
    w_router,
    w_shared_gate,
    w_shared_up,
    w_shared_down,
    w_expert_gate,
    w_expert_up,
    w_expert_down,
):
    micro_count, local_rows, width = tokens_in.shape
    length = local_rows * lax.axis_size("seq")
    devices = lax.axis_size(("seq", "fsdp"))
    experts = devices // 2
    picked = routes.shape[2]
    capacity = max(2, local_rows * picked * 4 // (experts * 3))
    start = lax.axis_index("seq") * local_rows
    factor = (NOPE + ROPE) ** (-0.5)
    frequency = THETA ** (-jnp.arange(ROPE // 2, dtype=jnp.float32) * 2.0 / ROPE)
    own_places = start + jnp.arange(local_rows)
    all_places = jnp.arange(length)
    own_angles = own_places.astype(jnp.float32)[:, None] * frequency[None, :]
    expert_gate_output = w_expert_gate[0]
    expert_up_output = w_expert_up[0]
    expert_down = w_expert_down[0]
    expert_sum_totals = [
        jnp.zeros(expert_gate_output.shape, jnp.float32),
        jnp.zeros(expert_up_output.shape, jnp.float32),
        jnp.zeros(expert_down.shape, jnp.float32),
    ]
    accumulated = []
    outputs = []
    input_grads = []
    for micro_index in range(micro_count):
        forward_weights = (
            lax.all_gather(g_attn, ("seq", "fsdp"), axis=0, tiled=True),
            lax.all_gather(g_kv, ("seq", "fsdp"), axis=0, tiled=True),
            lax.all_gather(g_moe, ("seq", "fsdp"), axis=0, tiled=True),
            lax.all_gather(w_query, ("seq", "fsdp"), axis=0, tiled=True),
            lax.all_gather(w_kv_down, ("seq", "fsdp"), axis=0, tiled=True),
            lax.all_gather(w_kv_up, ("seq", "fsdp"), axis=1, tiled=True),
            lax.all_gather(w_out, ("seq", "fsdp"), axis=1, tiled=True),
            lax.all_gather(w_router, ("seq", "fsdp"), axis=0, tiled=True),
            lax.all_gather(w_shared_gate, ("seq", "fsdp"), axis=0, tiled=True),
            lax.all_gather(w_shared_up, ("seq", "fsdp"), axis=0, tiled=True),
            lax.all_gather(w_shared_down, ("seq", "fsdp"), axis=1, tiled=True),
        )
        if micro_index == 0:
            accumulated = [jnp.zeros(weight.shape, jnp.float32) for weight in forward_weights]
        (
            gain_one,
            gain_latent,
            gain_two,
            query_weight,
            down_weight,
            up_weight,
            out_weight,
            router_weight,
            shared_gate,
            shared_up,
            shared_down,
        ) = forward_weights
        inputs = tokens_in[micro_index].astype(jnp.float32)
        unit_one, factor_one = normed(inputs)
        normed_one = (unit_one * gain_one.astype(jnp.float32)).astype(jnp.bfloat16)
        query_raw = product(normed_one, query_weight).reshape(local_rows, HEADS, NOPE + ROPE)
        query = jnp.concatenate(
            [query_raw[..., :NOPE], rotate(query_raw[..., NOPE:], own_angles[:, None, :])], axis=-1
        ).astype(jnp.bfloat16)
        latent = product(normed_one, down_weight)
        unit_latent, factor_latent = normed(latent[:, :KVR])
        latent_norm = (unit_latent * gain_latent.astype(jnp.float32)).astype(jnp.bfloat16)
        key_rope = rotate(latent[:, KVR:], own_angles).astype(jnp.bfloat16)
        latent_all, rope_all = (
            lax.all_gather(latent_norm, "seq", axis=0, tiled=True),
            lax.all_gather(key_rope, "seq", axis=0, tiled=True),
        )
        key_value = product(latent_all, up_weight).astype(jnp.bfloat16)
        key_heads = key_value.reshape(length, HEADS, NOPE + VDIM)
        keys_nope = key_heads[..., :NOPE]
        values = key_heads[..., NOPE:]
        segment_all = segments[micro_index]
        segment_own = lax.dynamic_slice_in_dim(segment_all, start, local_rows)
        allowed = (segment_own[:, None] == segment_all[None, :]) & (
            all_places[None, :] <= own_places[:, None]
        )
        scores = score_block(query, keys_nope, rope_all, allowed, factor)
        largest = jnp.max(scores, axis=-1, keepdims=True)
        powers = jnp.exp(scores - largest)
        total = jnp.sum(powers, axis=-1, keepdims=True)
        log_total = largest + jnp.log(total)
        probs_low = (powers / total).astype(jnp.bfloat16)
        attended = (
            jnp.einsum("hqk,khd->qhd", probs_low, values, preferred_element_type=jnp.float32)
            .astype(jnp.bfloat16)
            .reshape(local_rows, HEADS * VDIM)
        )
        residual = inputs + product(attended, out_weight)
        unit_two, factor_two = normed(residual)
        normed_two = (unit_two * gain_two.astype(jnp.float32)).astype(jnp.bfloat16)
        logits = product(normed_two, router_weight)
        shifted = jnp.exp(logits - jnp.max(logits, axis=-1, keepdims=True))
        router = shifted / jnp.sum(shifted, axis=-1, keepdims=True)
        route_rows = routes[micro_index]
        choose = (route_rows[:, :, None] == jnp.arange(experts)[None, None, :]).astype(jnp.float32)
        gates = jnp.sum(choose * router[:, None, :], axis=-1)
        shared_gate_pre = product(normed_two, shared_gate)
        shared_up_pre = product(normed_two, shared_up)
        shared_silu, shared_slope = silu_parts(shared_gate_pre)
        shared_hidden = (shared_silu * shared_up_pre).astype(jnp.bfloat16)
        shared_out = product(shared_hidden, shared_down)
        expert_ids = route_rows.reshape(-1)
        marks = (expert_ids[:, None] == jnp.arange(experts)[None, :]).astype(jnp.int32)
        ranks = jnp.sum(jnp.cumsum(marks, axis=0) * marks, axis=1) - 1
        owners = jnp.arange(local_rows * picked) // picked
        slot_token = jnp.zeros((experts, capacity), jnp.int32).at[expert_ids, ranks].set(owners)
        slot_live = jnp.zeros((experts, capacity), jnp.bfloat16).at[expert_ids, ranks].set(1)
        gathered_rows = normed_two[slot_token] * slot_live[:, :, None]
        outgoing = jnp.broadcast_to(gathered_rows[:, None], (experts, 2, capacity, width)).reshape(
            devices, capacity, width
        )
        arrived = lax.all_to_all(outgoing, ("seq", "fsdp"), split_axis=0, concat_axis=0, tiled=True)
        received_token_rows = arrived.reshape(devices * capacity, width)
        expert_gate_pre = product(received_token_rows, expert_gate_output)
        expert_up_pre = product(received_token_rows, expert_up_output)
        expert_swish_activation, expert_slope = silu_parts(expert_gate_pre)
        expert_hidden = (expert_swish_activation * expert_up_pre).astype(jnp.bfloat16)
        halves_out = (
            product(expert_hidden, expert_down)
            .astype(jnp.bfloat16)
            .reshape(devices, capacity, width)
        )
        returned = lax.all_to_all(
            halves_out, ("seq", "fsdp"), split_axis=0, concat_axis=0, tiled=True
        ).reshape(experts, 2, capacity, width)
        merged = returned[:, 0].astype(jnp.float32) + returned[:, 1].astype(jnp.float32)
        route_out = merged[expert_ids, ranks].reshape(local_rows, picked, width)
        routed = jnp.sum(gates[:, :, None] * route_out, axis=1)
        outputs.append((residual + shared_out + routed).astype(jnp.bfloat16))
        backward_weights = (
            lax.all_gather(g_attn, ("seq", "fsdp"), axis=0, tiled=True),
            lax.all_gather(g_kv, ("seq", "fsdp"), axis=0, tiled=True),
            lax.all_gather(g_moe, ("seq", "fsdp"), axis=0, tiled=True),
            lax.all_gather(w_query, ("seq", "fsdp"), axis=0, tiled=True),
            lax.all_gather(w_kv_down, ("seq", "fsdp"), axis=0, tiled=True),
            lax.all_gather(w_kv_up, ("seq", "fsdp"), axis=1, tiled=True),
            lax.all_gather(w_out, ("seq", "fsdp"), axis=1, tiled=True),
            lax.all_gather(w_router, ("seq", "fsdp"), axis=0, tiled=True),
            lax.all_gather(w_shared_gate, ("seq", "fsdp"), axis=0, tiled=True),
            lax.all_gather(w_shared_up, ("seq", "fsdp"), axis=0, tiled=True),
            lax.all_gather(w_shared_down, ("seq", "fsdp"), axis=1, tiled=True),
        )
        (
            gain_one,
            gain_latent,
            gain_two,
            query_weight,
            down_weight,
            up_weight,
            out_weight,
            router_weight,
            shared_gate,
            shared_up,
            shared_down,
        ) = backward_weights
        grad_top = cotangent[micro_index]
        grad_output = grad_top.astype(jnp.float32)
        grad_gates = jnp.sum(grad_output[:, None, :] * route_out, axis=-1)
        grad_route = (
            (gates[:, :, None] * grad_output[:, None, :])
            .astype(jnp.bfloat16)
            .reshape(local_rows * picked, width)
        )
        grad_slots = (
            jnp.zeros((experts, capacity, width), jnp.bfloat16)
            .at[expert_ids, ranks]
            .set(grad_route)
        )
        grad_outgoing = jnp.broadcast_to(
            grad_slots[:, None], (experts, 2, capacity, width)
        ).reshape(devices, capacity, width)
        grad_arrived = lax.all_to_all(
            grad_outgoing, ("seq", "fsdp"), split_axis=0, concat_axis=0, tiled=True
        ).reshape(devices * capacity, width)
        expert_sum_totals[2] = expert_sum_totals[2] + left_product_input(
            expert_hidden, grad_arrived
        )
        expert_hidden_gradient = right_product_input(grad_arrived, expert_down)
        expert_gate_gradient = (expert_hidden_gradient * expert_up_pre * expert_slope).astype(
            jnp.bfloat16
        )
        expert_up_gradient = (expert_hidden_gradient * expert_swish_activation).astype(jnp.bfloat16)
        expert_sum_totals[0] = expert_sum_totals[0] + left_product_input(
            received_token_rows, expert_gate_gradient
        )
        expert_sum_totals[1] = expert_sum_totals[1] + left_product_input(
            received_token_rows, expert_up_gradient
        )
        row_gradients = right_product_input(
            expert_gate_gradient, expert_gate_output
        ) + right_product_input(expert_up_gradient, expert_up_output)
        grad_back = (
            lax.all_to_all(
                row_gradients.reshape(devices, capacity, width).astype(jnp.bfloat16),
                ("seq", "fsdp"),
                split_axis=0,
                concat_axis=0,
                tiled=True,
            )
            .astype(jnp.float32)
            .reshape(experts, 2, capacity, width)
        )
        grad_merged = grad_back[:, 0] + grad_back[:, 1]
        grad_normed_two = jnp.sum(
            grad_merged[expert_ids, ranks].reshape(local_rows, picked, width), axis=1
        )
        grad_router_in = jnp.sum(choose * grad_gates[:, :, None], axis=1)
        grad_logits = (
            router * (grad_router_in - jnp.sum(router * grad_router_in, axis=-1, keepdims=True))
        ).astype(jnp.bfloat16)
        accumulated[7] = accumulated[7] + left_product_input(normed_two, grad_logits)
        accumulated[10] = accumulated[10] + left_product_input(shared_hidden, grad_top)
        grad_shared_hidden = right_product_input(grad_top, shared_down)
        grad_sgate = (grad_shared_hidden * shared_up_pre * shared_slope).astype(jnp.bfloat16)
        grad_sup = (grad_shared_hidden * shared_silu).astype(jnp.bfloat16)
        accumulated[8] = accumulated[8] + left_product_input(normed_two, grad_sgate)
        accumulated[9] = accumulated[9] + left_product_input(normed_two, grad_sup)
        grad_normed_two = (
            grad_normed_two
            + right_product_input(grad_logits, router_weight)
            + right_product_input(grad_sgate, shared_gate)
            + right_product_input(grad_sup, shared_up)
        )
        accumulated[2] = accumulated[2] + jnp.sum(grad_normed_two * unit_two, axis=0)
        grad_residual = grad_output + norm_back(
            grad_normed_two * gain_two.astype(jnp.float32), unit_two, factor_two
        )
        grad_attn_out = grad_residual.astype(jnp.bfloat16)
        accumulated[6] = accumulated[6] + left_product_input(attended, grad_attn_out)
        grad_attended = (
            right_product_input(grad_attn_out, out_weight)
            .astype(jnp.bfloat16)
            .reshape(local_rows, HEADS, VDIM)
        )
        scores = score_block(query, keys_nope, rope_all, allowed, factor)
        probs_full = jnp.exp(scores - log_total)
        probs_low = probs_full.astype(jnp.bfloat16)
        grad_probs = jnp.einsum(
            "qhd,khd->hqk", grad_attended, values, preferred_element_type=jnp.float32
        )
        grad_values = jnp.einsum(
            "hqk,qhd->khd", probs_low, grad_attended, preferred_element_type=jnp.float32
        )
        grad_scores = (
            probs_full * (grad_probs - jnp.sum(probs_full * grad_probs, axis=-1, keepdims=True))
        ).astype(jnp.bfloat16)
        grad_query_nope = (
            jnp.einsum("hqk,khd->qhd", grad_scores, keys_nope, preferred_element_type=jnp.float32)
            * factor
        )
        grad_query_rope = (
            jnp.einsum("hqk,kd->qhd", grad_scores, rope_all, preferred_element_type=jnp.float32)
            * factor
        )
        grad_keys_nope = (
            jnp.einsum(
                "hqk,qhd->khd", grad_scores, query[..., :NOPE], preferred_element_type=jnp.float32
            )
            * factor
        )
        grad_keys_rope = (
            jnp.einsum(
                "hqk,qhd->kd", grad_scores, query[..., NOPE:], preferred_element_type=jnp.float32
            )
            * factor
        )
        grad_key_value_all = jnp.concatenate([grad_keys_nope, grad_values], axis=-1).reshape(
            length, HEADS * (NOPE + VDIM)
        )
        up_exact = up_weight.astype(jnp.float32)
        accumulated[5] = accumulated[5] + left_exact(
            latent_all.astype(jnp.float32), grad_key_value_all
        )
        partial_latent = right_exact(grad_key_value_all, up_exact)
        grad_latent_norm, grad_rope = (
            lax.psum_scatter(
                partial_latent.astype(jnp.bfloat16), "seq", scatter_dimension=0, tiled=True
            ).astype(jnp.float32),
            lax.psum_scatter(
                grad_keys_rope.astype(jnp.bfloat16), "seq", scatter_dimension=0, tiled=True
            ).astype(jnp.float32),
        )
        accumulated[1] = accumulated[1] + jnp.sum(grad_latent_norm * unit_latent, axis=0)
        grad_compressed = norm_back(
            grad_latent_norm * gain_latent.astype(jnp.float32), unit_latent, factor_latent
        )
        grad_latent = jnp.concatenate(
            [grad_compressed, rotate(grad_rope, -own_angles)], axis=-1
        ).astype(jnp.bfloat16)
        accumulated[4] = accumulated[4] + left_product_input(normed_one, grad_latent)
        grad_query_raw = (
            jnp.concatenate(
                [grad_query_nope, rotate(grad_query_rope, -own_angles[:, None, :])], axis=-1
            )
            .astype(jnp.bfloat16)
            .reshape(local_rows, HEADS * (NOPE + ROPE))
        )
        accumulated[3] = accumulated[3] + left_product_input(normed_one, grad_query_raw)
        grad_normed_one = right_product_input(grad_latent, down_weight) + right_product_input(
            grad_query_raw, query_weight
        )
        accumulated[0] = accumulated[0] + jnp.sum(grad_normed_one * unit_one, axis=0)
        input_grads.append(
            grad_residual
            + norm_back(grad_normed_one * gain_one.astype(jnp.float32), unit_one, factor_one)
        )
    reduced = (
        lax.psum_scatter(accumulated[0], ("seq", "fsdp"), scatter_dimension=0, tiled=True),
        lax.psum_scatter(accumulated[1], ("seq", "fsdp"), scatter_dimension=0, tiled=True),
        lax.psum_scatter(accumulated[2], ("seq", "fsdp"), scatter_dimension=0, tiled=True),
        lax.psum_scatter(accumulated[3], ("seq", "fsdp"), scatter_dimension=0, tiled=True),
        lax.psum_scatter(accumulated[4], ("seq", "fsdp"), scatter_dimension=0, tiled=True),
        lax.psum_scatter(accumulated[5], ("seq", "fsdp"), scatter_dimension=1, tiled=True),
        lax.psum_scatter(accumulated[6], ("seq", "fsdp"), scatter_dimension=1, tiled=True),
        lax.psum_scatter(accumulated[7], ("seq", "fsdp"), scatter_dimension=0, tiled=True),
        lax.psum_scatter(accumulated[8], ("seq", "fsdp"), scatter_dimension=0, tiled=True),
        lax.psum_scatter(accumulated[9], ("seq", "fsdp"), scatter_dimension=0, tiled=True),
        lax.psum_scatter(accumulated[10], ("seq", "fsdp"), scatter_dimension=1, tiled=True),
    )
    return (
        jnp.stack(outputs),
        jnp.stack(input_grads),
        reduced[0],
        reduced[1],
        reduced[2],
        reduced[3],
        reduced[4],
        reduced[5],
        reduced[6],
        reduced[7],
        reduced[8],
        reduced[9],
        reduced[10],
        expert_sum_totals[0][None],
        expert_sum_totals[1][None],
        expert_sum_totals[2][None],
    )


def solution(mesh):
    return jax.shard_map(
        per_device,
        mesh=mesh,
        in_specs=(
            P("fsdp", "seq", None),
            P("fsdp", None),
            P("fsdp", "seq", None),
            P("fsdp", "seq", None),
            P(("seq", "fsdp")),
            P(("seq", "fsdp")),
            P(("seq", "fsdp")),
            P(("seq", "fsdp"), None),
            P(("seq", "fsdp"), None),
            P(None, ("seq", "fsdp")),
            P(None, ("seq", "fsdp")),
            P(("seq", "fsdp"), None),
            P(("seq", "fsdp"), None),
            P(("seq", "fsdp"), None),
            P(None, ("seq", "fsdp")),
            P(("seq", "fsdp"), None, None),
            P(("seq", "fsdp"), None, None),
            P(("seq", "fsdp"), None, None),
        ),
        out_specs=(
            P("fsdp", "seq", None),
            P("fsdp", "seq", None),
            P(("seq", "fsdp")),
            P(("seq", "fsdp")),
            P(("seq", "fsdp")),
            P(("seq", "fsdp"), None),
            P(("seq", "fsdp"), None),
            P(None, ("seq", "fsdp")),
            P(None, ("seq", "fsdp")),
            P(("seq", "fsdp"), None),
            P(("seq", "fsdp"), None),
            P(("seq", "fsdp"), None),
            P(None, ("seq", "fsdp")),
            P(("seq", "fsdp"), None, None),
            P(("seq", "fsdp"), None, None),
            P(("seq", "fsdp"), None, None),
        ),
        check_vma=False,
    )
```

profile of v0, /device:TPU:0, one launch (start us, length us, event | category | flops | bytes accessed | tf_op | source)
XLA Modules:
  0.0 5303.6 jit_solution(17660771073228470210)
XLA Ops:
  10.6 42.2 all-reduce.7
  88.9 37.7 scatter_fusion
  127.3 37.9 scatter_fusion.1
  210.8 57.3 %all-gather.17.cloned.1.call-done = bf16[2048,3072]{1,0:T(8,128)(2,1)} async-done(((bf16[64,3072]{1,0:T(8,128)(2,1)}), bf16[2048,3072]{1,0:T(8,128)(2,1)}) %all-gather.17.cloned.1.call-update) | async-done | bytes 12582928 | tf_op jit(solution)/shard_map/all_gather | solution.py:130
  312.6 33.9 all-gather.19.cloned.1.call-done
  375.4 297.0 %all-gather = bf16[32,64,16]{1,2,0:T(8,128)(2,1)S(1)} all-gather(bf16[1,64,16]{1,2,0:T(8,128)(2,1)S(1)} %bitcast.492), channel_id=1, replica_groups=mesh['seq'=8,'fsdp'=4] {'seq','fsdp'}, dimensions={0}, use_global_device_ids=true | all-gather | bytes 67584 | tf_op jit(solution)/shard_map/all_gather | solution.py:134
  699.3 137.3 %scatter_fusion.4 = bf16[16,64,2048]{2,1,0:T(8,128)(2,1)} fusion(bf16[16,64,2048]{2,1,0:T(8,128)(2,1)} %broadcast.505.clone, s32[768]{0:T(1024)S(1)} %get-tuple-element.37, bf16[768,2048]{1,0:T(8,128)(2,1)} %multiply_convert_fusion.3), kind=kCustom, calls=%fused_computation.10 | custom fusion | bytes 9443328 | tf_op jit(solution)/shard_map/scatter | solution.py:268
  869.6 211.1 %all-to-all-done.4 = bf16[32,64,2048]{2,1,0:T(8,128)(2,1)} async-done(((bf16[32,64,2048]{2,1,0:T(8,128)(2,1)}), bf16[32,64,2048]{2,1,0:T(8,128)(2,1)}, u32[]{:S(2)}, u32[]{:S(2)}) %all-to-all-start.4) | async-done | bytes 8388640 | tf_op jit(solution)/shard_map/all_to_all | solution.py:273
  1140.2 207.4 %all-to-all-done.1 = bf16[32,64,2048]{2,1,0:T(8,128)(2,1)} async-done(((bf16[32,64,2048]{2,1,0:T(8,128)(2,1)}), bf16[32,64,2048]{2,1,0:T(8,128)(2,1)}, u32[]{:S(2)}, u32[]{:S(2)}) %all-to-all-start.1) | async-done | bytes 8388640 | tf_op jit(solution)/shard_map/all_to_all | solution.py:224
  1356.9 37.7 scatter_fusion.2
  1394.7 37.9 scatter_fusion.3
  1681.0 137.3 %scatter_fusion.5 = bf16[16,64,2048]{2,1,0:T(8,128)(2,1)} fusion(bf16[16,64,2048]{2,1,0:T(8,128)(2,1)} %broadcast.505, s32[768]{0:T(1024)S(1)} %copy-done.8, bf16[768,2048]{1,0:T(8,128)(2,1)} %multiply_convert_fusion.2), kind=kCustom, calls=%fused_computation.11 | custom fusion | bytes 9443328 | tf_op jit(solution)/shard_map/scatter | solution.py:268
  1876.9 160.2 %all-to-all-done.6 = bf16[32,64,2048]{2,1,0:T(8,128)(2,1)} async-done(((bf16[32,64,2048]{2,1,0:T(8,128)(2,1)}), bf16[32,64,2048]{2,1,0:T(8,128)(2,1)}, u32[]{:S(2)}, u32[]{:S(2)}) %all-to-all-start.6) | async-done | bytes 8388640 | tf_op jit(solution)/shard_map/all_to_all | solution.py:273
  2094.9 156.6 %all-to-all-done.3 = bf16[32,64,2048]{2,1,0:T(8,128)(2,1)} async-done(((bf16[32,64,2048]{2,1,0:T(8,128)(2,1)}), bf16[32,64,2048]{2,1,0:T(8,128)(2,1)}, u32[]{:S(2)}, u32[]{:S(2)}) %all-to-all-start.3) | async-done | bytes 8388640 | tf_op jit(solution)/shard_map/all_to_all | solution.py:224
  2329.8 111.7 %all-to-all-done.7 = bf16[32,64,2048]{2,1,0:T(8,128)(2,1)} async-done(((bf16[32,64,2048]{2,1,0:T(8,128)(2,1)}), bf16[32,64,2048]{2,1,0:T(8,128)(2,1)}, u32[]{:S(2)}, u32[]{:S(2)}) %all-to-all-start.7) | async-done | bytes 8388640 | tf_op jit(solution)/shard_map/all_to_all | solution.py:294
  2573.3 31.4 convolution_convert_fusion.7
  2675.2 37.9 reduce-scatter.41.cloned.1.call-done
  3005.6 42.5 all-reduce.6
  3054.6 446.1 %reduce-scatter.33.cloned.1.call-done = f32[64,2816]{1,0:T(8,128)} async-done(((f32[2048,2816]{1,0:T(8,128)}), f32[64,2816]{1,0:T(8,128)}) %reduce-scatter.33.cloned.1.call-update) | async-done | bytes 720912 | tf_op jit(solution)/shard_map/reduce_scatter | solution.py:418
  3500.8 495.9 %reduce-scatter.31.cloned.1.call-done = f32[64,2816]{1,0:T(8,128)} async-done(((f32[2048,2816]{1,0:T(8,128)}), f32[64,2816]{1,0:T(8,128)}) %reduce-scatter.31.cloned.1.call-update) | async-done | bytes 720912 | tf_op jit(solution)/shard_map/reduce_scatter | solution.py:417
  3996.7 496.0 %reduce-scatter.35.cloned.1.call-done = f32[2816,64]{0,1:T(8,128)} async-done(((f32[2816,2048]{0,1:T(8,128)}), f32[2816,64]{0,1:T(8,128)}) %reduce-scatter.35.cloned.1.call-update) | async-done | bytes 720912 | tf_op jit(solution)/shard_map/reduce_scatter | solution.py:419
  4492.6 187.5 %reduce-scatter.27.cloned.1.call-done = f32[512,128]{1,0:T(8,128)} async-done(((f32[512,4096]{1,0:T(8,128)}), f32[512,128]{1,0:T(8,128)}) %reduce-scatter.27.cloned.1.call-update) | async-done | bytes 262160 | tf_op jit(solution)/shard_map/reduce_scatter | solution.py:414
  4680.1 364.7 %reduce-scatter.29.cloned.1.call-done = f32[2048,64]{0,1:T(8,128)} async-done(((f32[2048,2048]{0,1:T(8,128)}), f32[2048,64]{0,1:T(8,128)}) %reduce-scatter.29.cloned.1.call-update) | async-done | bytes 524304 | tf_op jit(solution)/shard_map/reduce_scatter | solution.py:415
  5044.8 251.5 %reduce-scatter.23.cloned.1.call-done = f32[64,3072]{1,0:T(8,128)} async-done(((f32[2048,3072]{1,0:T(8,128)}), f32[64,3072]{1,0:T(8,128)}) %reduce-scatter.23.cloned.1.call-update) | async-done | bytes 786448 | tf_op jit(solution)/shard_map/reduce_scatter | solution.py:412
  (766 shorter events, 1229.3 us)
Async XLA Ops:
  8.0 169.0 %all-gather.13.cloned.1.call-start = ((), (), s32[]{:S(2)}) async-start(), calls=%async_computation.21 | async-start | bytes 1179648 | tf_op jit(solution)/shard_map/all_gather | solution.py:166
  80.3 187.8 %all-gather.17.cloned.1.call-start = ((), (), s32[]{:S(2)}) async-start(), calls=%async_computation.23 | async-start | bytes 12976128 | tf_op jit(solution)/shard_map/all_gather | solution.py:130
  80.8 265.7 %all-gather.19.cloned.1.call-start = ((), (), s32[]{:S(2)}) async-start(), calls=%async_computation.24 | async-start | bytes 8650752 | tf_op jit(solution)/shard_map/all_gather | solution.py:133
  81.4 1361.1 %all-gather.27.cloned.1.call-start = ((), (), s32[]{:S(2)}) async-start(), calls=%async_computation.28 | async-start | bytes 1179648 | tf_op jit(solution)/shard_map/all_gather | solution.py:166
  82.0 1393.9 %all-gather.25.cloned.1.call-start = ((), (), s32[]{:S(2)}) async-start(), calls=%async_computation.27 | async-start | bytes 11894784 | tf_op jit(solution)/shard_map/all_gather | solution.py:137
  371.6 465.1 %all-to-all-start = ((bf16[32,64,2048]{2,1,0:T(8,128)(2,1)}), bf16[32,64,2048]{2,1,0:T(8,128)(2,1)}, u32[]{:S(2)}, u32[]{:S(2)}) async-start(bf16[32,64,2048]{2,1,0:T(8,128)(2,1)} %bitcast.460), calls=%async_computation | async-start | bytes 16777216 | tf_op jit(solution)/shard_map/all_to_all | solution.py:213
  843.5 237.2 %all-to-all-start.4 = ((bf16[32,64,2048]{2,1,0:T(8,128)(2,1)}), bf16[32,64,2048]{2,1,0:T(8,128)(2,1)}, u32[]{:S(2)}, u32[]{:S(2)}) async-start(bf16[32,64,2048]{2,1,0:T(8,128)(2,1)} %bitcast.462), calls=%async_computation.4 | async-start | bytes 16777216 | tf_op jit(solution)/shard_map/all_to_all | solution.py:273
  847.2 658.7 %all-gather.23.cloned.1.call-start = ((), (), s32[]{:S(2)}) async-start(), calls=%async_computation.26 | async-start | bytes 11894784 | tf_op jit(solution)/shard_map/all_gather | solution.py:136
  1105.0 242.6 %all-to-all-start.1 = ((bf16[32,64,2048]{2,1,0:T(8,128)(2,1)}), bf16[32,64,2048]{2,1,0:T(8,128)(2,1)}, u32[]{:S(2)}, u32[]{:S(2)}) async-start(bf16[32,64,2048]{2,1,0:T(8,128)(2,1)} %bitcast.472), calls=%async_computation.1 | async-start | bytes 16777216 | tf_op jit(solution)/shard_map/all_to_all | solution.py:224
  1114.1 398.9 %all-gather.21.cloned.1.call-start = ((), (), s32[]{:S(2)}) async-start(), calls=%async_computation.25 | async-start | bytes 11894784 | tf_op jit(solution)/shard_map/all_gather | solution.py:135
  1347.6 227.8 %all-to-all-start.5 = ((bf16[32,64,2048]{2,1,0:T(8,128)(2,1)}), bf16[32,64,2048]{2,1,0:T(8,128)(2,1)}, u32[]{:S(2)}, u32[]{:S(2)}) async-start(bf16[32,64,2048]{2,1,0:T(8,128)(2,1)} %bitcast.470), calls=%async_computation.5 | async-start | bytes 16777216 | tf_op jit(solution)/shard_map/all_to_all | solution.py:294
  1650.8 189.2 %all-to-all-start.2 = ((bf16[32,64,2048]{2,1,0:T(8,128)(2,1)}), bf16[32,64,2048]{2,1,0:T(8,128)(2,1)}, u32[]{:S(2)}, u32[]{:S(2)}) async-start(bf16[32,64,2048]{2,1,0:T(8,128)(2,1)} %bitcast.461), calls=%async_computation.2 | async-start | bytes 16777216 | tf_op jit(solution)/shard_map/all_to_all | solution.py:213
  1846.9 190.2 %all-to-all-start.6 = ((bf16[32,64,2048]{2,1,0:T(8,128)(2,1)}), bf16[32,64,2048]{2,1,0:T(8,128)(2,1)}, u32[]{:S(2)}, u32[]{:S(2)}) async-start(bf16[32,64,2048]{2,1,0:T(8,128)(2,1)} %bitcast.463), calls=%async_computation.6 | async-start | bytes 16777216 | tf_op jit(solution)/shard_map/all_to_all | solution.py:273
  2061.5 190.0 %all-to-all-start.3 = ((bf16[32,64,2048]{2,1,0:T(8,128)(2,1)}), bf16[32,64,2048]{2,1,0:T(8,128)(2,1)}, u32[]{:S(2)}, u32[]{:S(2)}) async-start(bf16[32,64,2048]{2,1,0:T(8,128)(2,1)} %bitcast.473), calls=%async_computation.3 | async-start | bytes 16777216 | tf_op jit(solution)/shard_map/all_to_all | solution.py:224
  2251.5 190.0 %all-to-all-start.7 = ((bf16[32,64,2048]{2,1,0:T(8,128)(2,1)}), bf16[32,64,2048]{2,1,0:T(8,128)(2,1)}, u32[]{:S(2)}, u32[]{:S(2)}) async-start(bf16[32,64,2048]{2,1,0:T(8,128)(2,1)} %bitcast.471), calls=%async_computation.7 | async-start | bytes 16777216 | tf_op jit(solution)/shard_map/all_to_all | solution.py:294
  2260.1 395.0 %reduce-scatter.43.cloned.1.call-start = ((), (), s32[]{:S(2)}) async-start(), calls=%async_computation.39 | async-start | bytes 294912
  2653.2 343.3 %reduce-scatter.45.cloned.1.call-start = ((), (), s32[]{:S(2)}) async-start(), calls=%async_computation.40 | async-start | bytes 1081344
  2655.0 399.6 %reduce-scatter.25.cloned.1.call-start = ((), (), s32[]{:S(2)}) async-start(), calls=%async_computation.30 | async-start | bytes 5406720 | tf_op jit(solution)/shard_map/reduce_scatter | solution.py:413
  2719.6 781.2 %reduce-scatter.33.cloned.1.call-start = ((), (), s32[]{:S(2)}) async-start(), calls=%async_computation.34 | async-start | bytes 23789568 | tf_op jit(solution)/shard_map/reduce_scatter | solution.py:418
  2744.1 1252.6 %reduce-scatter.31.cloned.1.call-start = ((), (), s32[]{:S(2)}) async-start(), calls=%async_computation.33 | async-start | bytes 23789568 | tf_op jit(solution)/shard_map/reduce_scatter | solution.py:417
  2769.5 1723.1 %reduce-scatter.35.cloned.1.call-start = ((), (), s32[]{:S(2)}) async-start(), calls=%async_computation.35 | async-start | bytes 23789568 | tf_op jit(solution)/shard_map/reduce_scatter | solution.py:419
  2795.5 1884.6 %reduce-scatter.27.cloned.1.call-start = ((), (), s32[]{:S(2)}) async-start(), calls=%async_computation.31 | async-start | bytes 8650752 | tf_op jit(solution)/shard_map/reduce_scatter | solution.py:414
  2832.8 2212.0 %reduce-scatter.29.cloned.1.call-start = ((), (), s32[]{:S(2)}) async-start(), calls=%async_computation.32 | async-start | bytes 17301504 | tf_op jit(solution)/shard_map/reduce_scatter | solution.py:415
  2856.1 2440.2 %reduce-scatter.23.cloned.1.call-start = ((), (), s32[]{:S(2)}) async-start(), calls=%async_computation.29 | async-start | bytes 25952256 | tf_op jit(solution)/shard_map/reduce_scatter | solution.py:412
  (224 other events, 9216.7 us)
Sparse Core Ops, SparseCore 0:
  10.9 60.7 all-gather.10
  79.6 22.4 all-gather.12
  105.0 65.9 all-gather.14
  173.8 94.2 all-gather.16
  270.8 75.6 all-gather.18
  348.8 22.1 all-gather.26
  373.9 197.5 all-gather.24
  850.9 191.6 all-gather.22
  1117.8 191.6 all-gather.20
  2559.3 37.4 reduce-scatter.42
  2600.6 33.5 reduce-scatter.38
  2637.3 36.0 reduce-scatter.36
  2677.1 35.9 reduce-scatter.40
  2715.2 135.2 reduce-scatter.44
  2853.4 150.8 reduce-scatter.24
  3007.1 493.6 reduce-scatter.32
  3503.6 493.0 reduce-scatter.30
  3999.5 493.0 reduce-scatter.34
  4495.6 184.4 reduce-scatter.26
  4682.9 361.8 reduce-scatter.28
  5052.9 243.3 reduce-scatter.22
where the time goes:
time: 5320 us; the launch traced here: 5300 us
  waiting for transfers between devices  3280 us (62%)
  local copies, waits for them, and re-layouts  699 us (13%)
  matrix products  679 us (13%)
  blocking collectives  401 us (8%)
  other arithmetic  169 us (3%)
  starting transfers between devices  60.6 us (1%)
    reduce_scatter x1, waiting for transfers between devices, per_device(): lax.psum_scatter(accumulated[10], ('seq', 'fsdp'), scatter_dimension=1, t...  496 us
    reduce_scatter x1, waiting for transfers between devices, per_device(): lax.psum_scatter(accumulated[8], ('seq', 'fsdp'), scatter_dimension=0, ti...  496 us
    reduce_scatter x1, waiting for transfers between devices, per_device(): lax.psum_scatter(accumulated[9], ('seq', 'fsdp'), scatter_dimension=0, ti...  446 us
    all_to_all x2, waiting for transfers between devices, per_device(): lax.all_to_all(grad_outgoing, ('seq', 'fsdp'), split_axis=0, concat_axis=...  371 us
    reduce_scatter x1, waiting for transfers between devices, per_device(): lax.psum_scatter(accumulated[6], ('seq', 'fsdp'), scatter_dimension=1, ti...  365 us
    all_to_all x2, waiting for transfers between devices, per_device(): lax.all_to_all(halves_out, ('seq', 'fsdp'), split_axis=0, concat_axis=0,...  364 us
    all_gather x1, blocking collectives, per_device(): lax.all_gather(w_router, ('seq', 'fsdp'), axis=0, tiled=True)  297 us
    scatter x2, local copies, waits for them, and re-layouts, per_device(): grad_slots = jnp.zeros((experts, capacity, width), jnp.bfloat16).at[exper...  275 us
  transfers between devices with their start and end apart: 29, of which 17 were waited for; matrix products, arithmetic and copies ran while one was open for 24% of the time, Pallas kernels for 0%

commit v1 on v0

v1 whole, which is shorter than its diff:
```python
import functools

import jax
import jax.numpy as jnp
from jax import lax
from jax.experimental import pallas as pl
from jax.experimental.pallas import tpu as pltpu
from jax.sharding import PartitionSpec as P

HEADS = 16
NOPE = 128
ROPE = 64
VDIM = 128
KVR = 512

EPS = 1e-06
THETA = 10000.0
NEGATIVE = -1e30
BOTH = ("seq", "fsdp")
VMEM_LIMIT = 60 * 2**20
F32 = jnp.float32
BF16 = jnp.bfloat16


def product(left, right):
    return jnp.dot(left, right, preferred_element_type=F32)


def left_product(left, right):
    return lax.dot_general(left, right, (((0,), (0,)), ((), ())), preferred_element_type=F32)


def right_product(left, right):
    return lax.dot_general(left, right, (((1,), (1,)), ((), ())), preferred_element_type=F32)


def normed(value):
    factor = lax.rsqrt(jnp.mean(value * value, axis=-1, keepdims=True) + EPS)
    return (value * factor, factor)


def norm_back(grad_unit, unit, factor):
    return factor * (grad_unit - unit * jnp.mean(grad_unit * unit, axis=-1, keepdims=True))


def rotate(value, angles):
    middle = value.shape[-1] // 2
    cosine = jnp.cos(angles)
    sine = jnp.sin(angles)
    first = value[..., :middle]
    second = value[..., middle:]
    return jnp.concatenate(
        [first * cosine - second * sine, second * cosine + first * sine], axis=-1
    )


def silu_parts(value):
    logistic = jax.nn.sigmoid(value)
    return (value * logistic, logistic * (1.0 + value * (1.0 - logistic)))


def halve(value, axis, bit):
    count = lax.axis_size("seq")
    keep = lax.index_in_dim(value, 0, axis, keepdims=False)
    send = lax.index_in_dim(value, 1, axis, keepdims=False)
    return add_pair(keep, lax.ppermute(send, "seq", [(i, i ^ (1 << bit)) for i in range(count)]))


def add_pair(left, right):
    return (left.astype(F32) + right.astype(F32)).astype(BF16)


def line_reduce(value, axis):
    count = lax.axis_size("fsdp")
    place = lax.axis_index("fsdp")

    def piece(index):
        return lax.dynamic_index_in_dim(
            value, jnp.clip(index, 0, count - 1), axis, keepdims=False
        )

    up = down = None
    for step in range(1, count):
        send_up = piece(place + count - step)
        send_down = piece(place - count + step)
        if up is not None:
            send_up = add_pair(send_up, up)
            send_down = add_pair(send_down, down)
        up = lax.ppermute(send_up, "fsdp", [(i, i + 1) for i in range(step)])
        down = lax.ppermute(send_down, "fsdp", [(i, i - 1) for i in range(count - step, count)])
    total = piece(place).astype(F32) + up.astype(F32) + down.astype(F32)
    return total.astype(BF16)


def cuts_of(width):
    unit = width // 8
    return (0, 3 * unit, 6 * unit, width)


def reduce_home(keeps, sends, rows):
    seqs, line = lax.axis_size("seq"), lax.axis_size("fsdp")
    bits = list(range(1, seqs.bit_length() - 1))
    orders = (
        bits[:1] + ["line"] + bits[1:],
        bits[::-1] + ["line"],
        ["line"] + bits[::-1],
    )
    results = []
    for order, keep, send in zip(orders, keeps, sends):
        got = lax.ppermute(send, "seq", [(i, i ^ 1) for i in range(seqs)])
        part = add_pair(keep, got).reshape((2,) * len(bits) + (line, rows, keep.shape[-1]))
        names = bits[::-1] + ["line"]
        for step in order:
            axis = names.index(step)
            part = line_reduce(part, axis) if step == "line" else halve(part, axis, step)
            names.pop(axis)
        results.append(part)
    return jnp.concatenate(results, axis=-1)


def one_hot(slots, capacity):
    rows = slots.shape[-1]
    return lax.broadcasted_iota(jnp.int32, (capacity, rows), 0) == slots


def hidden_kernel(
    blocks,
    capacity,
    experts,
    hidden,
    place_ref,
    slots_ref,
    tokens_ref,
    top_ref,
    wide_ref,
    shared_ref,
    gate_ref,
    up_ref,
    down_ref,
    taken_ref,
    taken_top_ref,
    hidden_ref,
    pre_ref,
    post_ref,
    shared_hidden_ref,
    shared_grad_ref,
    gate_grad_ref,
):
    rows = slots_ref.shape[-1]
    lanes = shared_ref.shape[-1]
    expert = place_ref[0]
    wide = jnp.dot(tokens_ref[...], wide_ref[...], preferred_element_type=F32)
    back = jnp.dot(top_ref[...], shared_ref[...], preferred_element_type=F32)
    first = wide[:, :lanes]
    second = wide[:, lanes:]
    silu, slope = silu_parts(first)
    shared_hidden_ref[...] = (silu * second).astype(BF16)
    shared_grad_ref[:, :lanes] = (back * second * slope).astype(BF16)
    shared_grad_ref[:, lanes:] = (back * silu).astype(BF16)
    lane = lax.broadcasted_iota(jnp.int32, first.shape, 1)
    logits = jnp.where((lane >= hidden) & (lane < hidden + experts), first, NEGATIVE)
    powers = jnp.exp(logits - jnp.max(logits, axis=-1, keepdims=True))
    total = jnp.sum(powers, axis=-1, keepdims=True)
    gates = jnp.sum(jnp.where(lane == hidden + expert, powers, 0.0), axis=-1, keepdims=True)
    gates = jnp.broadcast_to(gates / total, first.shape)
    slot_gates = []
    for block in range(blocks):
        chosen = one_hot(slots_ref[block], capacity)
        low = chosen.astype(BF16)
        own = pl.ds(block * rows, rows)
        there = pl.ds(block * capacity, capacity)
        taken_ref[there, :] = jnp.dot(
            low, tokens_ref[own, :], preferred_element_type=F32
        ).astype(BF16)
        taken_top_ref[there, :] = jnp.dot(
            low, top_ref[own, :], preferred_element_type=F32
        ).astype(BF16)
        slot_gates.append(
            jnp.dot(
                chosen.astype(F32),
                gates[block * rows : (block + 1) * rows],
                precision=lax.Precision.HIGHEST,
                preferred_element_type=F32,
            )[:, :1]
        )
    slot_gates = jnp.concatenate(slot_gates, axis=0)
    gate_pre = jnp.dot(taken_ref[...], gate_ref[...], preferred_element_type=F32)
    up_pre = jnp.dot(taken_ref[...], up_ref[...], preferred_element_type=F32)
    grad = jnp.dot(taken_top_ref[...], down_ref[...], preferred_element_type=F32)
    swish, slope = silu_parts(gate_pre)
    made = swish * up_pre
    hidden_ref[...] = (made * slot_gates).astype(BF16)
    slot_grads = jnp.sum(made * grad, axis=-1, keepdims=True)
    grad = grad * slot_gates
    pre_ref[...] = (grad * up_pre * slope).astype(BF16)
    post_ref[...] = (grad * swish).astype(BF16)
    for block in range(blocks):
        chosen = one_hot(slots_ref[block], capacity)
        gate_grad_ref[block] = jnp.sum(
            jnp.where(chosen, slot_grads[block * capacity : (block + 1) * capacity], 0.0),
            axis=0,
            keepdims=True,
        )


def whole_spec(array):
    return pl.BlockSpec(
        array.shape, lambda i, *_: (0,) * array.ndim, pipeline_mode=pl.Buffered(1)
    )


def hidden_stage(place, slots, tokens, top, weights, capacity, experts, hidden):
    wide_weight, shared_down, gate_weight, up_weight, down_weight = weights
    devices, _, rows = slots.shape
    blocks = 2 * lax.axis_size("fsdp")
    steps = devices // blocks
    width = tokens.shape[1]
    half = gate_weight.shape[1]
    lanes = shared_down.shape[1]
    count = blocks * capacity

    def rows_spec(size, columns):
        return pl.BlockSpec((size, columns), lambda i, *_: (i, 0))

    slots_spec = pl.BlockSpec((blocks, 1, rows), lambda i, *_: (i, 0, 0))
    flops = devices * 2 * (3 * capacity * width * half + rows * width * 3 * lanes)
    return pl.pallas_call(
        functools.partial(hidden_kernel, blocks, capacity, experts, hidden),
        grid_spec=pltpu.PrefetchScalarGridSpec(
            num_scalar_prefetch=1,
            grid=(steps,),
            in_specs=[
                slots_spec,
                rows_spec(blocks * rows, width),
                rows_spec(blocks * rows, width),
                *[whole_spec(weight) for weight in weights],
            ],
            out_specs=[
                rows_spec(count, width),
                rows_spec(count, width),
                rows_spec(count, half),
                rows_spec(count, half),
                rows_spec(count, half),
                rows_spec(blocks * rows, lanes),
                rows_spec(blocks * rows, 2 * lanes),
                slots_spec,
            ],
        ),
        out_shape=[
            jax.ShapeDtypeStruct((steps * count, width), BF16),
            jax.ShapeDtypeStruct((steps * count, width), BF16),
            jax.ShapeDtypeStruct((steps * count, half), BF16),
            jax.ShapeDtypeStruct((steps * count, half), BF16),
            jax.ShapeDtypeStruct((steps * count, half), BF16),
            jax.ShapeDtypeStruct((devices * rows, lanes), BF16),
            jax.ShapeDtypeStruct((devices * rows, 2 * lanes), BF16),
            jax.ShapeDtypeStruct(slots.shape, F32),
        ],
        compiler_params=pltpu.CompilerParams(vmem_limit_bytes=VMEM_LIMIT),
        cost_estimate=pl.CostEstimate(
            flops=flops, bytes_accessed=3 * devices * rows * width * 2, transcendentals=0
        ),
        name="hidden_stage",
    )(place, slots, tokens, top, *weights)


def combine_kernel(blocks, capacity, cuts, count, place_ref, slots_ref, *refs):
    lefts, rights = refs[:count], refs[count : 2 * count]
    shared_ref, shared_weight_ref = refs[2 * count : 2 * count + 2]
    outs = refs[2 * count + 2 : -1]
    rows_ref = refs[-1]
    rows = slots_ref.shape[-1]
    total = None
    for left, right in zip(lefts, rights):
        term = jnp.dot(left[...], right[...], preferred_element_type=F32)
        total = term if total is None else total + term
    rows_ref[...] = total.astype(BF16)
    half = blocks // 2
    for side in range(2):
        core = place_ref[1] ^ side
        for block in range(half):
            index = core * half + block
            chosen = one_hot(slots_ref[index], capacity).astype(BF16)
            there = pl.ds(pl.multiple_of(index * capacity, capacity), capacity)
            own = pl.ds(pl.multiple_of(index * rows, rows), rows)
            value = lax.dot_general(
                chosen,
                rows_ref[there, :],
                (((0,), (0,)), ((), ())),
                preferred_element_type=F32,
            ) + jnp.dot(
                shared_ref[own, :], shared_weight_ref[...], preferred_element_type=F32
            )
            value = value.astype(BF16)
            for part in range(3):
                outs[3 * side + part][pl.ds(block * rows, rows), :] = value[
                    :, cuts[part] : cuts[part + 1]
                ]


def combine_stage(place, slots, lefts, rights, shared, shared_weight, capacity):
    devices, _, rows = slots.shape
    blocks = 2 * lax.axis_size("fsdp")
    steps = devices // blocks
    width = rights[0].shape[1]
    cuts = cuts_of(width)
    half = blocks // 2 * rows

    def rows_spec(size, columns):
        return pl.BlockSpec((size, columns), lambda i, *_: (i, 0))

    out_specs = [
        pl.BlockSpec((half, high - low), lambda i, place: (i ^ place[2], 0))
        for _ in range(2)
        for low, high in zip(cuts[:-1], cuts[1:])
    ]
    out_shape = [
        jax.ShapeDtypeStruct((steps * half, high - low), BF16)
        for _ in range(2)
        for low, high in zip(cuts[:-1], cuts[1:])
    ]
    flops = 2 * devices * width * (
        capacity * sum(left.shape[1] for left in lefts) + rows * (capacity + shared.shape[1])
    )
    outs = pl.pallas_call(
        functools.partial(combine_kernel, blocks, capacity, cuts, len(lefts)),
        grid_spec=pltpu.PrefetchScalarGridSpec(
            num_scalar_prefetch=1,
            grid=(steps,),
            in_specs=[
                pl.BlockSpec((blocks, 1, rows), lambda i, *_: (i, 0, 0)),
                *[rows_spec(blocks * capacity, left.shape[1]) for left in lefts],
                *[whole_spec(right) for right in rights],
                rows_spec(blocks * rows, shared.shape[1]),
                whole_spec(shared_weight),
            ],
            out_specs=out_specs,
            scratch_shapes=[pltpu.VMEM((blocks * capacity, width), BF16)],
        ),
        out_shape=out_shape,
        compiler_params=pltpu.CompilerParams(vmem_limit_bytes=VMEM_LIMIT),
        cost_estimate=pl.CostEstimate(
            flops=flops, bytes_accessed=devices * rows * width * 3, transcendentals=0
        ),
        name="combine_stage",
    )(place, slots, *lefts, *rights, shared, shared_weight)
    return outs[:3], outs[3:]


def per_device(
    tokens_in,
    segments,
    routes,
    cotangent,
    g_attn,
    g_kv,
    g_moe,
    w_query,
    w_kv_down,
    w_kv_up,
    w_out,
    w_router,
    w_shared_gate,
    w_shared_up,
    w_shared_down,
    w_expert_gate,
    w_expert_up,
    w_expert_down,
):
    micro_count, rows, width = tokens_in.shape
    seqs, line = lax.axis_size("seq"), lax.axis_size("fsdp")
    devices = seqs * line
    length = rows * seqs
    experts = devices // 2
    picked = routes.shape[2]
    capacity = max(2, rows * picked * 4 // (experts * 3))
    capacity = -(-capacity // 16) * 16
    heads = HEADS // seqs
    me_seq = lax.axis_index("seq")
    me = me_seq * line + lax.axis_index("fsdp")
    expert = me // 2
    factor = (NOPE + ROPE) ** (-0.5)
    frequency = THETA ** (-jnp.arange(ROPE // 2, dtype=F32) * 2.0 / ROPE)
    places = jnp.arange(length)
    angles = places.astype(F32)[:, None] * frequency[None, :]
    own_angles = (me_seq * rows + jnp.arange(rows)).astype(F32)[:, None] * frequency[None, :]
    micros = range(micro_count)

    piece = w_kv_down.shape[0]
    kv_columns = w_kv_down.shape[1]
    small = jnp.concatenate(
        [
            w_kv_down,
            w_router,
            g_attn[:, None],
            g_moe[:, None],
            jnp.pad(g_kv, (0, piece - g_kv.shape[0]))[:, None],
            routes.reshape(piece, -1).astype(BF16),
        ],
        axis=1,
    )
    small = lax.all_gather(small, BOTH, axis=0, tiled=True)
    down_weight = small[:, :kv_columns]
    router_weight = small[:, kv_columns : kv_columns + experts]
    last = kv_columns + experts
    gain_one = small[:, last].astype(F32)
    gain_two = small[:, last + 1].astype(F32)
    gain_latent = small[:, last + 2].reshape(devices, piece)[:, : g_kv.shape[0]].reshape(-1)
    routes_all = small[:, last + 3 :].astype(jnp.int32).reshape((devices,) + routes.shape)
    gain_latent = gain_latent.astype(F32)

    query_width = heads * (NOPE + ROPE)
    out_width = heads * VDIM
    for_query = w_query.reshape(piece, seqs, query_width).transpose(1, 0, 2)
    for_out = w_out.reshape(seqs, out_width, piece).transpose(0, 2, 1)
    for_heads = jnp.concatenate([for_query, for_out], axis=2)
    for_heads = jnp.broadcast_to(
        for_heads[:, None], (seqs, line, piece, query_width + out_width)
    ).reshape(devices, piece, query_width + out_width)
    for_heads = lax.all_to_all(for_heads, BOTH, 0, 0, tiled=True)
    for_heads = for_heads.reshape(width, query_width + out_width)
    query_weight = for_heads[:, :query_width]
    out_weight = for_heads[:, query_width:]
    up_weight = lax.all_to_all(
        jnp.broadcast_to(w_kv_up[None], (line,) + w_kv_up.shape), "fsdp", 0, 0, tiled=True
    )
    up_weight = up_weight.transpose(1, 0, 2).reshape(KVR, -1)

    hidden = w_shared_gate.shape[1] // devices
    for_shared = jnp.concatenate(
        [
            w_shared_gate.reshape(piece, devices, hidden).transpose(1, 0, 2),
            w_shared_up.reshape(piece, devices, hidden).transpose(1, 0, 2),
            w_shared_down.reshape(devices, hidden, piece).transpose(0, 2, 1),
        ],
        axis=2,
    )
    for_shared = lax.all_to_all(for_shared, BOTH, 0, 0, tiled=True).reshape(width, 3 * hidden)
    lanes = -(-(hidden + experts) // 128) * 128

    def padded(parts):
        parts = jnp.concatenate(parts, axis=1)
        return jnp.pad(parts, ((0, 0), (0, lanes - parts.shape[1])))

    shared_gate = for_shared[:, :hidden]
    shared_up = for_shared[:, hidden : 2 * hidden]
    shared_down = padded([for_shared[:, 2 * hidden :]])
    wide_weight = jnp.concatenate(
        [padded([shared_gate, router_weight]), padded([shared_up])], axis=1
    )
    shared_in = jnp.concatenate([padded([shared_gate]), padded([shared_up])], axis=1)
    gate_weight = w_expert_gate[0]
    up_expert = w_expert_up[0]
    down_expert = w_expert_down[0]
    hidden_weights = (wide_weight, shared_down, gate_weight, up_expert, down_expert.T)
    place = jnp.stack([expert, me_seq & 1, me_seq >> 1]).astype(jnp.int32)

    attention = []
    residuals = []
    normed_alls = []
    top_alls = []
    tokens_all = [
        lax.all_gather(tokens_in[micro], "seq", axis=0, tiled=True) for micro in micros
    ]
    for micro in micros:
        unit_one, _ = normed(tokens_all[micro].astype(F32))
        normed_one = (unit_one * gain_one).astype(BF16)
        query_raw = product(normed_one, query_weight).reshape(length, heads, NOPE + ROPE)
        query = jnp.concatenate(
            [query_raw[..., :NOPE], rotate(query_raw[..., NOPE:], angles[:, None, :])], axis=-1
        ).astype(BF16)
        latent = product(normed_one, down_weight)
        unit_latent, _ = normed(latent[:, :KVR])
        latent_norm = (unit_latent * gain_latent).astype(BF16)
        key_rope = rotate(latent[:, KVR:], angles).astype(BF16)
        key_value = product(latent_norm, up_weight).astype(BF16)
        key_heads = key_value.reshape(length, heads, NOPE + VDIM)
        keys = jnp.concatenate(
            [
                key_heads[..., :NOPE],
                jnp.broadcast_to(key_rope[:, None, :], (length, heads, ROPE)),
            ],
            axis=-1,
        )
        values = key_heads[..., NOPE:]
        segment = segments[micro]
        allowed = (segment[:, None] == segment[None, :]) & (places[None, :] <= places[:, None])
        scores = jnp.einsum("qhd,khd->hqk", query, keys, preferred_element_type=F32) * factor
        scores = jnp.where(allowed[None], scores, NEGATIVE)
        largest = jnp.max(scores, axis=-1, keepdims=True)
        powers = jnp.exp(scores - largest)
        total = jnp.sum(powers, axis=-1, keepdims=True)
        log_total = largest + jnp.log(total)
        probs = (powers / total).astype(BF16)
        attended = (
            jnp.einsum("hqk,khd->qhd", probs, values, preferred_element_type=F32)
            .astype(BF16)
            .reshape(length, out_width)
        )
        out_part = right_product(attended, out_weight).astype(BF16)
        summed = lax.psum_scatter(out_part, "seq", scatter_dimension=0, tiled=True)
        residual = tokens_in[micro].astype(F32) + summed.astype(F32)
        unit_two, factor_two = normed(residual)
        normed_two = (unit_two * gain_two).astype(BF16)
        attention.append(
            (normed_one, latent_norm, query, keys, values, allowed, log_total, attended)
        )
        residuals.append((residual, unit_two, factor_two, normed_two))
        top_alls.append(lax.all_gather(cotangent[micro], BOTH, axis=0, tiled=True))
        normed_alls.append(lax.all_gather(normed_two, BOTH, axis=0, tiled=True))

    outputs = []
    grads_two = []
    gate_grads = []
    expert_grads = None
    for micro in micros:
        tokens_two = normed_alls[micro]
        top = top_alls[micro]
        hit = jnp.any(routes_all[:, micro] == expert, axis=-1)
        rank = jnp.cumsum(hit.astype(jnp.int32), axis=1) - 1
        slots = jnp.where(hit, rank, -1)[:, None, :]
        (
            taken,
            taken_top,
            hidden_gated,
            pre_grad,
            up_grad,
            shared_hidden,
            shared_pre_grad,
            gate_grad,
        ) = hidden_stage(
            place, slots, tokens_two, top, hidden_weights, capacity, experts, hidden
        )
        gate_grads.append(
            lax.all_to_all(gate_grad.reshape(devices, rows), BOTH, 0, 0, tiled=True)
        )
        keeps, sends = combine_stage(
            place,
            slots,
            (pre_grad, up_grad),
            (gate_weight.T, up_expert.T),
            shared_pre_grad,
            shared_in.T,
            capacity,
        )
        grads_two.append(reduce_home(keeps, sends, rows))
        keeps, sends = combine_stage(
            place, slots, (hidden_gated,), (down_expert,), shared_hidden, shared_down.T, capacity
        )
        outputs.append(
            (residuals[micro][0] + reduce_home(keeps, sends, rows).astype(F32)).astype(BF16)
        )
        grads = (
            left_product(taken, pre_grad),
            left_product(taken, up_grad),
            left_product(hidden_gated, taken_top),
            left_product(tokens_two, shared_pre_grad),
            left_product(top, shared_hidden),
        )
        expert_grads = (
            grads
            if expert_grads is None
            else tuple(old + new for old, new in zip(expert_grads, grads))
        )

    shared_grads = jnp.concatenate(
        [
            expert_grads[3][:, :hidden],
            expert_grads[3][:, lanes : lanes + hidden],
            expert_grads[4][:, :hidden],
        ],
        axis=1,
    ).astype(BF16)
    shared_grads = lax.all_to_all(
        shared_grads.reshape(devices, piece, 3 * hidden), BOTH, 0, 0, tiled=True
    ).astype(F32)
    grad_shared_gate = shared_grads[:, :, :hidden].transpose(1, 0, 2).reshape(piece, -1)
    grad_shared_up = shared_grads[:, :, hidden : 2 * hidden].transpose(1, 0, 2).reshape(piece, -1)
    grad_shared_down = shared_grads[:, :, 2 * hidden :].transpose(0, 2, 1).reshape(-1, piece)

    grad_gain_one = grad_gain_two = grad_gain_latent = grad_router = 0.0
    grad_heads = grad_up_weight = 0.0
    input_grads = []
    latent_grads = []
    for micro in micros:
        normed_one, latent_norm, query, keys, values, allowed, log_total, attended = attention[
            micro
        ]
        residual, unit_two, factor_two, normed_two = residuals[micro]
        logits = product(normed_two, router_weight)
        shifted = jnp.exp(logits - jnp.max(logits, axis=-1, keepdims=True))
        router = shifted / jnp.sum(shifted, axis=-1, keepdims=True)
        router_in = jnp.sum(gate_grads[micro].reshape(experts, 2, rows), axis=1).T
        grad_logits = (
            router * (router_in - jnp.sum(router * router_in, axis=-1, keepdims=True))
        ).astype(BF16)
        grad_router = grad_router + left_product(normed_two, grad_logits)
        grad_two = grads_two[micro].astype(F32) + right_product(grad_logits, router_weight)
        grad_gain_two = grad_gain_two + jnp.sum(grad_two * unit_two, axis=0)
        grad_residual = cotangent[micro].astype(F32) + norm_back(
            grad_two * gain_two, unit_two, factor_two
        )
        grad_attn_out = lax.all_gather(grad_residual.astype(BF16), "seq", axis=0, tiled=True)

        grad_attended = (
            product(grad_attn_out, out_weight).astype(BF16).reshape(length, heads, VDIM)
        )
        scores = jnp.einsum("qhd,khd->hqk", query, keys, preferred_element_type=F32) * factor
        probs_full = jnp.exp(jnp.where(allowed[None], scores, NEGATIVE) - log_total)
        probs = probs_full.astype(BF16)
        grad_probs = jnp.einsum("qhd,khd->hqk", grad_attended, values, preferred_element_type=F32)
        grad_values = jnp.einsum("hqk,qhd->khd", probs, grad_attended, preferred_element_type=F32)
        grad_scores = (
            probs_full * (grad_probs - jnp.sum(probs_full * grad_probs, axis=-1, keepdims=True))
        ).astype(BF16)
        grad_query = (
            jnp.einsum("hqk,khd->qhd", grad_scores, keys, preferred_element_type=F32) * factor
        )
        grad_keys = (
            jnp.einsum("hqk,qhd->khd", grad_scores, query, preferred_element_type=F32) * factor
        )
        grad_rope = jnp.sum(grad_keys[..., NOPE:], axis=1)
        grad_key_value = (
            jnp.concatenate([grad_keys[..., :NOPE], grad_values], axis=-1)
            .astype(BF16)
            .reshape(length, heads * (NOPE + VDIM))
        )
        grad_query_raw = (
            jnp.concatenate(
                [grad_query[..., :NOPE], rotate(grad_query[..., NOPE:], -angles[:, None, :])],
                axis=-1,
            )
            .astype(BF16)
            .reshape(length, query_width)
        )
        grad_one_part = right_product(grad_query_raw, query_weight)
        grad_latent_part = right_product(grad_key_value, up_weight)
        back = jnp.concatenate([grad_one_part, grad_latent_part, grad_rope], axis=1).astype(BF16)
        back = lax.psum_scatter(back, "seq", scatter_dimension=0, tiled=True).astype(F32)
        grad_heads = grad_heads + jnp.concatenate(
            [left_product(normed_one, grad_query_raw), left_product(grad_attn_out, attended)],
            axis=1,
        )
        grad_up_weight = grad_up_weight + left_product(grad_key_value, latent_norm)

        unit_one, factor_one = normed(tokens_in[micro].astype(F32))
        own_normed = (unit_one * gain_one).astype(BF16)
        latent = product(own_normed, down_weight)
        unit_latent, factor_latent = normed(latent[:, :KVR])
        grad_latent_norm = back[:, width : width + KVR]
        grad_gain_latent = grad_gain_latent + jnp.sum(grad_latent_norm * unit_latent, axis=0)
        grad_compressed = norm_back(grad_latent_norm * gain_latent, unit_latent, factor_latent)
        grad_latent = jnp.concatenate(
            [grad_compressed, rotate(back[:, width + KVR :], -own_angles)], axis=-1
        ).astype(BF16)
        latent_grads.append(grad_latent)
        grad_one = back[:, :width] + right_product(grad_latent, down_weight)
        grad_gain_one = grad_gain_one + jnp.sum(grad_one * unit_one, axis=0)
        input_grads.append(
            grad_residual + norm_back(grad_one * gain_one, unit_one, factor_one)
        )

    latents_all = lax.all_gather(jnp.concatenate(latent_grads, axis=1), "seq", axis=0, tiled=True)
    grad_down = 0.0
    for micro in micros:
        own_columns = lax.dynamic_slice_in_dim(
            attention[micro][0], me_seq * (width // seqs), width // seqs, axis=1
        )
        grad_down = grad_down + left_product(
            own_columns, latents_all[:, micro * kv_columns : (micro + 1) * kv_columns]
        )

    def sum_line(value):
        value = value.astype(BF16).reshape(line, -1, value.shape[-1])
        value = lax.all_to_all(value, "fsdp", 0, 0, tiled=True)
        return jnp.sum(value.astype(F32), axis=0)

    grad_kv_down = sum_line(grad_down)
    grad_kv_up = sum_line(grad_up_weight).T
    grad_heads = lax.all_to_all(
        grad_heads.astype(BF16).reshape(devices, piece, -1), BOTH, 0, 0, tiled=True
    )
    grad_heads = jnp.sum(grad_heads.reshape(seqs, line, piece, -1).astype(F32), axis=1)
    grad_query_weight = grad_heads[:, :, :query_width].transpose(1, 0, 2).reshape(piece, -1)
    grad_out_weight = grad_heads[:, :, query_width:].transpose(0, 2, 1).reshape(-1, piece)
    tiny = jnp.concatenate(
        [
            grad_router.reshape(devices, -1),
            grad_gain_one.reshape(devices, -1),
            grad_gain_two.reshape(devices, -1),
            grad_gain_latent.reshape(devices, -1),
        ],
        axis=1,
    )
    tiny = jnp.sum(lax.all_to_all(tiny, BOTH, 0, 0, tiled=True), axis=0)
    first = piece * experts
    return (
        jnp.stack(outputs),
        jnp.stack(input_grads),
        tiny[first : first + piece],
        tiny[first + 2 * piece :],
        tiny[first + piece : first + 2 * piece],
        grad_query_weight,
        grad_kv_down,
        grad_kv_up,
        grad_out_weight,
        tiny[:first].reshape(piece, experts),
        grad_shared_gate,
        grad_shared_up,
        grad_shared_down,
        expert_grads[0][None],
        expert_grads[1][None],
        expert_grads[2][None],
    )


def solution(mesh):
    return jax.shard_map(
        per_device,
        mesh=mesh,
        in_specs=(
            P("fsdp", "seq", None),
            P("fsdp", None),
            P("fsdp", "seq", None),
            P("fsdp", "seq", None),
            P(BOTH),
            P(BOTH),
            P(BOTH),
            P(BOTH, None),
            P(BOTH, None),
            P(None, BOTH),
            P(None, BOTH),
            P(BOTH, None),
            P(BOTH, None),
            P(BOTH, None),
            P(None, BOTH),
            P(BOTH, None, None),
            P(BOTH, None, None),
            P(BOTH, None, None),
        ),
        out_specs=(
            P("fsdp", "seq", None),
            P("fsdp", "seq", None),
            P(BOTH),
            P(BOTH),
            P(BOTH),
            P(BOTH, None),
            P(BOTH, None),
            P(None, BOTH),
            P(None, BOTH),
            P(BOTH, None),
            P(BOTH, None),
            P(BOTH, None),
            P(None, BOTH),
            P(BOTH, None, None),
            P(BOTH, None, None),
            P(BOTH, None, None),
        ),
        check_vma=False,
    )
```

time: 5320 us -> 1900 us (0.36)
  waiting for transfers between devices: 3280 us -> 872 us
  local copies, waits for them, and re-layouts: 699 us -> 149 us
  matrix products: 679 us -> 198 us
  blocking collectives: 401 us -> 0 us
  starting transfers between devices: 60.6 us -> 308 us
  Pallas kernels: 0 us -> 195 us
    reduce_scatter x7 -> x4, waiting for transfers between devices: 2240 us -> 86.6 us  [the longest x2 86.6 us: per_device(): summed = lax.psum_scatter(out_part, 'seq', scatter_dimension=0, tiled=True)]
    all_to_all x8 -> x10, waiting for transfers between devices: 869 us -> 65.2 us  [the longest x1 48.7 us: per_device(): lax.all_to_all(for_shared, BOTH, 0, 0, tiled=True)]
    dot_general x82 -> x52, matrix products: 661 us -> 188 us  [the longest x20 112 us: left_product(): lax.dot_general(left, right, (((0,), (0,)), ((), ())), preferred_element_...]
    scatter x6 -> x0, local copies, waits for them, and re-layouts: 426 us -> none  [the longest x2 275 us: per_device(): grad_slots = jnp.zeros((experts, capacity, width), jnp.bfloat16).at[exper...]
    all_gather x9 -> x10, waiting for transfers between devices: 109 us -> 431 us  [the longest x2 233 us: per_device(): normed_alls.append(lax.all_gather(normed_two, BOTH, axis=0, tiled=True))]
    all_gather x3 -> x0, blocking collectives: 316 us -> none  [the longest x1 297 us: per_device(): lax.all_gather(w_router, ('seq', 'fsdp'), axis=0, tiled=True)]
    ppermute x0 -> x108, waiting for transfers between devices: none -> 288 us  [the longest x24 155 us: halve(): lax.ppermute(send, 'seq', [(i, i ^ 1 << bit) for i in range(count)])]
    ppermute x0 -> x108, starting transfers between devices: none -> 253 us  [the longest x36 193 us: line_reduce(): up = lax.ppermute(send_up, 'fsdp', [(i, i + 1) for i in range(step)])]
  transfers between devices with their start and end apart: 29 -> 132, of which waited for: 17 -> 54; matrix products, arithmetic and copies ran while one was open for 24% -> 24% of each run, Pallas kernels for 0% -> 10%
where the time goes in v1:
time: 1900 us; the launch traced here: 1890 us
  waiting for transfers between devices  872 us (46%)
  starting transfers between devices  308 us (16%)
  matrix products  198 us (10%)
  Pallas kernels  195 us (10%)
  other arithmetic  150 us (8%)
  local copies, waits for them, and re-layouts  149 us (8%)
    all_gather x2, waiting for transfers between devices, per_device(): normed_alls.append(lax.all_gather(normed_two, BOTH, axis=0, tiled=True))  233 us
    ppermute x36, starting transfers between devices, line_reduce(): up = lax.ppermute(send_up, 'fsdp', [(i, i + 1) for i in range(step)])  193 us
    ppermute x24, waiting for transfers between devices, halve(): lax.ppermute(send, 'seq', [(i, i ^ 1 << bit) for i in range(count)])  155 us
    ppermute x36, waiting for transfers between devices, line_reduce(): up = lax.ppermute(send_up, 'fsdp', [(i, i + 1) for i in range(step)])  117 us
    dot_general x20, matrix products, left_product(): lax.dot_general(left, right, (((0,), (0,)), ((), ())), preferred_element_...  112 us
    pallas_call x4, Pallas kernels, combine_stage(): pl.pallas_call(functools.partial(combine_kernel, blocks, capacity, cuts,...  101 us
    pallas_call x2, Pallas kernels, hidden_stage(): pl.pallas_call(functools.partial(hidden_kernel, blocks, capacity, experts...  94.1 us
    reduce_scatter x2, waiting for transfers between devices, per_device(): summed = lax.psum_scatter(out_part, 'seq', scatter_dimension=0, tiled=True)  86.6 us
  transfers between devices with their start and end apart: 132, of which 54 were waited for; matrix products, arithmetic and copies ran while one was open for 24% of the time, Pallas kernels for 10%

profile of v1, /device:TPU:0, one launch (start us, length us, event | category | flops | bytes accessed | tf_op | source)
XLA Modules:
  0.0 1890.8 jit_solution(15741478764686506594)
XLA Ops:
  27.3 61.9 %all-gather.15.cloned.1.call-done = bf16[2048,619]{1,0:T(8,128)(2,1)} async-done(((bf16[64,619]{1,0:T(8,128)(2,1)}), bf16[2048,619]{1,0:T(8,128)(2,1)}) %all-gather.15.cloned.1.call-update) | async-done | bytes 2535440 | tf_op jit(solution)/shard_map/all_gather | solution.py:402
  92.8 34.4 %all-gather.31.cloned.1.call-done = bf16[1,1024,2048]{2,1,0:T(8,128)(2,1)} async-done(((bf16[1,128,2048]{2,1,0:T(8,128)(2,1)}), bf16[1,1024,2048]{2,1,0:T(8,128)(2,1)}) %all-gather.31.cloned.1.call-update) | async-done | bytes 4194320 | tf_op jit(solution)/shard_map/all_gather | solution.py:463
  130.3 36.1 %all-gather.27.cloned.1.call-done = bf16[1,1024,2048]{2,1,0:T(8,128)(2,1)} async-done(((bf16[1,128,2048]{2,1,0:T(8,128)(2,1)}), bf16[1,1024,2048]{2,1,0:T(8,128)(2,1)}) %all-gather.27.cloned.1.call-update) | async-done | bytes 4194320 | tf_op jit(solution)/shard_map/all_gather | solution.py:463
  238.2 31.1 %reduce-scatter.7.cloned.1.call-done = bf16[128,2048]{1,0:T(8,128)(2,1)} async-done(((bf16[1024,2048]{1,0:T(8,128)(2,1)}), bf16[128,2048]{1,0:T(8,128)(2,1)}) %reduce-scatter.7.cloned.1.call-update) | async-done | bytes 524304 | tf_op jit(solution)/shard_map/reduce_scatter | solution.py:501
  269.3 55.5 %reduce-scatter.5.cloned.1.call-done = bf16[128,2048]{1,0:T(8,128)(2,1)} async-done(((bf16[1024,2048]{1,0:T(8,128)(2,1)}), bf16[128,2048]{1,0:T(8,128)(2,1)}) %reduce-scatter.5.cloned.1.call-update) | async-done | bytes 524304 | tf_op jit(solution)/shard_map/reduce_scatter | solution.py:501
  356.6 48.7 %all-to-all-done.2 = bf16[32,64,264]{2,1,0:T(8,128)(2,1)S(1)} async-done(((bf16[32,64,264]{2,1,0:T(8,128)(2,1)}), bf16[32,64,264]{2,1,0:T(8,128)(2,1)S(1)}, u32[]{:S(2)}, u32[]{:S(2)}) %all-to-all-start.2) | async-done | bytes 1081376 | tf_op jit(solution)/shard_map/all_to_all | solution.py:438
  450.2 16.4 all-gather.33.cloned.1.call-done
  466.6 116.7 %all-gather.19.cloned.1.call-done.tokens_ref = bf16[4096,2048]{1,0:T(8,128)(2,1)} async-done(((bf16[128,2048]{1,0:T(8,128)(2,1)}), bf16[4096,2048]{1,0:T(8,128)(2,1)}) %all-gather.19.cloned.1.call-update) | async-done | bytes 16777232 | tf_op jit(solution)/shard_map/all_gather | solution.py:510
  583.3 47.2 %hidden_stage.3 = (bf16[2048,2048]{1,0:T(8,128)(2,1)}, bf16[2048,2048]{1,0:T(8,128)(2,1)}, bf16[2048,704]{1,0:T(8,128)(2,1)}, bf16[2048,704]{1,0:T(8,128)(2,1)},...) custom-call(s32[3]{0:T(128)} %pad_add_fusion.place_ref, ...), custom_call_target="tpu_custom_call" | custom-call | flops 24159191040 | bytes 50331648 | tf_op jit(solution)/shard_map/hidden_stage/pallas_call | solution.py:227
  630.5 21.2 %combine_stage.5 = (bf16[2048,768]{1,0:T(8,128)(2,1)}, bf16[2048,768]{1,0:T(8,128)(2,1)}, bf16[2048,512]{1,0:T(8,128)(2,1)}, bf16[2048,768]{1,0:T(8,128)(2,1)}, ...) custom-call(s32[3]{0:T(128)} %pad_add_fusion.place_ref, s32[32,1,128]{2,1,0:T(1,128)} %copy_select_fusion.slots_ref, ...), custom_call_target="tpu_custom_call" | custom-call | flops 9126805504 | bytes 25165824 | tf_op jit(solution)/shard_map/combine_stage/pallas_call | solution.py:325
  652.5 47.5 %all-gather.29.cloned.1.call-done = bf16[1,4096,2048]{2,1,0:T(8,128)(2,1)} async-done(((bf16[1,128,2048]{2,1,0:T(8,128)(2,1)}), bf16[1,4096,2048]{2,1,0:T(8,128)(2,1)}) %all-gather.29.cloned.1.call-update) | async-done | bytes 16777232 | tf_op jit(solution)/shard_map/all_gather | solution.py:509
  699.9 116.7 %all-gather.17.cloned.1.call-done.tokens_ref = bf16[4096,2048]{1,0:T(8,128)(2,1)} async-done(((bf16[128,2048]{1,0:T(8,128)(2,1)}), bf16[4096,2048]{1,0:T(8,128)(2,1)}) %all-gather.17.cloned.1.call-update) | async-done | bytes 16777232 | tf_op jit(solution)/shard_map/all_gather | solution.py:510
  816.6 46.9 %hidden_stage.2 = (bf16[2048,2048]{1,0:T(8,128)(2,1)}, bf16[2048,2048]{1,0:T(8,128)(2,1)}, bf16[2048,704]{1,0:T(8,128)(2,1)}, bf16[2048,704]{1,0:T(8,128)(2,1)},...) custom-call(s32[3]{0:T(128)} %pad_add_fusion.place_ref, ...), custom_call_target="tpu_custom_call" | custom-call | flops 24159191040 | bytes 50331648 | tf_op jit(solution)/shard_map/hidden_stage/pallas_call | solution.py:227
  863.5 29.1 %combine_stage.6 = (bf16[2048,768]{1,0:T(8,128)(2,1)}, bf16[2048,768]{1,0:T(8,128)(2,1)}, bf16[2048,512]{1,0:T(8,128)(2,1)}, bf16[2048,768]{1,0:T(8,128)(2,1)}, ...) custom-call(s32[3]{0:T(128)} %pad_add_fusion.place_ref, s32[32,1,128]{2,1,0:T(1,128)} %copy_select_fusion.1.slots_ref, ...), custom_call_target="tpu_custom_call" | custom-call | flops 17179869184 | bytes 25165824 | tf_op jit(solution)/shard_map/combine_stage/pallas_call | solution.py:325
  896.1 29.1 %combine_stage.7 = (bf16[2048,768]{1,0:T(8,128)(2,1)}, bf16[2048,768]{1,0:T(8,128)(2,1)}, bf16[2048,512]{1,0:T(8,128)(2,1)}, bf16[2048,768]{1,0:T(8,128)(2,1)}, ...) custom-call(s32[3]{0:T(128)} %pad_add_fusion.place_ref, s32[32,1,128]{2,1,0:T(1,128)} %copy_select_fusion.slots_ref, ...), custom_call_target="tpu_custom_call" | custom-call | flops 17179869184 | bytes 25165824 | tf_op jit(solution)/shard_map/combine_stage/pallas_call | solution.py:325
  1084.1 29.8 %collective-permute-done.52 = bf16[2,128,512]{2,1,0:T(8,128)(2,1)S(1)} collective-permute-done((bf16[2,128,512]{2,1,0:T(8,128)(2,1)S(1)}, bf16[2,128,512]{2,1,0:T(8,128)(2,1)S(1)}, u32[]{:S(2)}, u32[]{:S(2)}) %collective-permute-start.52) | collective-permute-done | bytes 262176 | tf_op jit(solution)/shard_map/ppermute | solution.py:66
  1120.2 36.9 %collective-permute-done.106 = bf16[2,128,512]{2,1,0:T(8,128)(2,1)S(1)} collective-permute-done((bf16[2,128,512]{2,1,0:T(8,128)(2,1)S(1)}, bf16[2,128,512]{2,1,0:T(8,128)(2,1)S(1)}, u32[]{:S(2)}, u32[]{:S(2)}) %collective-permute-start.106) | collective-permute-done | bytes 262176 | tf_op jit(solution)/shard_map/ppermute | solution.py:66
  1184.8 27.4 %collective-permute-done.82 = bf16[2,4,128,768]{3,2,0,1:T(8,128)(2,1)S(1)} collective-permute-done((bf16[2,4,128,768]{3,2,0,1:T(8,128)(2,1)S(1)}, bf16[2,4,128,768]{3,2,0,1:T(8,128)(2,1)S(1)}, u32[]{:S(2)}, u32[]{:S(2)}) %collective-permute-start.82) | collective-permute-done | bytes 1572896 | tf_op jit(solution)/shard_map/ppermute | solution.py:66
  1328.6 28.2 %collective-permute-start.41 = (bf16[128,768]{1,0:T(8,128)(2,1)S(1)}, bf16[128,768]{1,0:T(8,128)(2,1)S(1)}, u32[]{:S(2)}, u32[]{:S(2)}) collective-permute-start(bf16[128,768]{1,0:T(8,128)(2,1)S(1)} %get-tuple-element.303), channel_id=1, source_target_pairs={{0,1},{1,2},{2,3},{4,5},{5,6},{6,7},{8,9},{9,10},{10,11},{12,13},{... | collective-permute-start | bytes 589832 | tf_op jit(solution)/shard_map/ppermute | solution.py:89
  1407.6 21.5 %combine_stage.4 = (bf16[2048,768]{1,0:T(8,128)(2,1)}, bf16[2048,768]{1,0:T(8,128)(2,1)}, bf16[2048,512]{1,0:T(8,128)(2,1)}, bf16[2048,768]{1,0:T(8,128)(2,1)}, ...) custom-call(s32[3]{0:T(128)} %pad_add_fusion.place_ref, s32[32,1,128]{2,1,0:T(1,128)} %copy_select_fusion.1.slots_ref, ...), custom_call_target="tpu_custom_call" | custom-call | flops 9126805504 | bytes 25165824 | tf_op jit(solution)/shard_map/combine_stage/pallas_call | solution.py:325
  1540.0 12.6 add_bitcast_fusion
  1672.0 13.0 collective-permute-done.11
  1736.6 40.2 %collective-permute-done.13 = bf16[128,768]{1,0:T(8,128)(2,1)S(1)} collective-permute-done((bf16[128,768]{1,0:T(8,128)(2,1)S(1)}, bf16[128,768]{1,0:T(8,128)(2,1)S(1)}, u32[]{:S(2)}, u32[]{:S(2)}) %collective-permute-start.13) | collective-permute-done | bytes 196640 | tf_op jit(solution)/shard_map/ppermute | solution.py:89
  1780.9 18.6 collective-permute-start.14
  (986 shorter events, 905.6 us)
Async XLA Ops:
  13.0 114.2 %all-gather.31.cloned.1.call-start = ((), (), s32[]{:S(2)}) async-start(), calls=%async_computation.26 | async-start | bytes 4718592 | tf_op jit(solution)/shard_map/all_gather | solution.py:463
  15.3 151.1 %all-gather.27.cloned.1.call-start = ((), (), s32[]{:S(2)}) async-start(), calls=%async_computation.24 | async-start | bytes 4718592 | tf_op jit(solution)/shard_map/all_gather | solution.py:463
  18.2 157.5 %all-to-all-start.1 = ((bf16[32,64,640]{2,1,0:T(8,128)(2,1)}), bf16[32,64,640]{2,1,0:T(8,128)(2,1)S(1)}, u32[]{:S(2)}, u32[]{:S(2)}) async-start(bf16[32,64,640]{2,1,0:T(8,128)(2,1)} %bitcast.12), calls=%async_computation.1 | async-start | bytes 5242880 | tf_op jit(solution)/shard_map/all_to_all | solution.py:420
  219.7 105.1 %reduce-scatter.5.cloned.1.call-start = ((), (), s32[]{:S(2)}) async-start(), calls=%async_computation.15 | async-start | bytes 4718592 | tf_op jit(solution)/shard_map/reduce_scatter | solution.py:501
  235.9 230.7 %all-gather.33.cloned.1.call-start = ((), (), s32[]{:S(2)}) async-start(), calls=%async_computation.27 | async-start | bytes 17301504 | tf_op jit(solution)/shard_map/all_gather | solution.py:509
  238.2 345.1 %all-gather.19.cloned.1.call-start = ((), (), s32[]{:S(2)}) async-start(), calls=%async_computation.18 | async-start | bytes 17301504 | tf_op jit(solution)/shard_map/all_gather | solution.py:510
  329.2 370.8 %all-gather.29.cloned.1.call-start = ((), (), s32[]{:S(2)}) async-start(), calls=%async_computation.25 | async-start | bytes 17301504 | tf_op jit(solution)/shard_map/all_gather | solution.py:509
  329.9 486.7 %all-gather.17.cloned.1.call-start = ((), (), s32[]{:S(2)}) async-start(), calls=%async_computation.16 | async-start | bytes 17301504 | tf_op jit(solution)/shard_map/all_gather | solution.py:510
  651.7 354.5 %collective-permute-start.27 = (bf16[2048,768]{1,0:T(8,128)(2,1)}, bf16[2048,768]{1,0:T(8,128)(2,1)}, u32[]{:S(2)}, u32[]{:S(2)}) collective-permute-start(bf16[2048,768]{1,0:T(8,128)(2,1)} %get-tuple-element.67), channel_id=1, source_target_pairs={{0,4},{4,0},{8,12},{12,8},{16,20},{20,16},{24,28},{28,24},{1,5},{5... | collective-permute-start | bytes 9437192 | tf_op jit(solution)/shard_map/ppermute | solution.py:110
  652.0 357.2 %collective-permute-start.36 = (bf16[2048,768]{1,0:T(8,128)(2,1)}, bf16[2048,768]{1,0:T(8,128)(2,1)}, u32[]{:S(2)}, u32[]{:S(2)}) collective-permute-start(bf16[2048,768]{1,0:T(8,128)(2,1)} %get-tuple-element.69), channel_id=1, source_target_pairs={{0,4},{4,0},{8,12},{12,8},{16,20},{20,16},{24,28},{28,24},{1,5},{5... | collective-permute-start | bytes 9437192 | tf_op jit(solution)/shard_map/ppermute | solution.py:110
  652.2 307.7 %collective-permute-start.45 = (bf16[2048,512]{1,0:T(8,128)(2,1)}, bf16[2048,512]{1,0:T(8,128)(2,1)}, u32[]{:S(2)}, u32[]{:S(2)}) collective-permute-start(bf16[2048,512]{1,0:T(8,128)(2,1)} %get-tuple-element.71), channel_id=1, source_target_pairs={{0,4},{4,0},{8,12},{12,8},{16,20},{20,16},{24,28},{28,24},{1,5},{5... | collective-permute-start | bytes 6291464 | tf_op jit(solution)/shard_map/ppermute | solution.py:110
  952.7 538.0 %all-gather.21.cloned.1.call-start = ((), (), s32[]{:S(2)}) async-start(), calls=%async_computation.19 | async-start | bytes 4718592 | tf_op jit(solution)/shard_map/all_gather | solution.py:603
  1038.3 137.1 %collective-permute-start.28 = (bf16[2,4,128,768]{3,2,0,1:T(8,128)(2,1)S(1)}, bf16[2,4,128,768]{3,2,0,1:T(8,128)(2,1)S(1)}, u32[]{:S(2)}, u32[]{:S(2)}) collective-permute-start(bf16[2,4,128,768]{3,2,0,1:T(8,128)(2,1)S(1)} %bitcast.813), channel_id=1, source_target_pairs={{0,8},{4,12},{8,0},{12,4},{16,24},{20,28},{24,16},{28,20},{1,9},{5... | collective-permute-start | bytes 4718600 | tf_op jit(solution)/shard_map/ppermute | solution.py:66
  1071.0 110.4 %collective-permute-start.37 = (bf16[2,4,128,768]{3,2,1,0:T(8,128)(2,1)S(1)}, bf16[2,4,128,768]{3,2,1,0:T(8,128)(2,1)S(1)}, u32[]{:S(2)}, u32[]{:S(2)}) collective-permute-start(bf16[2,4,128,768]{3,2,1,0:T(8,128)(2,1)S(1)} %bitcast.817), channel_id=1, source_target_pairs={{0,16},{4,20},{8,24},{12,28},{16,0},{20,4},{24,8},{28,12},{1,17},{... | collective-permute-start | bytes 4718600 | tf_op jit(solution)/shard_map/ppermute | solution.py:66
  1397.3 114.7 %all-gather.23.cloned.1.call-start = ((), (), s32[]{:S(2)}) async-start(), calls=%async_computation.21 | async-start | bytes 4718592 | tf_op jit(solution)/shard_map/all_gather | solution.py:603
  1461.3 104.7 %all-to-all-start.9 = ((bf16[32,64,264]{2,1,0:T(8,128)(2,1)}), bf16[32,64,264]{2,1,0:T(8,128)(2,1)}, u32[]{:S(2)}, u32[]{:S(2)}) async-start(bf16[32,64,264]{2,1,0:T(8,128)(2,1)} %pad_maximum_fusion.4), calls=%async_computation.13 | async-start | bytes 3145728 | tf_op jit(solution)/shard_map/all_to_all | solution.py:574
  1467.3 339.3 %reduce-scatter.9.cloned.1.call-start = ((), (), s32[]{:S(2)}) async-start(), calls=%async_computation.20 | async-start | bytes 6193152 | tf_op jit(solution)/shard_map/reduce_scatter | solution.py:639
  1467.3 121.3 %collective-permute-start = (bf16[2048,768]{1,0:T(8,128)(2,1)}, bf16[2048,768]{1,0:T(8,128)(2,1)}, u32[]{:S(2)}, u32[]{:S(2)}) collective-permute-start(bf16[2048,768]{1,0:T(8,128)(2,1)} %get-tuple-element.59), channel_id=1, source_target_pairs={{0,4},{4,0},{8,12},{12,8},{16,20},{20,16},{24,28},{28,24},{1,5},{5... | collective-permute-start | bytes 9437192 | tf_op jit(solution)/shard_map/ppermute | solution.py:110
  1467.6 141.2 %collective-permute-start.9 = (bf16[2048,768]{1,0:T(8,128)(2,1)}, bf16[2048,768]{1,0:T(8,128)(2,1)}, u32[]{:S(2)}, u32[]{:S(2)}) collective-permute-start(bf16[2048,768]{1,0:T(8,128)(2,1)} %get-tuple-element.61), channel_id=1, source_target_pairs={{0,4},{4,0},{8,12},{12,8},{16,20},{20,16},{24,28},{28,24},{1,5},{5... | collective-permute-start | bytes 9437192 | tf_op jit(solution)/shard_map/ppermute | solution.py:110
  1539.9 269.0 %reduce-scatter.11.cloned.1.call-start = ((), (), s32[]{:S(2)}) async-start(), calls=%async_computation.22 | async-start | bytes 6193152 | tf_op jit(solution)/shard_map/reduce_scatter | solution.py:639
  1660.8 118.5 %collective-permute-start.26 = (bf16[128,512]{1,0:T(8,128)(2,1)}, bf16[128,512]{1,0:T(8,128)(2,1)S(1)}, u32[]{:S(2)}, u32[]{:S(2)}) collective-permute-start(bf16[128,512]{1,0:T(8,128)(2,1)} %slice_bitcast_fusion.35), channel_id=1, source_target_pairs={{0,8},{4,12},{8,0},{12,4},{16,24},{20,28},{24,16},{28,20},{1,9},{5... | collective-permute-start | bytes 393224 | tf_op jit(solution)/shard_map/ppermute | solution.py:66
  1666.8 134.9 %collective-permute-start.4 = (bf16[2,128,768]{2,1,0:T(8,128)(2,1)}, bf16[2,128,768]{2,1,0:T(8,128)(2,1)}, u32[]{:S(2)}, u32[]{:S(2)}) collective-permute-start(bf16[2,128,768]{2,1,0:T(8,128)(2,1)} %get-tuple-element.268), channel_id=1, source_target_pairs={{0,1},{1,2},{2,3},{4,5},{5,6},{6,7},{8,9},{9,10},{10,11},{12,13},{... | collective-permute-start | bytes 1179656 | tf_op jit(solution)/shard_map/ppermute | solution.py:89
  1724.8 104.6 %all-to-all-start.6 = ((bf16[32,64,640]{2,1,0:T(8,128)(2,1)}), bf16[32,64,640]{2,1,0:T(8,128)(2,1)}, u32[]{:S(2)}, u32[]{:S(2)}) async-start(bf16[32,64,640]{2,1,0:T(8,128)(2,1)} %fusion.10), calls=%async_computation.10 | async-start | bytes 5242880 | tf_op jit(solution)/shard_map/all_to_all | solution.py:680
  1729.4 132.4 %all-gather.25.cloned.1.call-start = ((), (), s32[]{:S(2)}) async-start(), calls=%async_computation.23 | async-start | bytes 2654208 | tf_op jit(solution)/shard_map/all_gather | solution.py:663
  (291 other events, 5484.2 us)
Sparse Core Ops, SparseCore 0:
  13.1 76.0 all-gather.14
  91.6 35.5 all-gather.30
  129.7 36.7 all-gather.26
  219.8 49.4 reduce-scatter.6
  273.4 51.3 reduce-scatter.4
  328.3 138.3 all-gather.32
  470.2 113.0 all-gather.18
  586.8 113.0 all-gather.28
  703.5 113.0 all-gather.16
  1397.4 37.7 all-gather.20
  1459.6 52.3 all-gather.22
  1540.0 58.0 reduce-scatter.8
  1636.1 65.8 reduce-scatter.10
  1818.4 34.0 all-gather.24

commit v2 on v1

v2 whole, which is shorter than its diff:
```python
import functools

import jax
import jax.numpy as jnp
from jax import lax
from jax.experimental import pallas as pl
from jax.experimental.pallas import tpu as pltpu
from jax.sharding import PartitionSpec as P

HEADS = 16
NOPE = 128
ROPE = 64
VDIM = 128
KVR = 512

EPS = 1e-06
THETA = 10000.0
NEGATIVE = -1e30
BOTH = ("seq", "fsdp")
VMEM_LIMIT = 60 * 2**20
F32 = jnp.float32
BF16 = jnp.bfloat16


def product(left, right):
    return jnp.dot(left, right, preferred_element_type=F32)


def left_product(left, right):
    return lax.dot_general(left, right, (((0,), (0,)), ((), ())), preferred_element_type=F32)


def right_product(left, right):
    return lax.dot_general(left, right, (((1,), (1,)), ((), ())), preferred_element_type=F32)


def normed(value):
    factor = lax.rsqrt(jnp.mean(value * value, axis=-1, keepdims=True) + EPS)
    return (value * factor, factor)


def norm_back(grad_unit, unit, factor):
    return factor * (grad_unit - unit * jnp.mean(grad_unit * unit, axis=-1, keepdims=True))


def rotate(value, angles):
    middle = value.shape[-1] // 2
    cosine = jnp.cos(angles)
    sine = jnp.sin(angles)
    first = value[..., :middle]
    second = value[..., middle:]
    return jnp.concatenate(
        [first * cosine - second * sine, second * cosine + first * sine], axis=-1
    )


def silu_parts(value):
    logistic = jax.nn.sigmoid(value)
    return (value * logistic, logistic * (1.0 + value * (1.0 - logistic)))


def add_pair(left, right):
    return (left.astype(F32) + right.astype(F32)).astype(BF16)


def swap(value, bit):
    count = lax.axis_size("seq")
    return lax.ppermute(value, "seq", [(i, i ^ (1 << bit)) for i in range(count)])


def chip_bits():
    return list(range(1, lax.axis_size("seq").bit_length() - 1))


def halves_of(width):
    middle = -(-width // 256) * 128
    return ((0, middle), (middle, width))


class Flow:
    def __init__(self, steps):
        self.steps = steps
        self.value = None
        self.pending = next(steps)

    def arrive(self, arrived):
        try:
            self.pending = self.steps.send(arrived)
        except StopIteration as stop:
            self.pending = None
            self.value = stop.value


class Slots:
    def __init__(self):
        self.token = jnp.zeros((8, 128), F32)

    def tie(self, values):
        return lax.optimization_barrier((values, self.token))[0]

    def run(self, flows, compute=None, *inputs):
        flows = [flow for flow in flows if flow.pending is not None]
        pending = [flow.pending for flow in flows]
        made = compute(*self.tie(inputs)) if compute else ()
        pending, made, self.token = lax.optimization_barrier((pending, made, self.token))
        for flow, arrived in zip(flows, pending):
            flow.arrive(arrived)
        return made

    def finish(self, flow, *others):
        while flow.pending is not None:
            self.run((flow,) + others)
        return flow.value


def stacked(value, names):
    lead = len(names)
    axes = [names.index(bit) for bit in sorted(names, reverse=True)]
    value = value.transpose(axes + list(range(lead, value.ndim)))
    return value.reshape((-1,) + value.shape[lead:])


def spread(parts):
    bits = chip_bits()
    orders = (bits, bits[::-1])
    for step in range(len(bits)):
        arrived = yield [swap(part, order[step]) for part, order in zip(parts, orders)]
        parts = [jnp.stack(pair) for pair in zip(parts, arrived)]
    return [stacked(part, order[::-1]) for part, order in zip(parts, orders)]


def fold(parts, lead):
    bits = chip_bits()
    for step in range(len(bits)):
        kept, sent = [], []
        for part, order in zip(parts, (bits, bits[::-1])):
            names = sorted(order[step:], reverse=True)
            part = part.reshape((2,) * len(names) + part.shape[lead:])
            axis = names.index(order[step])
            kept.append(lax.index_in_dim(part, 0, axis, keepdims=False))
            sent.append(swap(lax.index_in_dim(part, 1, axis, keepdims=False), order[step]))
        arrived = yield sent
        parts = [add_pair(keep, got) for keep, got in zip(kept, arrived)]
        lead = len(bits) - step - 1
    return parts


def gather_seq(own):
    parts = yield from spread([own[:, low:high] for low, high in halves_of(own.shape[1])])
    near = jnp.concatenate(parts, axis=-1)
    (far,) = yield [swap(near, 0)]
    return jnp.concatenate([near, far], axis=0).reshape(-1, own.shape[1])


def scatter_seq(value, rows):
    half = value.shape[0] // 2
    (far,) = yield [swap(value[half:], 0)]
    near = add_pair(value[:half], far).reshape(-1, rows, value.shape[1])
    parts = yield from fold(
        [near[..., low:high] for low, high in halves_of(value.shape[1])], 1
    )
    return jnp.concatenate(parts, axis=-1)


def exchange(value, axes):
    (arrived,) = yield [lax.all_to_all(value, axes, 0, 0, tiled=True)]
    return arrived


def line_reduce(value):
    count = lax.axis_size("fsdp")
    place = lax.axis_index("fsdp")

    def piece(index):
        return lax.dynamic_index_in_dim(value, jnp.clip(index, 0, count - 1), 0, keepdims=False)

    up = down = None
    for step in range(1, count):
        send_up = piece(place + count - step)
        send_down = piece(place - count + step)
        if up is not None:
            send_up = add_pair(send_up, up)
            send_down = add_pair(send_down, down)
        up, down = yield [
            lax.ppermute(send_up, "fsdp", [(i, i + 1) for i in range(step)]),
            lax.ppermute(send_down, "fsdp", [(i, i - 1) for i in range(count - step, count)]),
        ]
    return piece(place).astype(F32) + up.astype(F32) + down.astype(F32)


def reduce_all(keeps, sends, rows):
    arrived = yield [swap(send, 0) for send in sends]
    line = lax.axis_size("fsdp")
    parts = [
        add_pair(keep, got).reshape(-1, line, rows, keep.shape[-1])
        for keep, got in zip(keeps, arrived)
    ]
    parts = yield from fold(parts, 1)
    return (yield from line_reduce(jnp.concatenate(parts, axis=-1)))


def one_hot(slots, capacity):
    rows = slots.shape[-1]
    return lax.broadcasted_iota(jnp.int32, (capacity, rows), 0) == slots


def hidden_kernel(
    blocks,
    capacity,
    experts,
    hidden,
    place_ref,
    slots_ref,
    tokens_ref,
    top_ref,
    wide_ref,
    shared_ref,
    gate_ref,
    up_ref,
    down_ref,
    taken_ref,
    taken_top_ref,
    hidden_ref,
    pre_ref,
    post_ref,
    shared_hidden_ref,
    shared_grad_ref,
    gate_grad_ref,
):
    rows = slots_ref.shape[-1]
    lanes = shared_ref.shape[-1]
    expert = place_ref[0]
    wide = jnp.dot(tokens_ref[...], wide_ref[...], preferred_element_type=F32)
    back = jnp.dot(top_ref[...], shared_ref[...], preferred_element_type=F32)
    first = wide[:, :lanes]
    second = wide[:, lanes:]
    silu, slope = silu_parts(first)
    shared_hidden_ref[...] = (silu * second).astype(BF16)
    shared_grad_ref[:, :lanes] = (back * second * slope).astype(BF16)
    shared_grad_ref[:, lanes:] = (back * silu).astype(BF16)
    lane = lax.broadcasted_iota(jnp.int32, first.shape, 1)
    logits = jnp.where((lane >= hidden) & (lane < hidden + experts), first, NEGATIVE)
    powers = jnp.exp(logits - jnp.max(logits, axis=-1, keepdims=True))
    total = jnp.sum(powers, axis=-1, keepdims=True)
    gates = jnp.sum(jnp.where(lane == hidden + expert, powers, 0.0), axis=-1, keepdims=True)
    gates = jnp.broadcast_to(gates / total, first.shape)
    slot_gates = []
    for block in range(blocks):
        chosen = one_hot(slots_ref[block], capacity)
        low = chosen.astype(BF16)
        own = pl.ds(block * rows, rows)
        there = pl.ds(block * capacity, capacity)
        taken_ref[there, :] = jnp.dot(
            low, tokens_ref[own, :], preferred_element_type=F32
        ).astype(BF16)
        taken_top_ref[there, :] = jnp.dot(
            low, top_ref[own, :], preferred_element_type=F32
        ).astype(BF16)
        slot_gates.append(
            jnp.dot(
                chosen.astype(F32),
                gates[block * rows : (block + 1) * rows],
                precision=lax.Precision.HIGHEST,
                preferred_element_type=F32,
            )[:, :1]
        )
    slot_gates = jnp.concatenate(slot_gates, axis=0)
    gate_pre = jnp.dot(taken_ref[...], gate_ref[...], preferred_element_type=F32)
    up_pre = jnp.dot(taken_ref[...], up_ref[...], preferred_element_type=F32)
    grad = jnp.dot(taken_top_ref[...], down_ref[...], preferred_element_type=F32)
    swish, slope = silu_parts(gate_pre)
    made = swish * up_pre
    hidden_ref[...] = (made * slot_gates).astype(BF16)
    slot_grads = jnp.sum(made * grad, axis=-1, keepdims=True)
    grad = grad * slot_gates
    pre_ref[...] = (grad * up_pre * slope).astype(BF16)
    post_ref[...] = (grad * swish).astype(BF16)
    for block in range(blocks):
        chosen = one_hot(slots_ref[block], capacity)
        gate_grad_ref[block] = jnp.sum(
            jnp.where(chosen, slot_grads[block * capacity : (block + 1) * capacity], 0.0),
            axis=0,
            keepdims=True,
        )


def scores_of(qn_ref, qr_ref, kv_ref, kr_ref, seg_q, seg_k, pos_q, pos_k, head, factor):
    lane = lax.broadcasted_iota(jnp.int32, qr_ref.shape, 1)
    turned = jnp.where(lane // ROPE == head, qr_ref[...], jnp.zeros((), BF16))
    query = jnp.concatenate([qn_ref[...], turned], axis=1)
    keys = jnp.concatenate([kv_ref[:, :NOPE], kr_ref[...]], axis=1)
    scores = lax.dot_general(
        query, keys, (((1,), (1,)), ((), ())), preferred_element_type=F32
    )
    allowed = (seg_q[...] == seg_k[...]) & (pos_k[...] <= pos_q[...])
    scores = jnp.where(allowed, scores * factor, NEGATIVE)
    powers = jnp.exp(scores - jnp.max(scores, axis=-1, keepdims=True))
    return query, keys, powers / jnp.sum(powers, axis=-1, keepdims=True)


def attend_kernel(
    factor, qn_ref, qr_ref, kv_ref, kr_ref, seg_q, seg_k, pos_q, pos_k, out_ref
):
    _, _, probs = scores_of(
        qn_ref, qr_ref, kv_ref, kr_ref, seg_q, seg_k, pos_q, pos_k, pl.program_id(1), factor
    )
    out_ref[...] = jnp.dot(
        probs.astype(BF16), kv_ref[:, NOPE:], preferred_element_type=F32
    ).astype(BF16)


def attend_back_kernel(
    factor,
    qn_ref,
    qr_ref,
    kv_ref,
    kr_ref,
    seg_q,
    seg_k,
    pos_q,
    pos_k,
    top_ref,
    grad_qn_ref,
    grad_qr_ref,
    grad_kv_ref,
    grad_kr_ref,
    sum_ref,
):
    step, head = pl.program_id(0), pl.program_id(1)
    last = pl.num_programs(0) - 1
    query, keys, probs = scores_of(
        qn_ref, qr_ref, kv_ref, kr_ref, seg_q, seg_k, pos_q, pos_k, head, factor
    )
    top = top_ref[...]
    grad_probs = lax.dot_general(
        top, kv_ref[:, NOPE:], (((1,), (1,)), ((), ())), preferred_element_type=F32
    )
    mean = jnp.sum(probs * grad_probs, axis=-1, keepdims=True)
    grad_scores = (probs * (grad_probs - mean)).astype(BF16)
    low = probs.astype(BF16)
    grad_query = jnp.dot(grad_scores, keys, preferred_element_type=F32) * factor
    grad_qn_ref[...] = grad_query[:, :NOPE].astype(BF16)
    turned = grad_query[:, NOPE:]
    lane = lax.broadcasted_iota(jnp.int32, turned.shape, 1)
    turned = jnp.where(lane // ROPE == head, turned, 0.0)
    grad_keys = left_product(grad_scores, query) * factor
    grad_values = left_product(low, top)

    @pl.when(head == 0)
    def _():
        grad_qr_ref[...] = turned

    @pl.when(head != 0)
    def _():
        grad_qr_ref[...] += turned

    @pl.when((step == 0) & (head == 0))
    def _():
        grad_kr_ref[...] = grad_keys[:, NOPE:]

    @pl.when((step != 0) | (head != 0))
    def _():
        grad_kr_ref[...] += grad_keys[:, NOPE:]

    @pl.when(step == 0)
    def _():
        sum_ref[head, :, :NOPE] = grad_keys[:, :NOPE]
        sum_ref[head, :, NOPE:] = grad_values

    @pl.when(step != 0)
    def _():
        sum_ref[head, :, :NOPE] += grad_keys[:, :NOPE]
        sum_ref[head, :, NOPE:] += grad_values

    @pl.when(step == last)
    def _():
        grad_kv_ref[head] = sum_ref[head].astype(BF16)


def attend_specs(length, heads, turned, block):
    return [
        pl.BlockSpec((block, NOPE), lambda i, h: (i, h)),
        pl.BlockSpec((block, turned), lambda i, h: (i, 0)),
        pl.BlockSpec((length, NOPE + VDIM), lambda i, h: (0, h)),
        pl.BlockSpec((length, turned), lambda i, h: (0, 0)),
        pl.BlockSpec((block, 1), lambda i, h: (i, 0)),
        pl.BlockSpec((1, length), lambda i, h: (0, 0)),
        pl.BlockSpec((block, 1), lambda i, h: (i, 0)),
        pl.BlockSpec((1, length), lambda i, h: (0, 0)),
    ]


def attend_stage(factor, heads, inputs):
    length, turned = inputs[1].shape
    block = min(length, 256)
    return pl.pallas_call(
        functools.partial(attend_kernel, factor),
        grid=(length // block, heads),
        in_specs=attend_specs(length, heads, turned, block),
        out_specs=pl.BlockSpec((block, VDIM), lambda i, h: (i, h)),
        out_shape=jax.ShapeDtypeStruct((length, heads * VDIM), BF16),
        compiler_params=pltpu.CompilerParams(vmem_limit_bytes=VMEM_LIMIT),
        cost_estimate=pl.CostEstimate(
            flops=2 * heads * length * length * 384,
            bytes_accessed=8 * length * heads * NOPE,
            transcendentals=heads * length * length,
        ),
        name="attend_stage",
    )(*inputs)


def attend_back_stage(factor, heads, inputs, top):
    length, turned = inputs[1].shape
    block = min(length, 256)
    return pl.pallas_call(
        functools.partial(attend_back_kernel, factor),
        grid=(length // block, heads),
        in_specs=attend_specs(length, heads, turned, block)
        + [pl.BlockSpec((block, VDIM), lambda i, h: (i, h))],
        out_specs=[
            pl.BlockSpec((block, NOPE), lambda i, h: (i, h)),
            pl.BlockSpec((block, turned), lambda i, h: (i, 0)),
            pl.BlockSpec((heads, length, NOPE + VDIM), lambda i, h: (0, 0, 0)),
            pl.BlockSpec((length, turned), lambda i, h: (0, 0)),
        ],
        out_shape=[
            jax.ShapeDtypeStruct((length, heads * NOPE), BF16),
            jax.ShapeDtypeStruct((length, turned), F32),
            jax.ShapeDtypeStruct((heads, length, NOPE + VDIM), BF16),
            jax.ShapeDtypeStruct((length, turned), F32),
        ],
        scratch_shapes=[pltpu.VMEM((heads, length, NOPE + VDIM), F32)],
        compiler_params=pltpu.CompilerParams(vmem_limit_bytes=VMEM_LIMIT),
        cost_estimate=pl.CostEstimate(
            flops=2 * heads * length * length * 1024,
            bytes_accessed=16 * length * heads * NOPE,
            transcendentals=heads * length * length,
        ),
        name="attend_back_stage",
    )(*inputs, top)


def whole_spec(array):
    return pl.BlockSpec(
        array.shape, lambda i, *_: (0,) * array.ndim, pipeline_mode=pl.Buffered(1)
    )


def hidden_stage(place, slots, tokens, top, weights, capacity, experts, hidden):
    wide_weight, shared_down, gate_weight, up_weight, down_weight = weights
    devices, _, rows = slots.shape
    blocks = 2 * lax.axis_size("fsdp")
    steps = devices // blocks
    width = tokens.shape[1]
    half = gate_weight.shape[1]
    lanes = shared_down.shape[1]
    count = blocks * capacity

    def rows_spec(size, columns):
        return pl.BlockSpec((size, columns), lambda i, *_: (i, 0))

    slots_spec = pl.BlockSpec((blocks, 1, rows), lambda i, *_: (i, 0, 0))
    flops = devices * 2 * (3 * capacity * width * half + rows * width * 3 * lanes)
    return pl.pallas_call(
        functools.partial(hidden_kernel, blocks, capacity, experts, hidden),
        grid_spec=pltpu.PrefetchScalarGridSpec(
            num_scalar_prefetch=1,
            grid=(steps,),
            in_specs=[
                slots_spec,
                rows_spec(blocks * rows, width),
                rows_spec(blocks * rows, width),
                *[whole_spec(weight) for weight in weights],
            ],
            out_specs=[
                rows_spec(count, width),
                rows_spec(count, width),
                rows_spec(count, half),
                rows_spec(count, half),
                rows_spec(count, half),
                rows_spec(blocks * rows, lanes),
                rows_spec(blocks * rows, 2 * lanes),
                slots_spec,
            ],
        ),
        out_shape=[
            jax.ShapeDtypeStruct((steps * count, width), BF16),
            jax.ShapeDtypeStruct((steps * count, width), BF16),
            jax.ShapeDtypeStruct((steps * count, half), BF16),
            jax.ShapeDtypeStruct((steps * count, half), BF16),
            jax.ShapeDtypeStruct((steps * count, half), BF16),
            jax.ShapeDtypeStruct((devices * rows, lanes), BF16),
            jax.ShapeDtypeStruct((devices * rows, 2 * lanes), BF16),
            jax.ShapeDtypeStruct(slots.shape, F32),
        ],
        compiler_params=pltpu.CompilerParams(vmem_limit_bytes=VMEM_LIMIT),
        cost_estimate=pl.CostEstimate(
            flops=flops, bytes_accessed=3 * devices * rows * width * 2, transcendentals=0
        ),
        name="hidden_stage",
    )(place, slots, tokens, top, *weights)


def combine_kernel(blocks, capacity, cuts, count, place_ref, slots_ref, *refs):
    lefts, rights = refs[:count], refs[count : 2 * count]
    shared_ref, shared_weight_ref = refs[2 * count : 2 * count + 2]
    outs = refs[2 * count + 2 : -1]
    rows_ref = refs[-1]
    rows = slots_ref.shape[-1]
    total = None
    for left, right in zip(lefts, rights):
        term = jnp.dot(left[...], right[...], preferred_element_type=F32)
        total = term if total is None else total + term
    rows_ref[...] = total.astype(BF16)
    half = blocks // 2
    for side in range(2):
        core = place_ref[1] ^ side
        for block in range(half):
            index = core * half + block
            chosen = one_hot(slots_ref[index], capacity).astype(BF16)
            there = pl.ds(pl.multiple_of(index * capacity, capacity), capacity)
            own = pl.ds(pl.multiple_of(index * rows, rows), rows)
            value = lax.dot_general(
                chosen,
                rows_ref[there, :],
                (((0,), (0,)), ((), ())),
                preferred_element_type=F32,
            ) + jnp.dot(
                shared_ref[own, :], shared_weight_ref[...], preferred_element_type=F32
            )
            value = value.astype(BF16)
            for part, (low, high) in enumerate(cuts):
                outs[2 * side + part][pl.ds(block * rows, rows), :] = value[:, low:high]


def combine_stage(place, slots, lefts, rights, shared, shared_weight, capacity):
    devices, _, rows = slots.shape
    blocks = 2 * lax.axis_size("fsdp")
    steps = devices // blocks
    width = rights[0].shape[1]
    cuts = halves_of(width)
    half = blocks // 2 * rows

    def rows_spec(size, columns):
        return pl.BlockSpec((size, columns), lambda i, *_: (i, 0))

    out_specs = [
        pl.BlockSpec((half, high - low), lambda i, place: (i ^ place[2], 0))
        for _ in range(2)
        for low, high in cuts
    ]
    out_shape = [
        jax.ShapeDtypeStruct((steps * half, high - low), BF16)
        for _ in range(2)
        for low, high in cuts
    ]
    flops = 2 * devices * width * (
        capacity * sum(left.shape[1] for left in lefts) + rows * (capacity + shared.shape[1])
    )
    outs = pl.pallas_call(
        functools.partial(combine_kernel, blocks, capacity, cuts, len(lefts)),
        grid_spec=pltpu.PrefetchScalarGridSpec(
            num_scalar_prefetch=1,
            grid=(steps,),
            in_specs=[
                pl.BlockSpec((blocks, 1, rows), lambda i, *_: (i, 0, 0)),
                *[rows_spec(blocks * capacity, left.shape[1]) for left in lefts],
                *[whole_spec(right) for right in rights],
                rows_spec(blocks * rows, shared.shape[1]),
                whole_spec(shared_weight),
            ],
            out_specs=out_specs,
            scratch_shapes=[pltpu.VMEM((blocks * capacity, width), BF16)],
        ),
        out_shape=out_shape,
        compiler_params=pltpu.CompilerParams(vmem_limit_bytes=VMEM_LIMIT),
        cost_estimate=pl.CostEstimate(
            flops=flops, bytes_accessed=devices * rows * width * 3, transcendentals=0
        ),
        name="combine_stage",
    )(place, slots, *lefts, *rights, shared, shared_weight)
    return outs[:2], outs[2:]


def per_device(
    tokens_in,
    segments,
    routes,
    cotangent,
    g_attn,
    g_kv,
    g_moe,
    w_query,
    w_kv_down,
    w_kv_up,
    w_out,
    w_router,
    w_shared_gate,
    w_shared_up,
    w_shared_down,
    w_expert_gate,
    w_expert_up,
    w_expert_down,
):
    micro_count, rows, width = tokens_in.shape
    seqs, line = lax.axis_size("seq"), lax.axis_size("fsdp")
    devices = seqs * line
    length = rows * seqs
    experts = devices // 2
    picked = routes.shape[2]
    capacity = max(2, rows * picked * 4 // (experts * 3))
    capacity = -(-capacity // 16) * 16
    heads = HEADS // seqs
    me_seq = lax.axis_index("seq")
    me = me_seq * line + lax.axis_index("fsdp")
    expert = me // 2
    factor = (NOPE + ROPE) ** (-0.5)
    frequency = THETA ** (-jnp.arange(ROPE // 2, dtype=F32) * 2.0 / ROPE)
    order = jnp.arange(seqs)
    ranks = (order ^ me_seq) >> 1 | ((order ^ me_seq) & 1) * (seqs // 2)
    order = me_seq ^ ((order % (seqs // 2)) * 2 + order // (seqs // 2))

    def to_relative(value):
        return value.reshape(seqs, rows, -1)[order].reshape(value.shape)

    def to_absolute(value):
        return value.reshape(seqs, rows, -1)[ranks].reshape(value.shape)

    places = (order[:, None] * rows + jnp.arange(rows)[None, :]).reshape(-1)
    angles = places.astype(F32)[:, None] * frequency[None, :]
    own_angles = angles[:rows]
    micros = range(micro_count)

    slots = Slots()
    place = jnp.stack([expert, me_seq & 1, me_seq >> 1]).astype(jnp.int32)
    tokens = [Flow(gather_seq(tokens_in[micro])) for micro in micros]

    piece = w_kv_down.shape[0]
    kv_columns = w_kv_down.shape[1]
    small = jnp.concatenate(
        [
            w_kv_down,
            w_router,
            g_attn[:, None],
            g_moe[:, None],
            jnp.pad(g_kv, (0, piece - g_kv.shape[0]))[:, None],
            routes.reshape(piece, -1).astype(BF16),
        ],
        axis=1,
    )
    small = lax.all_gather(small, BOTH, axis=0, tiled=True)

    query_width = heads * (NOPE + ROPE)
    out_width = heads * VDIM
    for_query = w_query.reshape(piece, seqs, heads, NOPE + ROPE)
    for_query = jnp.concatenate(
        [
            for_query[..., :NOPE].reshape(piece, seqs, -1),
            for_query[..., NOPE:].reshape(piece, seqs, -1),
        ],
        axis=2,
    ).transpose(1, 0, 2)
    for_out = w_out.reshape(seqs, out_width, piece).transpose(0, 2, 1)
    for_heads = jnp.concatenate([for_query, for_out], axis=2)
    for_heads = jnp.broadcast_to(
        for_heads[:, None], (seqs, line, piece, query_width + out_width)
    ).reshape(devices, piece, query_width + out_width)
    for_heads = lax.all_to_all(for_heads, BOTH, 0, 0, tiled=True)
    up_weight = lax.all_to_all(
        jnp.broadcast_to(w_kv_up[None], (line,) + w_kv_up.shape), "fsdp", 0, 0, tiled=True
    )
    hidden = w_shared_gate.shape[1] // devices
    for_shared = jnp.concatenate(
        [
            w_shared_gate.reshape(piece, devices, hidden).transpose(1, 0, 2),
            w_shared_up.reshape(piece, devices, hidden).transpose(1, 0, 2),
            w_shared_down.reshape(devices, hidden, piece).transpose(0, 2, 1),
        ],
        axis=2,
    )
    for_shared = Flow(exchange(for_shared, BOTH))
    slots.finish(tokens[0], tokens[1])
    slots.finish(tokens[1])
    small, for_heads, up_weight = slots.run([], lambda *given: given, small, for_heads, up_weight)
    tops = [lax.all_gather(slots.tie(cotangent[0]), BOTH, axis=0, tiled=True), None]
    for_heads = for_heads.reshape(width, query_width + out_width)
    query_weight = for_heads[:, :query_width]
    out_weight = for_heads[:, query_width:]
    up_weight = up_weight.transpose(1, 0, 2).reshape(KVR, -1)
    down_weight = small[:, :kv_columns]
    router_weight = small[:, kv_columns : kv_columns + experts]
    last = kv_columns + experts
    gain_one = small[:, last].astype(F32)
    gain_two = small[:, last + 1].astype(F32)
    gain_latent = small[:, last + 2].reshape(devices, piece)[:, : g_kv.shape[0]].reshape(-1)
    routes_all = small[:, last + 3 :].astype(jnp.int32).reshape((devices,) + routes.shape)
    gain_latent = gain_latent.astype(F32)

    def projections(tokens):
        unit_one, _ = normed(tokens.astype(F32))
        normed_one = (unit_one * gain_one).astype(BF16)
        query_raw = product(normed_one, query_weight)
        query = query_raw[:, : heads * NOPE].astype(BF16)
        turned = query_raw[:, heads * NOPE :].reshape(length, heads, ROPE)
        turned = turned_lanes(rotate(turned, angles[:, None, :]).reshape(length, -1))
        latent = product(normed_one, down_weight)
        unit_latent, factor_latent = normed(latent[:, :KVR])
        latent_norm = (unit_latent * gain_latent).astype(BF16)
        key_rope = rotate(latent[:, KVR:], angles).astype(BF16)
        key_value = product(latent_norm, up_weight).astype(BF16)
        key_rope = turned_lanes(jnp.tile(key_rope, (1, heads)))
        return (
            normed_one,
            latent_norm,
            (query, turned, key_value, key_rope),
            unit_latent[:rows],
            factor_latent[:rows],
        )

    def turned_lanes(value):
        return jnp.pad(value.astype(BF16), ((0, 0), (0, -value.shape[1] % 128)))

    def marks_of(micro):
        segment = segments[micro].reshape(seqs, rows)[order].reshape(-1)
        return segment[:, None], segment[None, :], places[:, None], places[None, :]

    def attend(projected, marks):
        attended = attend_stage(factor, heads, projected[2] + marks)
        return attended, right_product(attended, out_weight).astype(BF16)

    def home_forward(micro, summed):
        residual = tokens_in[micro].astype(F32) + summed.astype(F32)
        unit_two, factor_two = normed(residual)
        normed_two = (unit_two * gain_two).astype(BF16)
        return residual, unit_two, factor_two, normed_two

    marks = [marks_of(micro) for micro in micros]
    projected = [None, None]
    attended = [None, None]
    residuals = [None, None]
    normed_alls = [None, None]
    projected[0] = slots.run([], projections, tokens[0].value)
    attended[0] = slots.run([], attend, projected[0], marks[0])
    summed = Flow(scatter_seq(attended[0][1], rows))
    projected[1] = slots.run([summed, for_shared], projections, tokens[1].value)
    attended[1] = slots.run([summed], attend, projected[1], marks[1])
    summed_two = Flow(scatter_seq(attended[1][1], rows))
    slots.finish(summed, summed_two)
    residuals[0] = home_forward(0, summed.value)
    normed_alls[0] = lax.all_gather(residuals[0][3], BOTH, axis=0, tiled=True)
    slots.finish(summed_two)
    residuals[1] = home_forward(1, summed_two.value)
    normed_alls[1] = lax.all_gather(residuals[1][3], BOTH, axis=0, tiled=True)
    later, _ = lax.optimization_barrier((cotangent[1], residuals[1][3]))
    tops[1] = lax.all_gather(later, BOTH, axis=0, tiled=True)

    lanes = -(-(hidden + experts) // 128) * 128

    def padded(parts):
        parts = jnp.concatenate(parts, axis=1)
        return jnp.pad(parts, ((0, 0), (0, lanes - parts.shape[1])))

    for_shared = for_shared.value.reshape(width, 3 * hidden)
    shared_gate = for_shared[:, :hidden]
    shared_up = for_shared[:, hidden : 2 * hidden]
    shared_down = padded([for_shared[:, 2 * hidden :]])
    wide_weight = jnp.concatenate(
        [padded([shared_gate, router_weight]), padded([shared_up])], axis=1
    )
    shared_in = jnp.concatenate([padded([shared_gate]), padded([shared_up])], axis=1)
    gate_weight = w_expert_gate[0]
    up_expert = w_expert_up[0]
    down_expert = w_expert_down[0]
    hidden_weights = (wide_weight, shared_down, gate_weight, up_expert, down_expert.T)
    transposed = (gate_weight.T, up_expert.T, shared_in.T, shared_down.T)

    def slots_of(micro):
        hit = jnp.any(routes_all[:, micro] == expert, axis=-1)
        rank = jnp.cumsum(hit.astype(jnp.int32), axis=1) - 1
        return jnp.where(hit, rank, -1)[:, None, :]

    def hidden_of(seats, tokens, top):
        return hidden_stage(
            place, seats, tokens, top, hidden_weights, capacity, experts, hidden
        )

    def grads_to_tokens(seats, made):
        return combine_stage(
            place, seats, made[3:5], transposed[:2], made[6], transposed[2], capacity
        )

    def outputs_to_tokens(seats, made):
        return combine_stage(
            place, seats, made[2:3], (down_expert,), made[5], transposed[3], capacity
        )

    def routed_grads(made):
        taken, taken_top, hidden_gated, pre_grad, up_grad, _, _, _ = made
        return (
            left_product(taken, pre_grad),
            left_product(taken, up_grad),
            left_product(hidden_gated, taken_top),
        )

    def shared_grads_of(tokens, top, made):
        return left_product(tokens, made[6]), left_product(top, made[5])

    def added(function):
        def call(before, *values):
            return tuple(old + new for old, new in zip(before, function(*values)))

        return call

    def gate_grads_home(made):
        return Flow(exchange(made[-1].reshape(devices, rows), BOTH))

    def home_backward(micro, grad_two, gate_grad):
        _, unit_two, factor_two, normed_two = residuals[micro]
        logits = product(normed_two, router_weight)
        shifted = jnp.exp(logits - jnp.max(logits, axis=-1, keepdims=True))
        router = shifted / jnp.sum(shifted, axis=-1, keepdims=True)
        router_in = jnp.sum(gate_grad.reshape(experts, 2, rows), axis=1).T
        grad_logits = (
            router * (router_in - jnp.sum(router * router_in, axis=-1, keepdims=True))
        ).astype(BF16)
        grad_two = grad_two + right_product(grad_logits, router_weight)
        grad_residual = cotangent[micro].astype(F32) + norm_back(
            grad_two * gain_two, unit_two, factor_two
        )
        return (
            grad_residual,
            left_product(normed_two, grad_logits),
            jnp.sum(grad_two * unit_two, axis=0),
        )

    def attend_backward(grad_attn_out, projected, marks):
        grad_attended = to_relative(product(grad_attn_out, out_weight).astype(BF16))
        return attend_back_stage(factor, heads, projected[2] + marks, grad_attended)

    def projections_backward(grad_query, grad_turned, grad_key_value, grad_rope):
        grad_turned = grad_turned[:, : heads * ROPE].reshape(length, heads, ROPE)
        grad_turned = rotate(grad_turned, -angles[:, None, :]).reshape(length, -1)
        grad_query_raw = jnp.concatenate([grad_query, grad_turned.astype(BF16)], axis=1)
        grad_rope = jnp.sum(grad_rope[:, : heads * ROPE].reshape(length, heads, ROPE), axis=1)
        grad_key_value = grad_key_value.transpose(1, 0, 2).reshape(length, -1)
        grad_one_part = right_product(grad_query_raw, query_weight)
        grad_latent_part = right_product(grad_key_value, up_weight)
        back = jnp.concatenate([grad_one_part, grad_latent_part, grad_rope], axis=1)
        return back.astype(BF16), grad_query_raw, grad_key_value

    def head_grads(projected, attended, grad_attn_out, grad_query_raw, grad_key_value):
        return (
            left_product(projected[0], grad_query_raw),
            left_product(grad_attn_out, to_absolute(attended)),
            left_product(grad_key_value, projected[1]),
        )

    def latent_backward(back, projected):
        unit_latent, factor_latent = projected[3:]
        grad_latent_norm = back[:, width : width + KVR].astype(F32)
        grad_compressed = norm_back(grad_latent_norm * gain_latent, unit_latent, factor_latent)
        grad_latent = jnp.concatenate(
            [grad_compressed, rotate(back[:, width + KVR :].astype(F32), -own_angles)], axis=-1
        ).astype(BF16)
        return grad_latent, jnp.sum(grad_latent_norm * unit_latent, axis=0)

    def input_backward(micro, back, grad_latent, grad_residual):
        unit_one, factor_one = normed(tokens_in[micro].astype(F32))
        grad_one = back[:, :width].astype(F32) + right_product(grad_latent, down_weight)
        return (
            grad_residual + norm_back(grad_one * gain_one, unit_one, factor_one),
            jnp.sum(grad_one * unit_one, axis=0),
        )

    def line_blocks(value):
        return value.astype(BF16).reshape(line, -1, value.shape[-1])

    def down_grads(normed_one, latents):
        columns = lax.dynamic_slice_in_dim(
            normed_one, me_seq * (width // seqs), width // seqs, axis=1
        )
        return left_product(columns, latents)

    seats = [slots_of(micro) for micro in micros]
    made = [None, None]
    def home_and_out(micro):
        home = home_backward(micro, grads[micro].value, gate_grad[micro].value)
        return home, lax.all_gather(home[0].astype(BF16), "seq", axis=0, tiled=True)

    def attention_back(*given):
        return projections_backward(*attend_backward(*given))

    gate_grad = [None, None]
    grads = [None, None]
    sums = [None, None]
    homes = [None, None]
    attn_out = [None, None]
    backs = [None, None]
    back_sums = [None, None]
    latents = [None, None]
    latent_flows = [None, None]
    made[0] = slots.run([], hidden_of, seats[0], normed_alls[0], tops[0])
    gate_grad[0] = gate_grads_home(made[0])
    sides = slots.run([gate_grad[0]], grads_to_tokens, seats[0], made[0])
    grads[0] = Flow(reduce_all(*sides, rows))
    sides = slots.run([grads[0]], outputs_to_tokens, seats[0], made[0])
    sums[0] = Flow(reduce_all(*sides, rows))
    routed = slots.run([grads[0]], routed_grads, made[0])
    shared = slots.run([grads[0], sums[0]], shared_grads_of, normed_alls[0], tops[0], made[0])
    slots.run([grads[0]])
    slots.run([grads[0]])
    made[1] = slots.run([grads[0], sums[0]], hidden_of, seats[1], normed_alls[1], tops[1])
    slots.finish(grads[0])
    homes[0], attn_out[0] = home_and_out(0)
    gate_grad[1] = gate_grads_home(made[1])
    sides = slots.run([gate_grad[1], sums[0]], grads_to_tokens, seats[1], made[1])
    grads[1] = Flow(reduce_all(*sides, rows))
    sides = slots.run([grads[1], sums[0]], outputs_to_tokens, seats[1], made[1])
    sums[1] = Flow(reduce_all(*sides, rows))
    backs[0] = slots.run([grads[1]], attention_back, attn_out[0], projected[0], marks[0])
    back_sums[0] = Flow(scatter_seq(backs[0][0], rows))
    head_sums = slots.run(
        [grads[1], back_sums[0]],
        head_grads,
        projected[0],
        attended[0][0],
        attn_out[0],
        *backs[0][1:],
    )
    taken, taken_top, hidden_gated, pre_grad, up_grad, _, _, _ = made[1]
    parts = []
    for pair in ((taken, pre_grad), (taken, up_grad), (hidden_gated, taken_top)):
        parts.append(
            slots.run(
                [grads[1], back_sums[0], sums[0]],
                lambda old, left, right: old + left_product(left, right),
                routed[len(parts)],
                *pair,
            )
        )
    slots.finish(grads[1], back_sums[0])
    homes[1], attn_out[1] = home_and_out(1)
    slots.finish(back_sums[0])
    latents[0] = latent_backward(back_sums[0].value, projected[0])
    latent_flows[0] = Flow(gather_seq(latents[0][0]))
    slots.run([sums[1], sums[0], latent_flows[0]])
    shared = slots.run(
        [sums[1], latent_flows[0]],
        added(shared_grads_of),
        shared,
        normed_alls[1],
        tops[1],
        made[1],
    )
    shared = jnp.concatenate(
        [shared[0][:, :hidden], shared[0][:, lanes : lanes + hidden], shared[1][:, :hidden]],
        axis=1,
    )
    shared = Flow(exchange(shared.astype(BF16).reshape(devices, piece, 3 * hidden), BOTH))
    backs[1] = slots.run(
        [sums[1], latent_flows[0], shared], attention_back, attn_out[1], projected[1], marks[1]
    )
    back_sums[1] = Flow(scatter_seq(backs[1][0], rows))
    head_sums = slots.run(
        [back_sums[1], sums[1], sums[0]],
        added(head_grads),
        head_sums,
        projected[1],
        attended[1][0],
        attn_out[1],
        *backs[1][1:],
    )
    grad_heads = jnp.concatenate(head_sums[:2], axis=1).astype(BF16)
    grad_heads = Flow(exchange(grad_heads.reshape(devices, piece, -1), BOTH))
    grad_up = Flow(exchange(line_blocks(head_sums[2]), "fsdp"))
    slots.run([back_sums[1], sums[1], sums[0], grad_up])
    slots.finish(back_sums[1], sums[1], sums[0])
    latents[1] = latent_backward(back_sums[1].value, projected[1])
    latent_flows[1] = Flow(gather_seq(latents[1][0]))
    finals = [
        input_backward(micro, back_sums[micro].value, latents[micro][0], homes[micro][0])
        for micro in micros
    ]
    tiny = jnp.concatenate(
        [
            sum(home[1] for home in homes).reshape(devices, -1),
            sum(final[1] for final in finals).reshape(devices, -1),
            sum(home[2] for home in homes).reshape(devices, -1),
            sum(latent[1] for latent in latents).reshape(devices, -1),
        ],
        axis=1,
    )
    tiny = Flow(exchange(tiny, BOTH))
    slots.run([latent_flows[1], sums[1], sums[0]])
    slots.run([latent_flows[1], sums[1], sums[0], tiny])
    slots.finish(latent_flows[1], grad_heads)
    for flow in (sums[0], sums[1], latent_flows[0], tiny, grad_heads, shared, grad_up):
        slots.finish(flow)
    outputs = [
        (residuals[micro][0] + sums[micro].value).astype(BF16) for micro in micros
    ]
    grad_kv_down = sum(
        down_grads(projected[micro][0], latent_flows[micro].value) for micro in micros
    )
    grad_kv_down = lax.all_to_all(line_blocks(grad_kv_down), "fsdp", 0, 0, tiled=True)
    grad_kv_down = jnp.sum(grad_kv_down.astype(F32), axis=0)
    grad_kv_up = jnp.sum(grad_up.value.astype(F32), axis=0).T
    shared_grads = shared.value.astype(F32)
    grad_shared_gate = shared_grads[:, :, :hidden].transpose(1, 0, 2).reshape(piece, -1)
    grad_shared_up = shared_grads[:, :, hidden : 2 * hidden].transpose(1, 0, 2).reshape(piece, -1)
    grad_shared_down = shared_grads[:, :, 2 * hidden :].transpose(0, 2, 1).reshape(-1, piece)
    grad_heads = grad_heads.value.reshape(seqs, line, piece, -1)
    grad_heads = jnp.sum(grad_heads.astype(F32), axis=1)
    grad_query_weight = jnp.concatenate(
        [
            grad_heads[:, :, : heads * NOPE].reshape(seqs, piece, heads, NOPE),
            grad_heads[:, :, heads * NOPE : query_width].reshape(seqs, piece, heads, ROPE),
        ],
        axis=3,
    )
    grad_query_weight = grad_query_weight.transpose(1, 0, 2, 3).reshape(piece, -1)
    grad_out_weight = grad_heads[:, :, query_width:].transpose(0, 2, 1).reshape(-1, piece)
    tiny = jnp.sum(tiny.value, axis=0)
    first = piece * experts
    return (
        jnp.stack(outputs),
        jnp.stack([final[0] for final in finals]),
        tiny[first : first + piece],
        tiny[first + 2 * piece :],
        tiny[first + piece : first + 2 * piece],
        grad_query_weight,
        grad_kv_down,
        grad_kv_up,
        grad_out_weight,
        tiny[:first].reshape(piece, experts),
        grad_shared_gate,
        grad_shared_up,
        grad_shared_down,
        parts[0][None],
        parts[1][None],
        parts[2][None],
    )


def solution(mesh):
    return jax.shard_map(
        per_device,
        mesh=mesh,
        in_specs=(
            P("fsdp", "seq", None),
            P("fsdp", None),
            P("fsdp", "seq", None),
            P("fsdp", "seq", None),
            P(BOTH),
            P(BOTH),
            P(BOTH),
            P(BOTH, None),
            P(BOTH, None),
            P(None, BOTH),
            P(None, BOTH),
            P(BOTH, None),
            P(BOTH, None),
            P(BOTH, None),
            P(None, BOTH),
            P(BOTH, None, None),
            P(BOTH, None, None),
            P(BOTH, None, None),
        ),
        out_specs=(
            P("fsdp", "seq", None),
            P("fsdp", "seq", None),
            P(BOTH),
            P(BOTH),
            P(BOTH),
            P(BOTH, None),
            P(BOTH, None),
            P(None, BOTH),
            P(None, BOTH),
            P(BOTH, None),
            P(BOTH, None),
            P(BOTH, None),
            P(None, BOTH),
            P(BOTH, None, None),
            P(BOTH, None, None),
            P(BOTH, None, None),
        ),
        check_vma=False,
    )
```

time: 1900 us -> 1400 us (0.74)
  waiting for transfers between devices: 872 us -> 366 us
  starting transfers between devices: 308 us -> 167 us
  local copies, waits for them, and re-layouts: 149 us -> 217 us
  Pallas kernels: 195 us -> 248 us
  other arithmetic: 150 us -> 188 us
    all_gather x9 -> x6, waiting for transfers between devices: 369 us -> 90.7 us  [the longest x1 80.5 us: per_device(): normed_alls[0] = lax.all_gather(residuals[0][3], BOTH, axis=0, tiled=True)]
    ppermute x72 -> x76, starting transfers between devices: 217 us -> 104 us  [the longest x64 58.8 us: swap(): return lax.ppermute(value, 'seq', [(i, i ^ 1 << bit) for i in range(count)])]
    reduce_scatter x4 -> x0, waiting for transfers between devices: 86.6 us -> none  [the longest x2 86.6 us: per_device(): summed = lax.psum_scatter(out_part, 'seq', scatter_dimension=0, tiled=True)]
    all_gather x1, waiting for transfers between devices: 61.9 us -> 0.01 us  [per_device(): small = lax.all_gather(small, BOTH, axis=0, tiled=True)]
    pallas_call x0 -> x4, Pallas kernels: none -> 53.3 us  [the longest x2 31.9 us: attend_back_stage(): pl.pallas_call(functools.partial(attend_back_kernel, factor), grid=(lengt...]
    ppermute x72 -> x76, waiting for transfers between devices: 272 us -> 224 us  [the longest x64 202 us: swap(): return lax.ppermute(value, 'seq', [(i, i ^ 1 << bit) for i in range(count)])]
    convert_element_type x68 -> x52, other arithmetic: 57 us -> 99.2 us  [add_pair(): return (left.astype(F32) + right.astype(F32)).astype(BF16)]
    optimization_barrier x0 -> x23, local copies, waits for them, and re-layouts: none -> 37.3 us  [the longest x7 20.4 us: run(): lax.optimization_barrier((pending, made, self.token))]
  transfers between devices with their start and end apart: 132 -> 105, of which waited for: 54 -> 42; matrix products, arithmetic and copies ran while one was open for 24% -> 38% of each run, Pallas kernels for 10% -> 18%
where the time goes in v2:
time: 1400 us; the launch traced here: 1390 us
  waiting for transfers between devices  366 us (26%)
  Pallas kernels  248 us (18%)
  local copies, waits for them, and re-layouts  217 us (16%)
  other arithmetic  188 us (13%)
  matrix products  188 us (13%)
  starting transfers between devices  167 us (12%)
  between operations  18.1 us (1%)
    ppermute x64, waiting for transfers between devices, swap(): return lax.ppermute(value, 'seq', [(i, i ^ 1 << bit) for i in range(count)])  202 us
    dot_general x20, matrix products, left_product(): lax.dot_general(left, right, (((0,), (0,)), ((), ())), preferred_element_...  131 us
    pallas_call x4, Pallas kernels, combine_stage(): pl.pallas_call(functools.partial(combine_kernel, blocks, capacity, cuts,...  101 us
    convert_element_type x52, other arithmetic, add_pair(): return (left.astype(F32) + right.astype(F32)).astype(BF16)  99.2 us
    pallas_call x2, Pallas kernels, hidden_stage(): pl.pallas_call(functools.partial(hidden_kernel, blocks, capacity, experts...  93.8 us
    all_gather x1, waiting for transfers between devices, per_device(): normed_alls[0] = lax.all_gather(residuals[0][3], BOTH, axis=0, tiled=True)  80.5 us
    ppermute x64, starting transfers between devices, swap(): return lax.ppermute(value, 'seq', [(i, i ^ 1 << bit) for i in range(count)])  58.8 us
    ppermute x12, starting transfers between devices, line_reduce(): lax.ppermute(send_up, 'fsdp', [(i, i + 1) for i in range(step)])  45.3 us
  transfers between devices with their start and end apart: 105, of which 42 were waited for; matrix products, arithmetic and copies ran while one was open for 38% of the time, Pallas kernels for 18%

profile of v2, /device:TPU:0, one launch (start us, length us, event | category | flops | bytes accessed | tf_op | source)
XLA Modules:
  0.0 1391.2 jit_solution(17660658498508973776)
XLA Ops:
  40.2 24.6 %collective-permute-done = bf16[128,1024]{1,0:T(8,128)(2,1)S(1)} collective-permute-done((bf16[128,1024]{1,0:T(8,128)(2,1)S(1)}, bf16[128,1024]{1,0:T(8,128)(2,1)S(1)}, u32[]{:S(2)}, u32[]{:S(2)}) %collective-permute-start) | collective-permute-done | bytes 262176 | tf_op jit(solution)/shard_map/ppermute | solution.py:68
  76.5 20.2 %collective-permute-done.4 = bf16[2,128,1024]{2,1,0:T(8,128)(2,1)S(1)} collective-permute-done((bf16[2,128,1024]{2,1,0:T(8,128)(2,1)S(1)}, bf16[2,128,1024]{2,1,0:T(8,128)(2,1)S(1)}, u32[]{:S(2)}, u32[]{:S(2)}) %collective-permute-start.4) | collective-permute-done | bytes 524320 | tf_op jit(solution)/shard_map/ppermute | solution.py:68
  96.8 11.6 collective-permute-done.6
  175.2 10.8 attend_stage.2
  229.4 10.6 attend_stage.3
  262.2 11.2 collective-permute-done.16
  318.8 80.5 %all-gather.10.cloned.1.call-done.tokens_ref = bf16[4096,2048]{1,0:T(8,128)(2,1)} async-done(((bf16[128,2048]{1,0:T(8,128)(2,1)}), bf16[4096,2048]{1,0:T(8,128)(2,1)}) %all-gather.10.cloned.1.call-update) | async-done | bytes 16777232 | tf_op jit(solution)/shard_map/all_gather | solution.py:750
  399.3 47.1 %hidden_stage.2 = (bf16[2048,2048]{1,0:T(8,128)(2,1)}, bf16[2048,2048]{1,0:T(8,128)(2,1)}, bf16[2048,704]{1,0:T(8,128)(2,1)}, bf16[2048,704]{1,0:T(8,128)(2,1)},...) custom-call(s32[3]{0:T(128)} %pad_add_fusion.place_ref, ...), custom_call_target="tpu_custom_call" | custom-call | flops 24159191040 | bytes 50331648 | tf_op jit(solution)/shard_map/hidden_stage/pallas_call | solution.py:464
  449.2 29.3 %combine_stage.4 = (bf16[2048,1024]{1,0:T(8,128)(2,1)}, bf16[2048,1024]{1,0:T(8,128)(2,1)}, bf16[2048,1024]{1,0:T(8,128)(2,1)}, bf16[2048,1024]{1,0:T(8,128)(2,1)}) custom-call(s32[3]{0:T(128)} %pad_add_fusion.place_ref, s32[32,1,128]{2,1,0:T(1,128)} %copy_select_fusion.1.slots_ref, bf16[2048,704]{1,0:T(8,128)(2,1)} %get-tuple-element.475.refs_0_, ...), custom_call_target="tpu_custom_call" | custom-call | flops 17179869184 | bytes 25165824 | tf_op jit(solution)/shard_map/combine_stage/pallas_call | solution.py:560
  482.3 21.2 %combine_stage.5 = (bf16[2048,1024]{1,0:T(8,128)(2,1)}, bf16[2048,1024]{1,0:T(8,128)(2,1)}, bf16[2048,1024]{1,0:T(8,128)(2,1)}, bf16[2048,1024]{1,0:T(8,128)(2,1)}) custom-call(s32[3]{0:T(128)} %pad_add_fusion.place_ref, s32[32,1,128]{2,1,0:T(1,128)} %copy_select_fusion.1.slots_ref, bf16[2048,704]{1,0:T(8,128)(2,1)} %get-tuple-element.477.refs_0_, ...), custom_call_target="tpu_custom_call" | custom-call | flops 9126805504 | bytes 25165824 | tf_op jit(solution)/shard_map/combine_stage/pallas_call | solution.py:560
  517.9 11.1 fusion.265
  539.7 10.8 fusion.267
  550.5 21.7 %collective-permute-done.22 = bf16[2,4,128,1024]{3,2,1,0:T(8,128)(2,1)S(1)} collective-permute-done((bf16[2,4,128,1024]{3,2,1,0:T(8,128)(2,1)S(1)}, bf16[2,4,128,1024]{3,2,1,0:T(8,128)(2,1)S(1)}, u32[]{:S(2)}, u32[]{:S(2)}) %collective-permute-start.22) | collective-permute-done | bytes 2097184 | tf_op jit(solution)/shard_map/ppermute | solution.py:68
  590.7 11.5 fusion.269
  672.8 46.7 %hidden_stage.3 = (bf16[2048,2048]{1,0:T(8,128)(2,1)}, bf16[2048,2048]{1,0:T(8,128)(2,1)}, bf16[2048,704]{1,0:T(8,128)(2,1)}, bf16[2048,704]{1,0:T(8,128)(2,1)},...) custom-call(s32[3]{0:T(128)} %pad_add_fusion.place_ref, ...), custom_call_target="tpu_custom_call" | custom-call | flops 24159191040 | bytes 50331648 | tf_op jit(solution)/shard_map/hidden_stage/pallas_call | solution.py:464
  742.9 29.1 %combine_stage.6 = (bf16[2048,1024]{1,0:T(8,128)(2,1)}, bf16[2048,1024]{1,0:T(8,128)(2,1)}, bf16[2048,1024]{1,0:T(8,128)(2,1)}, bf16[2048,1024]{1,0:T(8,128)(2,1)}) custom-call(s32[3]{0:T(128)} %pad_add_fusion.place_ref, s32[32,1,128]{2,1,0:T(1,128)} %copy_select_fusion.slots_ref, bf16[2048,704]{1,0:T(8,128)(2,1)} %get-tuple-element.588.refs_0_, ...), custom_call_target="tpu_custom_call" | custom-call | flops 17179869184 | bytes 25165824 | tf_op jit(solution)/shard_map/combine_stage/pallas_call | solution.py:560
  786.7 21.0 %combine_stage.7 = (bf16[2048,1024]{1,0:T(8,128)(2,1)}, bf16[2048,1024]{1,0:T(8,128)(2,1)}, bf16[2048,1024]{1,0:T(8,128)(2,1)}, bf16[2048,1024]{1,0:T(8,128)(2,1)}) custom-call(s32[3]{0:T(128)} %pad_add_fusion.place_ref, s32[32,1,128]{2,1,0:T(1,128)} %copy_select_fusion.slots_ref, bf16[2048,704]{1,0:T(8,128)(2,1)} %get-tuple-element.611.refs_0_, ...), custom_call_target="tpu_custom_call" | custom-call | flops 9126805504 | bytes 25165824 | tf_op jit(solution)/shard_map/combine_stage/pallas_call | solution.py:560
  839.9 15.9 %attend_back_stage.2 = (bf16[1024,256]{1,0:T(8,128)(2,1)}, f32[1024,128]{1,0:T(8,128)}, bf16[2,1024,256]{2,1,0:T(8,128)(2,1)}, f32[1024,128]{1,0:T(8,128)}) custom-call(bf16[1024,256]{1,0:T(8,128)(2,1)} %copy.542.qn_ref, bf16[1024,128]{1,0:T(8,128)(2,1)} %copy.465.qr_ref, bf16[1024,512]{1,0:T(8,128)(2,1)} %convolution_convert_fusion.7.kv_ref, ...), custom_call_target="tpu_custom_call" | custom-call | flops 4294967296 | bytes 4194304 | tf_op jit(solution)/shard_map/attend_back_stage/pallas_call | solution.py:415
  946.1 12.0 convolution_add_fusion.2
  986.7 11.8 convolution_add_fusion.1
  1065.9 32.7 %collective-permute-done.68 = bf16[2,128,192]{2,1,0:T(8,128)(2,1)S(1)} collective-permute-done((bf16[2,128,192]{2,1,0:T(8,128)(2,1)S(1)}, bf16[2,128,192]{2,1,0:T(8,128)(2,1)S(1)}, u32[]{:S(2)}, u32[]{:S(2)}) %collective-permute-start.68) | collective-permute-done | bytes 98336 | tf_op jit(solution)/shard_map/ppermute | solution.py:68
  1135.4 16.0 %attend_back_stage.3 = (bf16[1024,256]{1,0:T(8,128)(2,1)}, f32[1024,128]{1,0:T(8,128)}, bf16[2,1024,256]{2,1,0:T(8,128)(2,1)}, f32[1024,128]{1,0:T(8,128)}) custom-call(bf16[1024,256]{1,0:T(8,128)(2,1)} %copy.543.qn_ref, bf16[1024,128]{1,0:T(8,128)(2,1)} %copy.487.qr_ref, bf16[1024,512]{1,0:T(8,128)(2,1)} %convolution_convert_fusion.6.kv_ref, ...), custom_call_target="tpu_custom_call" | custom-call | flops 4294967296 | bytes 4194304 | tf_op jit(solution)/shard_map/attend_back_stage/pallas_call | solution.py:415
  1238.6 15.1 %all-to-all-done.6 = bf16[4,128,512]{2,1,0:T(8,128)(2,1)} async-done(((bf16[4,128,512]{2,1,0:T(8,128)(2,1)}), bf16[4,128,512]{2,1,0:T(8,128)(2,1)}, u32[]{:S(2)}, u32[]{:S(2)}) %all-to-all-start.6) | async-done | bytes 524320 | tf_op jit(solution)/shard_map/all_to_all | solution.py:166
  1351.7 14.5 %all-to-all-done.8 = bf16[32,64,640]{2,1,0:T(8,128)(2,1)} async-done(((bf16[32,64,640]{2,1,0:T(8,128)(2,1)}), bf16[32,64,640]{2,1,0:T(8,128)(2,1)}, u32[]{:S(2)}, u32[]{:S(2)}) %all-to-all-start.8) | async-done | bytes 2621472 | tf_op jit(solution)/shard_map/all_to_all | solution.py:166
  (1021 shorter events, 836.3 us)
Async XLA Ops:
  15.4 101.8 %all-gather.8.cloned.1.call-start = ((), (), s32[]{:S(2)}) async-start(), calls=%async_computation.10 | async-start | bytes 2703360 | tf_op jit(solution)/shard_map/all_gather | solution.py:651
  31.8 85.5 %all-to-all-start = ((bf16[32,64,640]{2,1,0:T(8,128)(2,1)}), bf16[32,64,640]{2,1,0:T(8,128)(2,1)}, u32[]{:S(2)}, u32[]{:S(2)}) async-start(bf16[32,64,640]{2,1,0:T(8,128)(2,1)} %bitcast.708), calls=%async_computation | async-start | bytes 5242880 | tf_op jit(solution)/shard_map/all_to_all | solution.py:668
  35.6 283.2 %all-gather.12.cloned.1.call-start = ((), (), s32[]{:S(2)}) async-start(), calls=%async_computation.12 | async-start | bytes 17301504 | tf_op jit(solution)/shard_map/all_gather | solution.py:685
  132.1 82.9 %all-to-all-start.2 = ((bf16[32,64,264]{2,1,0:T(8,128)(2,1)}), bf16[32,64,264]{2,1,0:T(8,128)(2,1)}, u32[]{:S(2)}, u32[]{:S(2)}) async-start(bf16[32,64,264]{2,1,0:T(8,128)(2,1)} %pad_maximum_fusion.8), calls=%async_computation.2 | async-start | bytes 3145728 | tf_op jit(solution)/shard_map/all_to_all | solution.py:166
  137.4 261.9 %all-gather.10.cloned.1.call-start = ((), (), s32[]{:S(2)}) async-start(), calls=%async_computation.11 | async-start | bytes 17301504 | tf_op jit(solution)/shard_map/all_gather | solution.py:750
  284.3 378.3 %all-gather.14.cloned.1.call-start = ((), (), s32[]{:S(2)}) async-start(), calls=%async_computation.13 | async-start | bytes 17301504 | tf_op jit(solution)/shard_map/all_gather | solution.py:753
  284.8 388.0 %all-gather.16.cloned.1.call-start = ((), (), s32[]{:S(2)}) async-start(), calls=%async_computation.14 | async-start | bytes 17301504 | tf_op jit(solution)/shard_map/all_gather | solution.py:755
  509.3 62.9 %collective-permute-start.22 = (bf16[2,4,128,1024]{3,2,1,0:T(8,128)(2,1)S(1)}, bf16[2,4,128,1024]{3,2,1,0:T(8,128)(2,1)S(1)}, u32[]{:S(2)}, u32[]{:S(2)}) collective-permute-start(bf16[2,4,128,1024]{3,2,1,0:T(8,128)(2,1)S(1)} %slice_bitcast_fusion.6), channel_id=1, source_target_pairs={{0,8},{4,12},{8,0},{12,4},{16,24},{20,28},{24,16},{28,20},{1,9},{5... | collective-permute-start | bytes 6291464 | tf_op jit(solution)/shard_map/ppermute | solution.py:68
  516.1 59.6 %collective-permute-start.23 = (bf16[2,4,128,1024]{3,2,1,0:T(8,128)(2,1)S(1)}, bf16[2,4,128,1024]{3,2,1,0:T(8,128)(2,1)S(1)}, u32[]{:S(2)}, u32[]{:S(2)}) collective-permute-start(bf16[2,4,128,1024]{3,2,1,0:T(8,128)(2,1)S(1)} %bitcast.762), channel_id=1, source_target_pairs={{0,16},{4,20},{8,24},{12,28},{16,0},{20,4},{24,8},{28,12},{1,17},{... | collective-permute-start | bytes 6291464 | tf_op jit(solution)/shard_map/ppermute | solution.py:68
  539.2 76.2 %collective-permute-start.26 = (bf16[2048,1024]{1,0:T(8,128)(2,1)}, bf16[2048,1024]{1,0:T(8,128)(2,1)S(1)}, u32[]{:S(2)}, u32[]{:S(2)}) collective-permute-start(bf16[2048,1024]{1,0:T(8,128)(2,1)} %get-tuple-element.481), channel_id=1, source_target_pairs={{0,4},{4,0},{8,12},{12,8},{16,20},{20,16},{24,28},{28,24},{1,5},{5... | collective-permute-start | bytes 12582920 | tf_op jit(solution)/shard_map/ppermute | solution.py:68
  539.6 75.8 %collective-permute-start.27 = (bf16[2048,1024]{1,0:T(8,128)(2,1)}, bf16[2048,1024]{1,0:T(8,128)(2,1)S(1)}, u32[]{:S(2)}, u32[]{:S(2)}) collective-permute-start(bf16[2048,1024]{1,0:T(8,128)(2,1)} %get-tuple-element.482), channel_id=1, source_target_pairs={{0,4},{4,0},{8,12},{12,8},{16,20},{20,16},{24,28},{28,24},{1,5},{5... | collective-permute-start | bytes 12582920 | tf_op jit(solution)/shard_map/ppermute | solution.py:68
  624.4 95.1 %collective-permute-start.34 = (bf16[2,4,128,1024]{3,2,1,0:T(8,128)(2,1)}, bf16[2,4,128,1024]{3,2,1,0:T(8,128)(2,1)}, u32[]{:S(2)}, u32[]{:S(2)}) collective-permute-start(bf16[2,4,128,1024]{3,2,1,0:T(8,128)(2,1)} %slice_bitcast_fusion.4), channel_id=1, source_target_pairs={{0,8},{4,12},{8,0},{12,4},{16,24},{20,28},{24,16},{28,20},{1,9},{5... | collective-permute-start | bytes 6291464 | tf_op jit(solution)/shard_map/ppermute | solution.py:68
  646.2 73.3 %collective-permute-start.35 = (bf16[2,4,128,1024]{3,2,1,0:T(8,128)(2,1)}, bf16[2,4,128,1024]{3,2,1,0:T(8,128)(2,1)}, u32[]{:S(2)}, u32[]{:S(2)}) collective-permute-start(bf16[2,4,128,1024]{3,2,1,0:T(8,128)(2,1)} %bitcast.106), channel_id=1, source_target_pairs={{0,16},{4,20},{8,24},{12,28},{16,0},{20,4},{24,8},{28,12},{1,17},{... | collective-permute-start | bytes 6291464 | tf_op jit(solution)/shard_map/ppermute | solution.py:68
  654.4 65.1 %collective-permute-start.32 = (bf16[128,2048]{1,0:T(8,128)(2,1)S(1)}, bf16[128,2048]{1,0:T(8,128)(2,1)}, u32[]{:S(2)}, u32[]{:S(2)}) collective-permute-start(bf16[128,2048]{1,0:T(8,128)(2,1)S(1)} %get-tuple-element.828), channel_id=1, source_target_pairs={{0,1},{1,2},{2,3},{4,5},{5,6},{6,7},{8,9},{9,10},{10,11},{12,13},{... | collective-permute-start | bytes 1572872 | tf_op jit(solution)/shard_map/ppermute | solution.py:185
  726.7 101.4 %all-gather.18.cloned.1.call-start = ((), (), s32[]{:S(2)}) async-start(), calls=%async_computation.15 | async-start | bytes 4718592 | tf_op jit(solution)/shard_map/all_gather | solution.py:888
  742.4 382.1 %all-gather.20.cloned.1.call-start = ((), (), s32[]{:S(2)}) async-start(), calls=%async_computation.16 | async-start | bytes 4718592 | tf_op jit(solution)/shard_map/all_gather | solution.py:888
  888.4 69.7 %collective-permute-start.52 = (bf16[128,2048]{1,0:T(8,128)(2,1)}, bf16[128,2048]{1,0:T(8,128)(2,1)}, u32[]{:S(2)}, u32[]{:S(2)}) collective-permute-start(bf16[128,2048]{1,0:T(8,128)(2,1)} %get-tuple-element.821), channel_id=1, source_target_pairs={{2,1},{3,2},{6,5},{7,6},{10,9},{11,10},{14,13},{15,14},{18,17},{19... | collective-permute-start | bytes 1572872 | tf_op jit(solution)/shard_map/ppermute | solution.py:186
  958.1 68.5 %collective-permute-start.59 = (bf16[2048,1024]{1,0:T(8,128)(2,1)}, bf16[2048,1024]{1,0:T(8,128)(2,1)}, u32[]{:S(2)}, u32[]{:S(2)}) collective-permute-start(bf16[2048,1024]{1,0:T(8,128)(2,1)} %get-tuple-element.603), channel_id=1, source_target_pairs={{0,4},{4,0},{8,12},{12,8},{16,20},{20,16},{24,28},{28,24},{1,5},{5... | collective-permute-start | bytes 12582920 | tf_op jit(solution)/shard_map/ppermute | solution.py:68
  958.2 68.4 %collective-permute-start.60 = (bf16[2048,1024]{1,0:T(8,128)(2,1)}, bf16[2048,1024]{1,0:T(8,128)(2,1)}, u32[]{:S(2)}, u32[]{:S(2)}) collective-permute-start(bf16[2048,1024]{1,0:T(8,128)(2,1)} %get-tuple-element.604), channel_id=1, source_target_pairs={{0,4},{4,0},{8,12},{12,8},{16,20},{20,16},{24,28},{28,24},{1,5},{5... | collective-permute-start | bytes 12582920 | tf_op jit(solution)/shard_map/ppermute | solution.py:68
  1035.5 71.4 %collective-permute-start.65 = (bf16[2,4,128,1024]{3,2,1,0:T(8,128)(2,1)S(1)}, bf16[2,4,128,1024]{3,2,1,0:T(8,128)(2,1)S(1)}, u32[]{:S(2)}, u32[]{:S(2)}) collective-permute-start(bf16[2,4,128,1024]{3,2,1,0:T(8,128)(2,1)S(1)} %slice_bitcast_fusion), channel_id=1, source_target_pairs={{0,8},{4,12},{8,0},{12,4},{16,24},{20,28},{24,16},{28,20},{1,9},{5... | collective-permute-start | bytes 6291464 | tf_op jit(solution)/shard_map/ppermute | solution.py:68
  1042.5 64.3 %collective-permute-start.66 = (bf16[2,4,128,1024]{3,2,1,0:T(8,128)(2,1)S(1)}, bf16[2,4,128,1024]{3,2,1,0:T(8,128)(2,1)S(1)}, u32[]{:S(2)}, u32[]{:S(2)}) collective-permute-start(bf16[2,4,128,1024]{3,2,1,0:T(8,128)(2,1)S(1)} %bitcast.761), channel_id=1, source_target_pairs={{0,16},{4,20},{8,24},{12,28},{16,0},{20,4},{24,8},{28,12},{1,17},{... | collective-permute-start | bytes 6291464 | tf_op jit(solution)/shard_map/ppermute | solution.py:68
  1045.3 61.5 %collective-permute-start.67 = (bf16[2,128,384]{2,1,0:T(8,128)(2,1)S(1)}, bf16[2,128,384]{2,1,0:T(8,128)(2,1)S(1)}, u32[]{:S(2)}, u32[]{:S(2)}) collective-permute-start(bf16[2,128,384]{2,1,0:T(8,128)(2,1)S(1)} %get-tuple-element.881), channel_id=1, source_target_pairs={{0,16},{4,20},{8,24},{12,28},{16,0},{20,4},{24,8},{28,12},{1,17},{... | collective-permute-start | bytes 589832 | tf_op jit(solution)/shard_map/ppermute | solution.py:68
  1109.0 61.1 %collective-permute-start.69 = (bf16[4,128,1024]{2,1,0:T(8,128)(2,1)}, bf16[4,128,1024]{2,1,0:T(8,128)(2,1)}, u32[]{:S(2)}, u32[]{:S(2)}) collective-permute-start(bf16[4,128,1024]{2,1,0:T(8,128)(2,1)} %slice_bitcast_fusion.13), channel_id=1, source_target_pairs={{0,16},{4,20},{8,24},{12,28},{16,0},{20,4},{24,8},{28,12},{1,17},{... | collective-permute-start | bytes 3145736 | tf_op jit(solution)/shard_map/ppermute | solution.py:68
  1303.5 62.7 %all-to-all-start.8 = ((bf16[32,64,640]{2,1,0:T(8,128)(2,1)}), bf16[32,64,640]{2,1,0:T(8,128)(2,1)}, u32[]{:S(2)}, u32[]{:S(2)}) async-start(bf16[32,64,640]{2,1,0:T(8,128)(2,1)} %pad_maximum_fusion.4), calls=%async_computation.8 | async-start | bytes 5242880 | tf_op jit(solution)/shard_map/all_to_all | solution.py:166
  (287 other events, 4184.6 us)
Sparse Core Ops, SparseCore 0:
  21.2 81.5 all-gather.7
  117.4 148.9 all-gather.11
  284.4 114.8 all-gather.9
  402.1 113.3 all-gather.13
  518.3 154.4 all-gather.15
  742.5 44.2 all-gather.17
  1029.8 54.9 all-gather.19

commit v3 on v2

--- a/solution.py
+++ b/solution.py
@@ -59,10 +59,6 @@
     return (value * logistic, logistic * (1.0 + value * (1.0 - logistic)))
 
 
-def add_pair(left, right):
-    return (left.astype(F32) + right.astype(F32)).astype(BF16)
-
-
 def swap(value, bit):
     count = lax.axis_size("seq")
     return lax.ppermute(value, "seq", [(i, i ^ (1 << bit)) for i in range(count)])
@@ -129,20 +125,22 @@
     return [stacked(part, order[::-1]) for part, order in zip(parts, orders)]
 
 
-def fold(parts, lead):
+def total_of(terms):
+    return sum((term.astype(F32) for term in terms[1:]), terms[0].astype(F32))
+
+
+def fold(parts):
     bits = chip_bits()
     for step in range(len(bits)):
         kept, sent = [], []
-        for part, order in zip(parts, (bits, bits[::-1])):
-            names = sorted(order[step:], reverse=True)
-            part = part.reshape((2,) * len(names) + part.shape[lead:])
-            axis = names.index(order[step])
-            kept.append(lax.index_in_dim(part, 0, axis, keepdims=False))
-            sent.append(swap(lax.index_in_dim(part, 1, axis, keepdims=False), order[step]))
+        for terms, order in zip(parts, (bits, bits[::-1])):
+            axis = sorted(order[step:], reverse=True).index(order[step])
+            kept.append([lax.index_in_dim(term, 0, axis, keepdims=False) for term in terms])
+            send = total_of([lax.index_in_dim(term, 1, axis, keepdims=False) for term in terms])
+            sent.append(swap(send.astype(BF16), order[step]))
         arrived = yield sent
-        parts = [add_pair(keep, got) for keep, got in zip(kept, arrived)]
-        lead = len(bits) - step - 1
-    return parts
+        parts = [terms + [got] for terms, got in zip(kept, arrived)]
+    return [total_of(terms) for terms in parts]
 
 
 def gather_seq(own):
@@ -155,9 +153,10 @@
 def scatter_seq(value, rows):
     half = value.shape[0] // 2
     (far,) = yield [swap(value[half:], 0)]
-    near = add_pair(value[:half], far).reshape(-1, rows, value.shape[1])
+    shape = (2,) * len(chip_bits()) + (rows, value.shape[1])
+    terms = [value[:half].reshape(shape), far.reshape(shape)]
     parts = yield from fold(
-        [near[..., low:high] for low, high in halves_of(value.shape[1])], 1
+        [[term[..., low:high] for term in terms] for low, high in halves_of(value.shape[1])]
     )
     return jnp.concatenate(parts, axis=-1)
 
@@ -167,36 +166,100 @@
     return arrived
 
 
-def line_reduce(value):
+def exchange_line(value):
     count = lax.axis_size("fsdp")
     place = lax.axis_index("fsdp")
 
     def piece(index):
-        return lax.dynamic_index_in_dim(value, jnp.clip(index, 0, count - 1), 0, keepdims=False)
-
-    up = down = None
+        return lax.dynamic_index_in_dim(value, index % count, 0, keepdims=False)
+
+    arrived = yield [
+        lax.ppermute(
+            piece(place + turn), "fsdp", [(i, (i + turn) % count) for i in range(count)]
+        )
+        for turn in range(1, count)
+    ]
+    return sum((part.astype(F32) for part in arrived), piece(place).astype(F32))
+
+
+def line_gather(own):
+    count = lax.axis_size("fsdp")
+    ups, downs = [], []
+    up = down = own
     for step in range(1, count):
-        send_up = piece(place + count - step)
-        send_down = piece(place - count + step)
-        if up is not None:
-            send_up = add_pair(send_up, up)
-            send_down = add_pair(send_down, down)
         up, down = yield [
-            lax.ppermute(send_up, "fsdp", [(i, i + 1) for i in range(step)]),
-            lax.ppermute(send_down, "fsdp", [(i, i - 1) for i in range(count - step, count)]),
+            lax.ppermute(up, "fsdp", [(i, i + 1) for i in range(step - 1, count - 1)]),
+            lax.ppermute(down, "fsdp", [(i, i - 1) for i in range(1, count - step + 1)]),
         ]
-    return piece(place).astype(F32) + up.astype(F32) + down.astype(F32)
+        ups.append(up)
+        downs.append(down)
+    around = jnp.stack(ups[::-1] + [own] + downs)
+    return lax.dynamic_slice_in_dim(around, count - 1 - lax.axis_index("fsdp"), count, 0)
+
+
+def gather_all(own, place):
+    width = own.shape[1]
+    block = yield from line_gather(own)
+    block = block.reshape(-1, width)
+    near = [block[:, low:high] for low, high in halves_of(width)]
+    fresh, far = near, None
+    bits = chip_bits()
+    orders = (bits, bits[::-1])
+    for step in range(len(bits)):
+        arrived = yield [swap(part, order[step]) for part, order in zip(near, orders)] + [
+            swap(part, 0) for part in fresh
+        ]
+        fresh, crossed = arrived[:2], arrived[2:]
+        near = [jnp.stack(pair) for pair in zip(near, fresh)]
+        far = crossed if far is None else [jnp.stack(pair) for pair in zip(far, crossed)]
+    crossed = yield [swap(part, 0) for part in fresh]
+    far = [jnp.stack(pair) for pair in zip(far, crossed)]
+    parts = [stacked(part, order[::-1]) for part, order in zip(near + far, orders + orders)]
+    return assemble(place, parts)
 
 
 def reduce_all(keeps, sends, rows):
     arrived = yield [swap(send, 0) for send in sends]
-    line = lax.axis_size("fsdp")
-    parts = [
-        add_pair(keep, got).reshape(-1, line, rows, keep.shape[-1])
-        for keep, got in zip(keeps, arrived)
-    ]
-    parts = yield from fold(parts, 1)
-    return (yield from line_reduce(jnp.concatenate(parts, axis=-1)))
+    shape = (2,) * len(chip_bits()) + (lax.axis_size("fsdp"), rows, keeps[0].shape[-1])
+    parts = yield from fold(
+        [[keep.reshape(shape), got.reshape(shape)] for keep, got in zip(keeps, arrived)]
+    )
+    parts = [part.astype(BF16) for part in parts]
+    return (yield from exchange_line(jnp.concatenate(parts, axis=-1)))
+
+
+def assemble_kernel(place_ref, low_ref, high_ref, other_low_ref, other_high_ref, out_ref):
+    count, middle = low_ref.shape[1:]
+    core = place_ref[1]
+    own = pl.ds(pl.multiple_of(core * count, count), count)
+    other = pl.ds(pl.multiple_of((1 - core) * count, count), count)
+    out_ref[own, :middle] = low_ref[0]
+    out_ref[own, middle:] = high_ref[0]
+    out_ref[other, :middle] = other_low_ref[0]
+    out_ref[other, middle:] = other_high_ref[0]
+
+
+def assemble(place, parts):
+    chips, count, _ = parts[0].shape
+    width = parts[0].shape[2] + parts[1].shape[2]
+    return pl.pallas_call(
+        assemble_kernel,
+        grid_spec=pltpu.PrefetchScalarGridSpec(
+            num_scalar_prefetch=1,
+            grid=(chips,),
+            in_specs=[
+                pl.BlockSpec((1,) + part.shape[1:], lambda i, place: (i ^ place[2], 0, 0))
+                for part in parts
+            ],
+            out_specs=pl.BlockSpec((2 * count, width), lambda i, _: (i, 0)),
+        ),
+        out_shape=jax.ShapeDtypeStruct((2 * chips * count, width), BF16),
+        compiler_params=pltpu.CompilerParams(vmem_limit_bytes=VMEM_LIMIT),
+        cost_estimate=pl.CostEstimate(
+            flops=0, bytes_accessed=8 * chips * count * width, transcendentals=0
+        ),
+        name="assemble",
+    )(place, *parts)
 
 
 def one_hot(slots, capacity):
@@ -204,7 +267,7 @@
     return lax.broadcasted_iota(jnp.int32, (capacity, rows), 0) == slots
 
 
-def hidden_kernel(
+def forward_kernel(
     blocks,
     capacity,
     experts,
@@ -212,32 +275,28 @@
     place_ref,
     slots_ref,
     tokens_ref,
-    top_ref,
     wide_ref,
-    shared_ref,
     gate_ref,
     up_ref,
-    down_ref,
     taken_ref,
-    taken_top_ref,
     hidden_ref,
-    pre_ref,
-    post_ref,
+    to_pre_ref,
+    to_up_ref,
+    made_ref,
     shared_hidden_ref,
-    shared_grad_ref,
-    gate_grad_ref,
+    shared_to_pre_ref,
+    shared_to_up_ref,
 ):
     rows = slots_ref.shape[-1]
-    lanes = shared_ref.shape[-1]
+    lanes = shared_hidden_ref.shape[-1]
     expert = place_ref[0]
     wide = jnp.dot(tokens_ref[...], wide_ref[...], preferred_element_type=F32)
-    back = jnp.dot(top_ref[...], shared_ref[...], preferred_element_type=F32)
     first = wide[:, :lanes]
     second = wide[:, lanes:]
     silu, slope = silu_parts(first)
     shared_hidden_ref[...] = (silu * second).astype(BF16)
-    shared_grad_ref[:, :lanes] = (back * second * slope).astype(BF16)
-    shared_grad_ref[:, lanes:] = (back * silu).astype(BF16)
+    shared_to_pre_ref[...] = (second * slope).astype(BF16)
+    shared_to_up_ref[...] = silu.astype(BF16)
     lane = lax.broadcasted_iota(jnp.int32, first.shape, 1)
     logits = jnp.where((lane >= hidden) & (lane < hidden + experts), first, NEGATIVE)
     powers = jnp.exp(logits - jnp.max(logits, axis=-1, keepdims=True))
@@ -247,14 +306,10 @@
     slot_gates = []
     for block in range(blocks):
         chosen = one_hot(slots_ref[block], capacity)
-        low = chosen.astype(BF16)
-        own = pl.ds(block * rows, rows)
-        there = pl.ds(block * capacity, capacity)
-        taken_ref[there, :] = jnp.dot(
-            low, tokens_ref[own, :], preferred_element_type=F32
-        ).astype(BF16)
-        taken_top_ref[there, :] = jnp.dot(
-            low, top_ref[own, :], preferred_element_type=F32
+        taken_ref[pl.ds(block * capacity, capacity), :] = jnp.dot(
+            chosen.astype(BF16),
+            tokens_ref[pl.ds(block * rows, rows), :],
+            preferred_element_type=F32,
         ).astype(BF16)
         slot_gates.append(
             jnp.dot(
@@ -267,14 +322,46 @@
     slot_gates = jnp.concatenate(slot_gates, axis=0)
     gate_pre = jnp.dot(taken_ref[...], gate_ref[...], preferred_element_type=F32)
     up_pre = jnp.dot(taken_ref[...], up_ref[...], preferred_element_type=F32)
-    grad = jnp.dot(taken_top_ref[...], down_ref[...], preferred_element_type=F32)
     swish, slope = silu_parts(gate_pre)
     made = swish * up_pre
+    made_ref[...] = made.astype(BF16)
     hidden_ref[...] = (made * slot_gates).astype(BF16)
-    slot_grads = jnp.sum(made * grad, axis=-1, keepdims=True)
-    grad = grad * slot_gates
-    pre_ref[...] = (grad * up_pre * slope).astype(BF16)
-    post_ref[...] = (grad * swish).astype(BF16)
+    to_pre_ref[...] = (up_pre * slope * slot_gates).astype(BF16)
+    to_up_ref[...] = (swish * slot_gates).astype(BF16)
+
+
+def backward_kernel(
+    blocks,
+    capacity,
+    slots_ref,
+    top_ref,
+    to_pre_ref,
+    to_up_ref,
+    made_ref,
+    shared_to_pre_ref,
+    shared_to_up_ref,
+    shared_ref,
+    down_ref,
+    taken_top_ref,
+    pre_ref,
+    post_ref,
+    shared_grad_ref,
+    gate_grad_ref,
+):
+    rows = slots_ref.shape[-1]
+    lanes = shared_ref.shape[-1]
+    back = jnp.dot(top_ref[...], shared_ref[...], preferred_element_type=F32)
+    shared_grad_ref[:, :lanes] = (back * shared_to_pre_ref[...].astype(F32)).astype(BF16)
+    shared_grad_ref[:, lanes:] = (back * shared_to_up_ref[...].astype(F32)).astype(BF16)
+    for block in range(blocks):
+        chosen = one_hot(slots_ref[block], capacity).astype(BF16)
+        taken_top_ref[pl.ds(block * capacity, capacity), :] = jnp.dot(
+            chosen, top_ref[pl.ds(block * rows, rows), :], preferred_element_type=F32
+        ).astype(BF16)
+    grad = jnp.dot(taken_top_ref[...], down_ref[...], preferred_element_type=F32)
+    pre_ref[...] = (grad * to_pre_ref[...].astype(F32)).astype(BF16)
+    post_ref[...] = (grad * to_up_ref[...].astype(F32)).astype(BF16)
+    slot_grads = jnp.sum(made_ref[...].astype(F32) * grad, axis=-1, keepdims=True)
     for block in range(blocks):
         chosen = one_hot(slots_ref[block], capacity)
         gate_grad_ref[block] = jnp.sum(
@@ -446,59 +533,75 @@
     )
 
 
-def hidden_stage(place, slots, tokens, top, weights, capacity, experts, hidden):
-    wide_weight, shared_down, gate_weight, up_weight, down_weight = weights
+def rows_spec(size, columns):
+    return pl.BlockSpec((size, columns), lambda i, *_: (i, 0))
+
+
+def forward_stage(place, slots, tokens, weights, capacity, experts, hidden, lanes):
     devices, _, rows = slots.shape
     blocks = 2 * lax.axis_size("fsdp")
     steps = devices // blocks
     width = tokens.shape[1]
-    half = gate_weight.shape[1]
-    lanes = shared_down.shape[1]
+    half = weights[1].shape[1]
     count = blocks * capacity
-
-    def rows_spec(size, columns):
-        return pl.BlockSpec((size, columns), lambda i, *_: (i, 0))
-
-    slots_spec = pl.BlockSpec((blocks, 1, rows), lambda i, *_: (i, 0, 0))
-    flops = devices * 2 * (3 * capacity * width * half + rows * width * 3 * lanes)
+    sizes = [(count, width)] + [(count, half)] * 4 + [(blocks * rows, lanes)] * 3
     return pl.pallas_call(
-        functools.partial(hidden_kernel, blocks, capacity, experts, hidden),
+        functools.partial(forward_kernel, blocks, capacity, experts, hidden),
         grid_spec=pltpu.PrefetchScalarGridSpec(
             num_scalar_prefetch=1,
             grid=(steps,),
             in_specs=[
-                slots_spec,
-                rows_spec(blocks * rows, width),
+                pl.BlockSpec((blocks, 1, rows), lambda i, *_: (i, 0, 0)),
                 rows_spec(blocks * rows, width),
                 *[whole_spec(weight) for weight in weights],
             ],
-            out_specs=[
-                rows_spec(count, width),
-                rows_spec(count, width),
-                rows_spec(count, half),
-                rows_spec(count, half),
-                rows_spec(count, half),
-                rows_spec(blocks * rows, lanes),
-                rows_spec(blocks * rows, 2 * lanes),
-                slots_spec,
-            ],
+            out_specs=[rows_spec(*size) for size in sizes],
         ),
         out_shape=[
-            jax.ShapeDtypeStruct((steps * count, width), BF16),
-            jax.ShapeDtypeStruct((steps * count, width), BF16),
-            jax.ShapeDtypeStruct((steps * count, half), BF16),
-            jax.ShapeDtypeStruct((steps * count, half), BF16),
-            jax.ShapeDtypeStruct((steps * count, half), BF16),
-            jax.ShapeDtypeStruct((devices * rows, lanes), BF16),
-            jax.ShapeDtypeStruct((devices * rows, 2 * lanes), BF16),
-            jax.ShapeDtypeStruct(slots.shape, F32),
+            jax.ShapeDtypeStruct((steps * size, columns), BF16) for size, columns in sizes
         ],
         compiler_params=pltpu.CompilerParams(vmem_limit_bytes=VMEM_LIMIT),
         cost_estimate=pl.CostEstimate(
-            flops=flops, bytes_accessed=3 * devices * rows * width * 2, transcendentals=0
+            flops=devices * 4 * width * (capacity * half + rows * lanes),
+            bytes_accessed=3 * devices * rows * width,
+            transcendentals=devices * capacity * half,
         ),
-        name="hidden_stage",
-    )(place, slots, tokens, top, *weights)
+        name="forward_stage",
+    )(place, slots, tokens, *weights)
+
+
+def backward_stage(slots, top, saved, weights, capacity):
+    devices, _, rows = slots.shape
+    blocks = 2 * lax.axis_size("fsdp")
+    steps = devices // blocks
+    width = top.shape[1]
+    lanes, half = (weight.shape[1] for weight in weights)
+    count = blocks * capacity
+    slots_spec = pl.BlockSpec((blocks, 1, rows), lambda i, *_: (i, 0, 0))
+    sizes = [(count, width)] + [(count, half)] * 2 + [(blocks * rows, 2 * lanes)]
+    return pl.pallas_call(
+        functools.partial(backward_kernel, blocks, capacity),
+        grid=(steps,),
+        in_specs=[
+            slots_spec,
+            rows_spec(blocks * rows, width),
+            *[rows_spec(count, half) for _ in range(3)],
+            *[rows_spec(blocks * rows, lanes) for _ in range(2)],
+            *[whole_spec(weight) for weight in weights],
+        ],
+        out_specs=[rows_spec(*size) for size in sizes] + [slots_spec],
+        out_shape=[
+            jax.ShapeDtypeStruct((steps * size, columns), BF16) for size, columns in sizes
+        ]
+        + [jax.ShapeDtypeStruct(slots.shape, F32)],
+        compiler_params=pltpu.CompilerParams(vmem_limit_bytes=VMEM_LIMIT),
+        cost_estimate=pl.CostEstimate(
+            flops=devices * 2 * width * (capacity * half + rows * lanes),
+            bytes_accessed=4 * devices * rows * width,
+            transcendentals=0,
+        ),
+        name="backward_stage",
+    )(slots, top, *saved, *weights)
 
 
 def combine_kernel(blocks, capacity, cuts, count, place_ref, slots_ref, *refs):
@@ -540,9 +643,6 @@
     width = rights[0].shape[1]
     cuts = halves_of(width)
     half = blocks // 2 * rows
-
-    def rows_spec(size, columns):
-        return pl.BlockSpec((size, columns), lambda i, *_: (i, 0))
 
     out_specs = [
         pl.BlockSpec((half, high - low), lambda i, place: (i ^ place[2], 0))
@@ -633,7 +733,6 @@
 
     slots = Slots()
     place = jnp.stack([expert, me_seq & 1, me_seq >> 1]).astype(jnp.int32)
-    tokens = [Flow(gather_seq(tokens_in[micro])) for micro in micros]
 
     piece = w_kv_down.shape[0]
     kv_columns = w_kv_down.shape[1]
@@ -665,24 +764,32 @@
     for_heads = jnp.broadcast_to(
         for_heads[:, None], (seqs, line, piece, query_width + out_width)
     ).reshape(devices, piece, query_width + out_width)
-    for_heads = lax.all_to_all(for_heads, BOTH, 0, 0, tiled=True)
-    up_weight = lax.all_to_all(
-        jnp.broadcast_to(w_kv_up[None], (line,) + w_kv_up.shape), "fsdp", 0, 0, tiled=True
+    ready, for_heads = lax.optimization_barrier((tokens_in, for_heads))
+    tokens = [Flow(gather_seq(ready[micro])) for micro in micros]
+    for_heads = Flow(exchange(for_heads, BOTH))
+    up_weight = Flow(
+        exchange(jnp.broadcast_to(w_kv_up[None], (line,) + w_kv_up.shape), "fsdp")
     )
     hidden = w_shared_gate.shape[1] // devices
-    for_shared = jnp.concatenate(
-        [
-            w_shared_gate.reshape(piece, devices, hidden).transpose(1, 0, 2),
-            w_shared_up.reshape(piece, devices, hidden).transpose(1, 0, 2),
-            w_shared_down.reshape(devices, hidden, piece).transpose(0, 2, 1),
-        ],
-        axis=2,
-    )
+
+    def pack_shared(gate, up, down):
+        return jnp.concatenate(
+            [
+                gate.reshape(piece, devices, hidden).transpose(1, 0, 2),
+                up.reshape(piece, devices, hidden).transpose(1, 0, 2),
+                down.reshape(devices, hidden, piece).transpose(0, 2, 1),
+            ],
+            axis=2,
+        )
+
+    for_shared = slots.run(tokens, pack_shared, w_shared_gate, w_shared_up, w_shared_down)
     for_shared = Flow(exchange(for_shared, BOTH))
+    slots.run([*tokens, for_heads, up_weight])
+    tops = [lax.all_gather(slots.tie(cotangent[0]), BOTH, axis=0, tiled=True), None]
     slots.finish(tokens[0], tokens[1])
     slots.finish(tokens[1])
-    small, for_heads, up_weight = slots.run([], lambda *given: given, small, for_heads, up_weight)
-    tops = [lax.all_gather(slots.tie(cotangent[0]), BOTH, axis=0, tiled=True), None]
+    (small,) = slots.run([], lambda *given: given, small)
+    for_heads, up_weight = for_heads.value, up_weight.value
     for_heads = for_heads.reshape(width, query_width + out_width)
     query_weight = for_heads[:, :query_width]
     out_weight = for_heads[:, query_width:]
@@ -747,12 +854,14 @@
     summed_two = Flow(scatter_seq(attended[1][1], rows))
     slots.finish(summed, summed_two)
     residuals[0] = home_forward(0, summed.value)
-    normed_alls[0] = lax.all_gather(residuals[0][3], BOTH, axis=0, tiled=True)
+    first, tops[0] = lax.optimization_barrier((residuals[0][3], tops[0]))
+    normed_alls[0] = lax.all_gather(first, BOTH, axis=0, tiled=True)
     slots.finish(summed_two)
     residuals[1] = home_forward(1, summed_two.value)
     normed_alls[1] = lax.all_gather(residuals[1][3], BOTH, axis=0, tiled=True)
-    later, _ = lax.optimization_barrier((cotangent[1], residuals[1][3]))
-    tops[1] = lax.all_gather(later, BOTH, axis=0, tiled=True)
+    top_flow = Flow(gather_all(slots.tie(cotangent[1]), place))
+    for _ in range(line):
+        slots.run([top_flow])
 
     lanes = -(-(hidden + experts) // 128) * 128
 
@@ -771,7 +880,8 @@
     gate_weight = w_expert_gate[0]
     up_expert = w_expert_up[0]
     down_expert = w_expert_down[0]
-    hidden_weights = (wide_weight, shared_down, gate_weight, up_expert, down_expert.T)
+    forward_weights = (wide_weight, gate_weight, up_expert)
+    backward_weights = (shared_down, down_expert.T)
     transposed = (gate_weight.T, up_expert.T, shared_in.T, shared_down.T)
 
     def slots_of(micro):
@@ -779,31 +889,34 @@
         rank = jnp.cumsum(hit.astype(jnp.int32), axis=1) - 1
         return jnp.where(hit, rank, -1)[:, None, :]
 
-    def hidden_of(seats, tokens, top):
-        return hidden_stage(
-            place, seats, tokens, top, hidden_weights, capacity, experts, hidden
-        )
-
-    def grads_to_tokens(seats, made):
+    def forward_of(seats, tokens):
+        return forward_stage(
+            place, seats, tokens, forward_weights, capacity, experts, hidden, lanes
+        )
+
+    def backward_of(seats, top, made):
+        return backward_stage(
+            seats, top, (made[2], made[3], made[4], made[6], made[7]), backward_weights, capacity
+        )
+
+    def grads_to_tokens(seats, back):
         return combine_stage(
-            place, seats, made[3:5], transposed[:2], made[6], transposed[2], capacity
+            place, seats, back[1:3], transposed[:2], back[3], transposed[2], capacity
         )
 
     def outputs_to_tokens(seats, made):
         return combine_stage(
-            place, seats, made[2:3], (down_expert,), made[5], transposed[3], capacity
-        )
-
-    def routed_grads(made):
-        taken, taken_top, hidden_gated, pre_grad, up_grad, _, _, _ = made
-        return (
-            left_product(taken, pre_grad),
-            left_product(taken, up_grad),
-            left_product(hidden_gated, taken_top),
-        )
-
-    def shared_grads_of(tokens, top, made):
-        return left_product(tokens, made[6]), left_product(top, made[5])
+            place, seats, made[1:2], (down_expert,), made[5], transposed[3], capacity
+        )
+
+    def routed_pairs(made, back):
+        return (made[0], back[1]), (made[0], back[2]), (made[1], back[0])
+
+    def routed_grads(*pairs):
+        return tuple(left_product(*pair) for pair in pairs)
+
+    def shared_grads_of(tokens, top, made, back):
+        return left_product(tokens, back[3]), left_product(top, made[5])
 
     def added(function):
         def call(before, *values):
@@ -812,7 +925,7 @@
         return call
 
     def gate_grads_home(made):
-        return Flow(exchange(made[-1].reshape(devices, rows), BOTH))
+        return Flow(exchange(made.reshape(devices, rows), BOTH))
 
     def home_backward(micro, grad_two, gate_grad):
         _, unit_two, factor_two, normed_two = residuals[micro]
@@ -837,16 +950,25 @@
         grad_attended = to_relative(product(grad_attn_out, out_weight).astype(BF16))
         return attend_back_stage(factor, heads, projected[2] + marks, grad_attended)
 
-    def projections_backward(grad_query, grad_turned, grad_key_value, grad_rope):
+    def latents_backward(grad_key_value, grad_rope):
+        grad_rope = jnp.sum(grad_rope[:, : heads * ROPE].reshape(length, heads, ROPE), axis=1)
+        grad_key_value = grad_key_value.transpose(1, 0, 2).reshape(length, -1)
+        grad_latent_part = right_product(grad_key_value, up_weight)
+        part = jnp.concatenate([grad_latent_part, grad_rope], axis=1).astype(BF16)
+        return part, grad_key_value
+
+    def queries_backward(grad_query, grad_turned):
         grad_turned = grad_turned[:, : heads * ROPE].reshape(length, heads, ROPE)
         grad_turned = rotate(grad_turned, -angles[:, None, :]).reshape(length, -1)
         grad_query_raw = jnp.concatenate([grad_query, grad_turned.astype(BF16)], axis=1)
-        grad_rope = jnp.sum(grad_rope[:, : heads * ROPE].reshape(length, heads, ROPE), axis=1)
-        grad_key_value = grad_key_value.transpose(1, 0, 2).reshape(length, -1)
-        grad_one_part = right_product(grad_query_raw, query_weight)
-        grad_latent_part = right_product(grad_key_value, up_weight)
-        back = jnp.concatenate([grad_one_part, grad_latent_part, grad_rope], axis=1)
-        return back.astype(BF16), grad_query_raw, grad_key_value
+        one_part = right_product(to_absolute(grad_query_raw), query_weight)
+        return one_part.astype(BF16), grad_query_raw
+
+    def projections_backward(grad_query, grad_turned, grad_key_value, grad_rope):
+        return (
+            *latents_backward(grad_key_value, grad_rope),
+            *queries_backward(grad_query, grad_turned),
+        )
 
     def head_grads(projected, attended, grad_attn_out, grad_query_raw, grad_key_value):
         return (
@@ -857,16 +979,16 @@
 
     def latent_backward(back, projected):
         unit_latent, factor_latent = projected[3:]
-        grad_latent_norm = back[:, width : width + KVR].astype(F32)
+        grad_latent_norm = back[:, :KVR].astype(F32)
         grad_compressed = norm_back(grad_latent_norm * gain_latent, unit_latent, factor_latent)
         grad_latent = jnp.concatenate(
-            [grad_compressed, rotate(back[:, width + KVR :].astype(F32), -own_angles)], axis=-1
+            [grad_compressed, rotate(back[:, KVR:].astype(F32), -own_angles)], axis=-1
         ).astype(BF16)
         return grad_latent, jnp.sum(grad_latent_norm * unit_latent, axis=0)
 
     def input_backward(micro, back, grad_latent, grad_residual):
         unit_one, factor_one = normed(tokens_in[micro].astype(F32))
-        grad_one = back[:, :width].astype(F32) + right_product(grad_latent, down_weight)
+        grad_one = back.astype(F32) + right_product(grad_latent, down_weight)
         return (
             grad_residual + norm_back(grad_one * gain_one, unit_one, factor_one),
             jnp.sum(grad_one * unit_one, axis=0),
@@ -896,91 +1018,121 @@
     homes = [None, None]
     attn_out = [None, None]
     backs = [None, None]
-    back_sums = [None, None]
-    latents = [None, None]
-    latent_flows = [None, None]
-    made[0] = slots.run([], hidden_of, seats[0], normed_alls[0], tops[0])
-    gate_grad[0] = gate_grads_home(made[0])
-    sides = slots.run([gate_grad[0]], grads_to_tokens, seats[0], made[0])
+    back = [None, None]
+    finals = [None, None]
+
+    def shared_home(shared_grads):
+        shared_grads = shared_grads.astype(F32)
+        return (
+            shared_grads[:, :, :hidden].transpose(1, 0, 2).reshape(piece, -1),
+            shared_grads[:, :, hidden : 2 * hidden].transpose(1, 0, 2).reshape(piece, -1),
+            shared_grads[:, :, 2 * hidden :].transpose(0, 2, 1).reshape(-1, piece),
+        )
+
+    made[0] = slots.run([], forward_of, seats[0], normed_alls[0])
+    back[0] = slots.run([top_flow], backward_of, seats[0], tops[0], made[0])
+    gate_grad[0] = gate_grads_home(back[0][4])
+    sides = slots.run([top_flow, gate_grad[0]], grads_to_tokens, seats[0], back[0])
     grads[0] = Flow(reduce_all(*sides, rows))
+    tops[1] = slots.finish(top_flow)
     sides = slots.run([grads[0]], outputs_to_tokens, seats[0], made[0])
     sums[0] = Flow(reduce_all(*sides, rows))
-    routed = slots.run([grads[0]], routed_grads, made[0])
-    shared = slots.run([grads[0], sums[0]], shared_grads_of, normed_alls[0], tops[0], made[0])
-    slots.run([grads[0]])
-    slots.run([grads[0]])
-    made[1] = slots.run([grads[0], sums[0]], hidden_of, seats[1], normed_alls[1], tops[1])
+    routed, shared = slots.run(
+        [grads[0], sums[0]],
+        lambda pairs, *given: (routed_grads(*pairs), shared_grads_of(*given)),
+        routed_pairs(made[0], back[0]),
+        normed_alls[0],
+        tops[0],
+        made[0],
+        back[0],
+    )
+    made[1] = slots.run([grads[0]], forward_of, seats[1], normed_alls[1])
+    back[1] = slots.run([], backward_of, seats[1], tops[1], made[1])
+    gate_grad[1] = gate_grads_home(back[1][4])
+    sides = slots.run(
+        [grads[0], sums[0], gate_grad[1]], grads_to_tokens, seats[1], back[1]
+    )
+    grads[1] = Flow(reduce_all(*sides, rows))
     slots.finish(grads[0])
     homes[0], attn_out[0] = home_and_out(0)
-    gate_grad[1] = gate_grads_home(made[1])
-    sides = slots.run([gate_grad[1], sums[0]], grads_to_tokens, seats[1], made[1])
-    grads[1] = Flow(reduce_all(*sides, rows))
     sides = slots.run([grads[1], sums[0]], outputs_to_tokens, seats[1], made[1])
     sums[1] = Flow(reduce_all(*sides, rows))
-    backs[0] = slots.run([grads[1]], attention_back, attn_out[0], projected[0], marks[0])
-    back_sums[0] = Flow(scatter_seq(backs[0][0], rows))
-    head_sums = slots.run(
-        [grads[1], back_sums[0]],
-        head_grads,
-        projected[0],
-        attended[0][0],
-        attn_out[0],
-        *backs[0][1:],
-    )
-    taken, taken_top, hidden_gated, pre_grad, up_grad, _, _, _ = made[1]
-    parts = []
-    for pair in ((taken, pre_grad), (taken, up_grad), (hidden_gated, taken_top)):
-        parts.append(
-            slots.run(
-                [grads[1], back_sums[0], sums[0]],
-                lambda old, left, right: old + left_product(left, right),
-                routed[len(parts)],
-                *pair,
-            )
-        )
-    slots.finish(grads[1], back_sums[0])
-    homes[1], attn_out[1] = home_and_out(1)
-    slots.finish(back_sums[0])
-    latents[0] = latent_backward(back_sums[0].value, projected[0])
-    latent_flows[0] = Flow(gather_seq(latents[0][0]))
-    slots.run([sums[1], sums[0], latent_flows[0]])
+    parts = slots.run(
+        [grads[1], sums[0]], added(routed_grads), routed, *routed_pairs(made[1], back[1])
+    )
     shared = slots.run(
-        [sums[1], latent_flows[0]],
+        [grads[1], sums[1]],
         added(shared_grads_of),
         shared,
         normed_alls[1],
         tops[1],
         made[1],
+        back[1],
     )
     shared = jnp.concatenate(
         [shared[0][:, :hidden], shared[0][:, lanes : lanes + hidden], shared[1][:, :hidden]],
         axis=1,
     )
     shared = Flow(exchange(shared.astype(BF16).reshape(devices, piece, 3 * hidden), BOTH))
-    backs[1] = slots.run(
-        [sums[1], latent_flows[0], shared], attention_back, attn_out[1], projected[1], marks[1]
-    )
-    back_sums[1] = Flow(scatter_seq(backs[1][0], rows))
+    parted, grad_key_value, one_part, grad_query_raw = slots.run(
+        [grads[1], sums[1]],
+        lambda *given: projections_backward(*attend_backward(*given)),
+        attn_out[0],
+        projected[0],
+        marks[0],
+    )
+    slots.finish(grads[1])
+    homes[1], attn_out[1] = home_and_out(1)
+    whole_part, _ = lax.optimization_barrier(
+        (jnp.concatenate([one_part, to_absolute(parted)], axis=1), homes[1][0])
+    )
+    whole_part = lax.psum_scatter(whole_part, "seq", scatter_dimension=0, tiled=True)
     head_sums = slots.run(
-        [back_sums[1], sums[1], sums[0]],
+        [],
+        head_grads,
+        projected[0],
+        attended[0][0],
+        attn_out[0],
+        grad_query_raw,
+        grad_key_value,
+    )
+    scored = slots.run([sums[1]], attend_backward, attn_out[1], projected[1], marks[1])
+    parted, grad_key_value = slots.run([shared], latents_backward, *scored[2:])
+    latent_sums = Flow(scatter_seq(parted, rows))
+    one_part, grad_query_raw = slots.run([latent_sums], queries_backward, *scored[:2])
+    one_part = lax.psum_scatter(one_part, "seq", scatter_dimension=0, tiled=True)
+    head_sums = slots.run(
+        [latent_sums, sums[1]],
         added(head_grads),
         head_sums,
         projected[1],
         attended[1][0],
         attn_out[1],
-        *backs[1][1:],
+        grad_query_raw,
+        grad_key_value,
     )
     grad_heads = jnp.concatenate(head_sums[:2], axis=1).astype(BF16)
     grad_heads = Flow(exchange(grad_heads.reshape(devices, piece, -1), BOTH))
-    grad_up = Flow(exchange(line_blocks(head_sums[2]), "fsdp"))
-    slots.run([back_sums[1], sums[1], sums[0], grad_up])
-    slots.finish(back_sums[1], sums[1], sums[0])
-    latents[1] = latent_backward(back_sums[1].value, projected[1])
-    latent_flows[1] = Flow(gather_seq(latents[1][0]))
-    finals = [
-        input_backward(micro, back_sums[micro].value, latents[micro][0], homes[micro][0])
-        for micro in micros
-    ]
+    grad_up = Flow(exchange_line(line_blocks(head_sums[2])))
+    latents = [latent_backward(whole_part[:, width:], projected[0]), None]
+    finals[0] = slots.run(
+        [latent_sums, grad_up],
+        functools.partial(input_backward, 0),
+        whole_part[:, :width],
+        latents[0][0],
+        homes[0][0],
+    )
+    slots.finish(latent_sums)
+    latents[1] = latent_backward(latent_sums.value, projected[1])
+    latent_flow = Flow(gather_seq(jnp.concatenate([latent[0] for latent in latents], axis=1)))
+    shared_final = slots.run([latent_flow], shared_home, shared.value)
+    finals[1] = slots.run(
+        [latent_flow, grad_heads],
+        functools.partial(input_backward, 1),
+        one_part,
+        latents[1][0],
+        homes[1][0],
+    )
     tiny = jnp.concatenate(
         [
             sum(home[1] for home in homes).reshape(devices, -1),
@@ -991,24 +1143,23 @@
         axis=1,
     )
     tiny = Flow(exchange(tiny, BOTH))
-    slots.run([latent_flows[1], sums[1], sums[0]])
-    slots.run([latent_flows[1], sums[1], sums[0], tiny])
-    slots.finish(latent_flows[1], grad_heads)
-    for flow in (sums[0], sums[1], latent_flows[0], tiny, grad_heads, shared, grad_up):
+    slots.finish(latent_flow)
+    grad_kv_down = sum(
+        down_grads(
+            projected[micro][0],
+            latent_flow.value[:, micro * kv_columns : (micro + 1) * kv_columns],
+        )
+        for micro in micros
+    )
+    grad_kv_down = Flow(exchange_line(line_blocks(grad_kv_down)))
+    slots.run([grad_kv_down, tiny, grad_heads, sums[0], sums[1]])
+    for flow in (sums[0], sums[1]):
         slots.finish(flow)
     outputs = [
         (residuals[micro][0] + sums[micro].value).astype(BF16) for micro in micros
     ]
-    grad_kv_down = sum(
-        down_grads(projected[micro][0], latent_flows[micro].value) for micro in micros
-    )
-    grad_kv_down = lax.all_to_all(line_blocks(grad_kv_down), "fsdp", 0, 0, tiled=True)
-    grad_kv_down = jnp.sum(grad_kv_down.astype(F32), axis=0)
-    grad_kv_up = jnp.sum(grad_up.value.astype(F32), axis=0).T
-    shared_grads = shared.value.astype(F32)
-    grad_shared_gate = shared_grads[:, :, :hidden].transpose(1, 0, 2).reshape(piece, -1)
-    grad_shared_up = shared_grads[:, :, hidden : 2 * hidden].transpose(1, 0, 2).reshape(piece, -1)
-    grad_shared_down = shared_grads[:, :, 2 * hidden :].transpose(0, 2, 1).reshape(-1, piece)
+    grad_kv_down = grad_kv_down.value
+    grad_kv_up = grad_up.value.T
     grad_heads = grad_heads.value.reshape(seqs, line, piece, -1)
     grad_heads = jnp.sum(grad_heads.astype(F32), axis=1)
     grad_query_weight = jnp.concatenate(
@@ -1033,9 +1184,7 @@
         grad_kv_up,
         grad_out_weight,
         tiny[:first].reshape(piece, experts),
-        grad_shared_gate,
-        grad_shared_up,
-        grad_shared_down,
+        *shared_final,
         parts[0][None],
         parts[1][None],
         parts[2][None],

time: 1400 us -> 1290 us (0.921)
  waiting for transfers between devices: 366 us -> 255 us
  Pallas kernels: 248 us -> 288 us
  local copies, waits for them, and re-layouts: 217 us -> 179 us
  other arithmetic: 188 us -> 223 us
  starting transfers between devices: 167 us -> 133 us
    all_gather x2 -> x1, waiting for transfers between devices: 90.7 us -> 0.01 us  [per_device(): normed_alls[0] = lax.all_gather(first, BOTH, axis=0, tiled=True)]
    ppermute x64, waiting for transfers between devices: 202 us -> 128 us  [swap(): return lax.ppermute(value, 'seq', [(i, i ^ 1 << bit) for i in range(count)])]
    ppermute x24, waiting for transfers between devices: 26.6 us -> 86.3 us  [the longest x3 68.1 us: line_gather(): lax.ppermute(down, 'fsdp', [(i, i - 1) for i in range(1, count - step + 1)])]
    pallas_call x2 -> x5, Pallas kernels: 93.8 us -> 133 us  [the longest x2 74.5 us: forward_stage(): pl.pallas_call(functools.partial(forward_kernel, blocks, capacity, expert...]
    ppermute x24, starting transfers between devices: 60.8 us -> 37.5 us  [the longest x18 25.3 us: exchange_line(): lax.ppermute(piece(place + turn), 'fsdp', [(i, (i + turn) % count) for i...]
    add x0 -> x11, other arithmetic: none -> 22.3 us  [the longest x8 19.9 us: total_of(): return sum((term.astype(F32) for term in terms[1:]), terms[0].astype(F32))]
    another operation x9 -> x16, other arithmetic: 4.9 us -> 26.3 us  [the longest x4 11.7 us: gather_all(): far = [jnp.stack(pair) for pair in zip(far, crossed)]]
    convert_element_type x56 -> x37, other arithmetic: 100 us -> 80.2 us  [the longest x26 60 us: fold(): sent.append(swap(send.astype(BF16), order[step]))]
  transfers between devices with their start and end apart: 105 -> 104, of which waited for: 42 -> 32; matrix products, arithmetic and copies ran while one was open for 38% -> 43% of each run, Pallas kernels for 18% -> 22%
where the time goes in v3:
time: 1290 us; the launch traced here: 1280 us
  Pallas kernels  288 us (22%)
  waiting for transfers between devices  255 us (20%)
  other arithmetic  223 us (17%)
  matrix products  187 us (14%)
  local copies, waits for them, and re-layouts  179 us (14%)
  starting transfers between devices  133 us (10%)
  between operations  17.7 us (1%)
    ppermute x64, waiting for transfers between devices, swap(): return lax.ppermute(value, 'seq', [(i, i ^ 1 << bit) for i in range(count)])  128 us
    dot_general x20, matrix products, left_product(): lax.dot_general(left, right, (((0,), (0,)), ((), ())), preferred_element_...  127 us
    pallas_call x4, Pallas kernels, combine_stage(): pl.pallas_call(functools.partial(combine_kernel, blocks, capacity, cuts,...  102 us
    pallas_call x2, Pallas kernels, forward_stage(): pl.pallas_call(functools.partial(forward_kernel, blocks, capacity, expert...  74.5 us
    ppermute x3, waiting for transfers between devices, line_gather(): lax.ppermute(down, 'fsdp', [(i, i - 1) for i in range(1, count - step + 1)])  68.1 us
    convert_element_type x26, other arithmetic, fold(): sent.append(swap(send.astype(BF16), order[step]))  60 us
    ppermute x64, starting transfers between devices, swap(): return lax.ppermute(value, 'seq', [(i, i ^ 1 << bit) for i in range(count)])  59.2 us
    pallas_call x2, Pallas kernels, backward_stage(): pl.pallas_call(functools.partial(backward_kernel, blocks, capacity), grid...  46.8 us
  transfers between devices with their start and end apart: 104, of which 32 were waited for; matrix products, arithmetic and copies ran while one was open for 43% of the time, Pallas kernels for 22%

profile of v3, /device:TPU:0, one launch (start us, length us, event | category | flops | bytes accessed | tf_op | source)
XLA Modules:
  0.0 1282.3 jit_solution(17121733736817268582)
XLA Ops:
  49.8 13.9 %collective-permute-done.3 = bf16[128,1024]{1,0:T(8,128)(2,1)} collective-permute-done((bf16[128,1024]{1,0:T(8,128)(2,1)}, bf16[128,1024]{1,0:T(8,128)(2,1)}, u32[]{:S(2)}, u32[]{:S(2)}) %collective-permute-start.3) | collective-permute-done | bytes 262176 | tf_op jit(solution)/shard_map/ppermute | solution.py:64
  95.1 12.8 %collective-permute-done.6 = bf16[2,128,1024]{2,1,0:T(8,128)(2,1)S(1)} collective-permute-done((bf16[2,128,1024]{2,1,0:T(8,128)(2,1)S(1)}, bf16[2,128,1024]{2,1,0:T(8,128)(2,1)S(1)}, u32[]{:S(2)}, u32[]{:S(2)}) %collective-permute-start.6) | collective-permute-done | bytes 524320 | tf_op jit(solution)/shard_map/ppermute | solution.py:64
  236.2 12.6 collective-permute-done.14
  309.6 36.0 %collective-permute-done.23 = bf16[128,2048]{1,0:T(8,128)(2,1)} collective-permute-done((bf16[128,2048]{1,0:T(8,128)(2,1)}, bf16[128,2048]{1,0:T(8,128)(2,1)}, u32[]{:S(2)}, u32[]{:S(2)}) %collective-permute-start.23) | collective-permute-done | bytes 524320 | tf_op jit(solution)/shard_map/ppermute | solution.py:192
  352.5 32.1 %collective-permute-done.25 = bf16[128,2048]{1,0:T(8,128)(2,1)} collective-permute-done((bf16[128,2048]{1,0:T(8,128)(2,1)}, bf16[128,2048]{1,0:T(8,128)(2,1)}, u32[]{:S(2)}, u32[]{:S(2)}) %collective-permute-start.25) | collective-permute-done | bytes 524320 | tf_op jit(solution)/shard_map/ppermute | solution.py:192
  431.8 37.2 %forward_stage.2 = (bf16[2048,2048]{1,0:T(8,128)(2,1)}, bf16[2048,704]{1,0:T(8,128)(2,1)}, bf16[2048,704]{1,0:T(8,128)(2,1)}, bf16[2048,704]{1,0:T(8,128)(2,1)},...) custom-call(s32[3]{0:T(128)} %pad_add_fusion.place_ref, ...), custom_call_target="tpu_custom_call" | custom-call | flops 16106127360 | bytes 25165824 | tf_op jit(solution)/shard_map/forward_stage/pallas_call | solution.py:548
  469.0 23.5 %backward_stage.2 = (bf16[2048,2048]{1,0:T(8,128)(2,1)}, bf16[2048,704]{1,0:T(8,128)(2,1)}, bf16[2048,704]{1,0:T(8,128)(2,1)}, bf16[4096,256]{1,0:T(8,128)(2,1)}, f32[32,1,128]{2,1,0:T(1,128)}) custom-call(s32[32,1,128]{2,1,0:T(1,128)} %copy_select_fusion.1.slots_ref, bf16[4096,2048]{1,0:T(8,128)(2,1)} %all-gather.9.cloned.1.call-done.top_ref, ...), custom_call_target="tpu_custom_call" | custom-call | flops 8053063680 | bytes 33554432 | tf_op jit(solution)/shard_map/backward_stage/pallas_call | solution.py:582
  495.7 29.2 %combine_stage.4 = (bf16[2048,1024]{1,0:T(8,128)(2,1)}, bf16[2048,1024]{1,0:T(8,128)(2,1)}, bf16[2048,1024]{1,0:T(8,128)(2,1)}, bf16[2048,1024]{1,0:T(8,128)(2,1)}) custom-call(s32[3]{0:T(128)} %pad_add_fusion.place_ref, s32[32,1,128]{2,1,0:T(1,128)} %copy_select_fusion.1.slots_ref, bf16[2048,704]{1,0:T(8,128)(2,1)} %get-tuple-element.582.refs_0_, ...), custom_call_target="tpu_custom_call" | custom-call | flops 17179869184 | bytes 25165824 | tf_op jit(solution)/shard_map/combine_stage/pallas_call | solution.py:660
  548.0 12.0 assemble.1.top_ref
  560.0 21.4 %combine_stage.5 = (bf16[2048,1024]{1,0:T(8,128)(2,1)}, bf16[2048,1024]{1,0:T(8,128)(2,1)}, bf16[2048,1024]{1,0:T(8,128)(2,1)}, bf16[2048,1024]{1,0:T(8,128)(2,1)}) custom-call(s32[3]{0:T(128)} %pad_add_fusion.place_ref, s32[32,1,128]{2,1,0:T(1,128)} %copy_select_fusion.1.slots_ref, bf16[2048,704]{1,0:T(8,128)(2,1)} %get-tuple-element.585.refs_0_, ...), custom_call_target="tpu_custom_call" | custom-call | flops 9126805504 | bytes 25165824 | tf_op jit(solution)/shard_map/combine_stage/pallas_call | solution.py:660
  607.8 11.5 fusion.237
  661.8 37.3 %forward_stage.3 = (bf16[2048,2048]{1,0:T(8,128)(2,1)}, bf16[2048,704]{1,0:T(8,128)(2,1)}, bf16[2048,704]{1,0:T(8,128)(2,1)}, bf16[2048,704]{1,0:T(8,128)(2,1)},...) custom-call(s32[3]{0:T(128)} %pad_add_fusion.place_ref, ...), custom_call_target="tpu_custom_call" | custom-call | flops 16106127360 | bytes 25165824 | tf_op jit(solution)/shard_map/forward_stage/pallas_call | solution.py:548
  709.9 23.2 %backward_stage.3 = (bf16[2048,2048]{1,0:T(8,128)(2,1)}, bf16[2048,704]{1,0:T(8,128)(2,1)}, bf16[2048,704]{1,0:T(8,128)(2,1)}, bf16[4096,256]{1,0:T(8,128)(2,1)}, f32[32,1,128]{2,1,0:T(1,128)}) custom-call(s32[32,1,128]{2,1,0:T(1,128)} %copy_select_fusion.slots_ref, bf16[4096,2048]{1,0:T(8,128)(2,1)} %assemble.1.top_ref, ...), custom_call_target="tpu_custom_call" | custom-call | flops 8053063680 | bytes 33554432 | tf_op jit(solution)/shard_map/backward_stage/pallas_call | solution.py:582
  737.1 29.7 %combine_stage.6 = (bf16[2048,1024]{1,0:T(8,128)(2,1)}, bf16[2048,1024]{1,0:T(8,128)(2,1)}, bf16[2048,1024]{1,0:T(8,128)(2,1)}, bf16[2048,1024]{1,0:T(8,128)(2,1)}) custom-call(s32[3]{0:T(128)} %pad_add_fusion.place_ref, s32[32,1,128]{2,1,0:T(1,128)} %copy_select_fusion.slots_ref, bf16[2048,704]{1,0:T(8,128)(2,1)} %get-tuple-element.676.refs_0_, ...), custom_call_target="tpu_custom_call" | custom-call | flops 17179869184 | bytes 25165824 | tf_op jit(solution)/shard_map/combine_stage/pallas_call | solution.py:660
  782.7 21.2 %combine_stage.7 = (bf16[2048,1024]{1,0:T(8,128)(2,1)}, bf16[2048,1024]{1,0:T(8,128)(2,1)}, bf16[2048,1024]{1,0:T(8,128)(2,1)}, bf16[2048,1024]{1,0:T(8,128)(2,1)}) custom-call(s32[3]{0:T(128)} %pad_add_fusion.place_ref, s32[32,1,128]{2,1,0:T(1,128)} %copy_select_fusion.slots_ref, bf16[2048,704]{1,0:T(8,128)(2,1)} %get-tuple-element.681.refs_0_, ...), custom_call_target="tpu_custom_call" | custom-call | flops 9126805504 | bytes 25165824 | tf_op jit(solution)/shard_map/combine_stage/pallas_call | solution.py:660
  824.2 11.2 convolution_add_fusion.2
  835.5 12.1 convolution_add_fusion.1
  887.0 13.8 %convolution_add_fusion.4 = bf16[2048,256]{1,0:T(8,128)(2,1)} fusion(f32[2048,256]{1,0:T(8,128)} %fusion.238, bf16[4096,2048]{1,0:T(8,128)(2,1)} %all-gather.13.cloned.1.call-done.tokens_ref, bf16[4096,256]{1,0:T(8,128)(2,1)} %get-tuple-element.696.refs_4_), kind=kOutput, calls=%fused_computation.75 | convolution fusion | flops 4296015872 | bytes 22020096 | tf_op jit(solution)/shard_map/dot_general | solution.py:30
  908.8 14.4 %collective-permute-done.58 = bf16[4,128,1024]{2,1,0:T(8,128)(2,1)S(1)} collective-permute-done((bf16[4,128,1024]{2,1,0:T(8,128)(2,1)S(1)}, bf16[4,128,1024]{2,1,0:T(8,128)(2,1)S(1)}, u32[]{:S(2)}, u32[]{:S(2)}) %collective-permute-start.58) | collective-permute-done | bytes 1048608 | tf_op jit(solution)/shard_map/ppermute | solution.py:64
  951.8 15.9 %attend_back_stage.2 = (bf16[1024,256]{1,0:T(8,128)(2,1)}, f32[1024,128]{1,0:T(8,128)}, bf16[2,1024,256]{2,1,0:T(8,128)(2,1)}, f32[1024,128]{1,0:T(8,128)}) custom-call(bf16[1024,256]{1,0:T(8,128)(2,1)} %copy.506.qn_ref, bf16[1024,128]{1,0:T(8,128)(2,1)} %copy.445.qr_ref, bf16[1024,512]{1,0:T(8,128)(2,1)} %convolution_convert_fusion.7.kv_ref, ...), custom_call_target="tpu_custom_call" | custom-call | flops 4294967296 | bytes 4194304 | tf_op jit(solution)/shard_map/attend_back_stage/pallas_call | solution.py:502
  1039.5 15.1 %all-gather.17.cloned.1.call-done = bf16[1024,2048]{1,0:T(8,128)(2,1)} async-done(((bf16[128,2048]{1,0:T(8,128)(2,1)}), bf16[1024,2048]{1,0:T(8,128)(2,1)}) %all-gather.17.cloned.1.call-update) | async-done | bytes 4194320 | tf_op jit(solution)/shard_map/all_gather | solution.py:1010
  1063.6 16.5 %attend_back_stage.3 = (bf16[1024,256]{1,0:T(8,128)(2,1)}, f32[1024,128]{1,0:T(8,128)}, bf16[2,1024,256]{2,1,0:T(8,128)(2,1)}, f32[1024,128]{1,0:T(8,128)}) custom-call(bf16[1024,256]{1,0:T(8,128)(2,1)} %copy.507.qn_ref, bf16[1024,128]{1,0:T(8,128)(2,1)} %copy.453.qr_ref, bf16[1024,512]{1,0:T(8,128)(2,1)} %convolution_convert_fusion.6.kv_ref, ...), custom_call_target="tpu_custom_call" | custom-call | flops 4294967296 | bytes 4194304 | tf_op jit(solution)/shard_map/attend_back_stage/pallas_call | solution.py:502
  1140.9 11.4 collective-permute-done.73
  1218.9 14.7 %all-to-all-done.6 = bf16[32,64,640]{2,1,0:T(8,128)(2,1)} async-done(((bf16[32,64,640]{2,1,0:T(8,128)(2,1)}), bf16[32,64,640]{2,1,0:T(8,128)(2,1)}, u32[]{:S(2)}, u32[]{:S(2)}) %all-to-all-start.6) | async-done | bytes 2621472 | tf_op jit(solution)/shard_map/all_to_all | solution.py:165
  (1004 shorter events, 785.6 us)
Async XLA Ops:
  30.7 80.6 %all-to-all-start = ((bf16[32,64,640]{2,1,0:T(8,128)(2,1)}), bf16[32,64,640]{2,1,0:T(8,128)(2,1)}, u32[]{:S(2)}, u32[]{:S(2)}) async-start(bf16[32,64,640]{2,1,0:T(8,128)(2,1)} %bitcast.3), calls=%async_computation | async-start | bytes 5242880 | tf_op jit(solution)/shard_map/all_to_all | solution.py:165
  34.5 92.1 %all-gather.7.cloned.1.call-start = ((), (), s32[]{:S(2)}) async-start(), calls=%async_computation.10 | async-start | bytes 2703360 | tf_op jit(solution)/shard_map/all_gather | solution.py:750
  36.1 239.2 %all-gather.9.cloned.1.call-start = ((), (), s32[]{:S(2)}) async-start(), calls=%async_computation.11 | async-start | bytes 17301504 | tf_op jit(solution)/shard_map/all_gather | solution.py:788
  122.0 77.4 %all-to-all-start.2 = ((bf16[32,64,264]{2,1,0:T(8,128)(2,1)}), bf16[32,64,264]{2,1,0:T(8,128)(2,1)}, u32[]{:S(2)}, u32[]{:S(2)}) async-start(bf16[32,64,264]{2,1,0:T(8,128)(2,1)} %pad_maximum_fusion.13), calls=%async_computation.2 | async-start | bytes 3145728 | tf_op jit(solution)/shard_map/all_to_all | solution.py:165
  126.4 305.4 %all-gather.11.cloned.1.call-start = ((), (), s32[]{:S(2)}) async-start(), calls=%async_computation.12 | async-start | bytes 17301504 | tf_op jit(solution)/shard_map/all_gather | solution.py:858
  275.4 369.6 %all-gather.13.cloned.1.call-start = ((), (), s32[]{:S(2)}) async-start(), calls=%async_computation.13 | async-start | bytes 17301504 | tf_op jit(solution)/shard_map/all_gather | solution.py:861
  422.4 70.1 %collective-permute-start.32 = (bf16[512,1024]{1,0:T(8,128)(2,1)}, bf16[512,1024]{1,0:T(8,128)(2,1)}, u32[]{:S(2)}, u32[]{:S(2)}) collective-permute-start(bf16[512,1024]{1,0:T(8,128)(2,1)} %collective-permute-done.26), channel_id=1, source_target_pairs={{0,4},{4,0},{8,12},{12,8},{16,20},{20,16},{24,28},{28,24},{1,5},{5... | collective-permute-start | bytes 3145736 | tf_op jit(solution)/shard_map/ppermute | solution.py:64
  422.4 70.1 %collective-permute-start.33 = (bf16[512,1024]{1,0:T(8,128)(2,1)}, bf16[512,1024]{1,0:T(8,128)(2,1)}, u32[]{:S(2)}, u32[]{:S(2)}) collective-permute-start(bf16[512,1024]{1,0:T(8,128)(2,1)} %collective-permute-done.27), channel_id=1, source_target_pairs={{0,4},{4,0},{8,12},{12,8},{16,20},{20,16},{24,28},{28,24},{1,5},{5... | collective-permute-start | bytes 3145736 | tf_op jit(solution)/shard_map/ppermute | solution.py:64
  426.5 66.1 %collective-permute-start.31 = (bf16[2,512,1024]{2,1,0:T(8,128)(2,1)}, bf16[2,512,1024]{2,1,0:T(8,128)(2,1)}, u32[]{:S(2)}, u32[]{:S(2)}) collective-permute-start(bf16[2,512,1024]{2,1,0:T(8,128)(2,1)} %get-tuple-element.964), channel_id=1, source_target_pairs={{0,8},{4,12},{8,0},{12,4},{16,24},{20,28},{24,16},{28,20},{1,9},{5... | collective-permute-start | bytes 6291464 | tf_op jit(solution)/shard_map/ppermute | solution.py:64
  431.8 60.8 %collective-permute-start.30 = (bf16[2,512,1024]{2,1,0:T(8,128)(2,1)}, bf16[2,512,1024]{2,1,0:T(8,128)(2,1)}, u32[]{:S(2)}, u32[]{:S(2)}) collective-permute-start(bf16[2,512,1024]{2,1,0:T(8,128)(2,1)} %get-tuple-element.966), channel_id=1, source_target_pairs={{0,16},{4,20},{8,24},{12,28},{16,0},{20,4},{24,8},{28,12},{1,17},{... | collective-permute-start | bytes 6291464 | tf_op jit(solution)/shard_map/ppermute | solution.py:64
  524.9 56.5 %collective-permute-start.36 = (bf16[2048,1024]{1,0:T(8,128)(2,1)}, bf16[2048,1024]{1,0:T(8,128)(2,1)}, u32[]{:S(2)}, u32[]{:S(2)}) collective-permute-start(bf16[2048,1024]{1,0:T(8,128)(2,1)} %get-tuple-element.563), channel_id=1, source_target_pairs={{0,4},{4,0},{8,12},{12,8},{16,20},{20,16},{24,28},{28,24},{1,5},{5... | collective-permute-start | bytes 12582920 | tf_op jit(solution)/shard_map/ppermute | solution.py:64
  525.1 56.4 %collective-permute-start.37 = (bf16[2048,1024]{1,0:T(8,128)(2,1)}, bf16[2048,1024]{1,0:T(8,128)(2,1)}, u32[]{:S(2)}, u32[]{:S(2)}) collective-permute-start(bf16[2048,1024]{1,0:T(8,128)(2,1)} %get-tuple-element.564), channel_id=1, source_target_pairs={{0,4},{4,0},{8,12},{12,8},{16,20},{20,16},{24,28},{28,24},{1,5},{5... | collective-permute-start | bytes 12582920 | tf_op jit(solution)/shard_map/ppermute | solution.py:64
  584.9 57.4 %collective-permute-start.39 = (bf16[2,4,128,1024]{3,2,1,0:T(8,128)(2,1)S(1)}, bf16[2,4,128,1024]{3,2,1,0:T(8,128)(2,1)S(1)}, u32[]{:S(2)}, u32[]{:S(2)}) collective-permute-start(bf16[2,4,128,1024]{3,2,1,0:T(8,128)(2,1)S(1)} %bitcast.694), channel_id=1, source_target_pairs={{0,16},{4,20},{8,24},{12,28},{16,0},{20,4},{24,8},{28,12},{1,17},{... | collective-permute-start | bytes 6291464 | tf_op jit(solution)/shard_map/ppermute | solution.py:64
  655.3 111.6 %collective-permute-start.48 = (bf16[2,4,128,1024]{3,2,1,0:T(8,128)(2,1)}, bf16[2,4,128,1024]{3,2,1,0:T(8,128)(2,1)}, u32[]{:S(2)}, u32[]{:S(2)}) collective-permute-start(bf16[2,4,128,1024]{3,2,1,0:T(8,128)(2,1)} %bitcast.137), channel_id=1, source_target_pairs={{0,16},{4,20},{8,24},{12,28},{16,0},{20,4},{24,8},{28,12},{1,17},{... | collective-permute-start | bytes 6291464 | tf_op jit(solution)/shard_map/ppermute | solution.py:64
  660.8 106.0 %collective-permute-start.47 = (bf16[2,4,128,1024]{3,2,1,0:T(8,128)(2,1)}, bf16[2,4,128,1024]{3,2,1,0:T(8,128)(2,1)}, u32[]{:S(2)}, u32[]{:S(2)}) collective-permute-start(bf16[2,4,128,1024]{3,2,1,0:T(8,128)(2,1)} %fusion.7), channel_id=1, source_target_pairs={{0,8},{4,12},{8,0},{12,4},{16,24},{20,28},{24,16},{28,20},{1,9},{5... | collective-permute-start | bytes 6291464 | tf_op jit(solution)/shard_map/ppermute | solution.py:64
  705.4 61.4 %collective-permute-start.46 = (bf16[128,2048]{1,0:T(8,128)(2,1)}, bf16[128,2048]{1,0:T(8,128)(2,1)S(1)}, u32[]{:S(2)}, u32[]{:S(2)}) collective-permute-start(bf16[128,2048]{1,0:T(8,128)(2,1)} %get-tuple-element.967), channel_id=1, source_target_pairs={{0,3},{1,0},{2,1},{3,2},{4,7},{5,4},{6,5},{7,6},{8,11},{9,8},{10,9... | collective-permute-start | bytes 1572872 | tf_op jit(solution)/shard_map/ppermute | solution.py:177
  708.7 58.1 %collective-permute-start.44 = (bf16[128,2048]{1,0:T(8,128)(2,1)}, bf16[128,2048]{1,0:T(8,128)(2,1)}, u32[]{:S(2)}, u32[]{:S(2)}) collective-permute-start(bf16[128,2048]{1,0:T(8,128)(2,1)} %get-tuple-element.968), channel_id=1, source_target_pairs={{0,1},{1,2},{2,3},{3,0},{4,5},{5,6},{6,7},{7,4},{8,9},{9,10},{10,1... | collective-permute-start | bytes 1572872 | tf_op jit(solution)/shard_map/ppermute | solution.py:177
  708.7 58.1 %collective-permute-start.45 = (bf16[128,2048]{1,0:T(8,128)(2,1)}, bf16[128,2048]{1,0:T(8,128)(2,1)}, u32[]{:S(2)}, u32[]{:S(2)}) collective-permute-start(bf16[128,2048]{1,0:T(8,128)(2,1)} %get-tuple-element.969), channel_id=1, source_target_pairs={{0,2},{1,3},{2,0},{3,1},{4,6},{5,7},{6,4},{7,5},{8,10},{9,11},{10,... | collective-permute-start | bytes 1572872 | tf_op jit(solution)/shard_map/ppermute | solution.py:177
  737.0 205.7 %all-gather.15.cloned.1.call-start = ((), (), s32[]{:S(2)}) async-start(), calls=%async_computation.14 | async-start | bytes 4718592 | tf_op jit(solution)/shard_map/all_gather | solution.py:1010
  874.1 180.6 %all-gather.17.cloned.1.call-start = ((), (), s32[]{:S(2)}) async-start(), calls=%async_computation.15 | async-start | bytes 4718592 | tf_op jit(solution)/shard_map/all_gather | solution.py:1010
  991.5 142.7 %reduce-scatter.3.cloned.1.call-start = ((), (), s32[]{:S(2)}) async-start(), calls=%async_computation.16 | async-start | bytes 6193152 | tf_op jit(solution)/shard_map/reduce_scatter | solution.py:1089
  1008.4 78.0 %all-to-all-start.5 = ((bf16[32,64,264]{2,1,0:T(8,128)(2,1)}), bf16[32,64,264]{2,1,0:T(8,128)(2,1)}, u32[]{:S(2)}, u32[]{:S(2)}) async-start(bf16[32,64,264]{2,1,0:T(8,128)(2,1)} %pad_maximum_fusion.14), calls=%async_computation.5 | async-start | bytes 3145728 | tf_op jit(solution)/shard_map/all_to_all | solution.py:165
  1013.9 192.4 %reduce-scatter.5.cloned.1.call-start = ((), (), s32[]{:S(2)}) async-start(), calls=%async_computation.17 | async-start | bytes 4718592 | tf_op jit(solution)/shard_map/reduce_scatter | solution.py:1103
  1170.8 62.8 %all-to-all-start.6 = ((bf16[32,64,640]{2,1,0:T(8,128)(2,1)}), bf16[32,64,640]{2,1,0:T(8,128)(2,1)}, u32[]{:S(2)}, u32[]{:S(2)}) async-start(bf16[32,64,640]{2,1,0:T(8,128)(2,1)} %pad_maximum_fusion.6), calls=%async_computation.7 | async-start | bytes 5242880 | tf_op jit(solution)/shard_map/all_to_all | solution.py:165
  (286 other events, 4079.3 us)
Sparse Core Ops, SparseCore 0:
  38.8 76.5 all-gather.6
  118.4 154.2 all-gather.8
  276.2 129.8 all-gather.10
  409.6 132.5 all-gather.12
  874.2 52.1 all-gather.14
  991.6 62.9 all-gather.16
  1058.1 57.4 reduce-scatter.2
  1123.3 53.4 reduce-scatter.4

commit v4 on v3

--- a/solution.py
+++ b/solution.py
@@ -831,8 +831,9 @@
         segment = segments[micro].reshape(seqs, rows)[order].reshape(-1)
         return segment[:, None], segment[None, :], places[:, None], places[None, :]
 
-    def attend(projected, marks):
-        attended = attend_stage(factor, heads, projected[2] + marks)
+    def attend(micro, query):
+        inputs = (query,) + projected[micro][2][1:] + marks[micro]
+        attended = attend_stage(factor, heads, inputs)
         return attended, right_product(attended, out_weight).astype(BF16)
 
     def home_forward(micro, summed):
@@ -847,10 +848,10 @@
     residuals = [None, None]
     normed_alls = [None, None]
     projected[0] = slots.run([], projections, tokens[0].value)
-    attended[0] = slots.run([], attend, projected[0], marks[0])
+    attended[0] = slots.run([], functools.partial(attend, 0), projected[0][2][0])
     summed = Flow(scatter_seq(attended[0][1], rows))
     projected[1] = slots.run([summed, for_shared], projections, tokens[1].value)
-    attended[1] = slots.run([summed], attend, projected[1], marks[1])
+    attended[1] = slots.run([summed], functools.partial(attend, 1), projected[1][2][0])
     summed_two = Flow(scatter_seq(attended[1][1], rows))
     slots.finish(summed, summed_two)
     residuals[0] = home_forward(0, summed.value)
@@ -946,9 +947,10 @@
             jnp.sum(grad_two * unit_two, axis=0),
         )
 
-    def attend_backward(grad_attn_out, projected, marks):
+    def attend_backward(micro, grad_attn_out):
         grad_attended = to_relative(product(grad_attn_out, out_weight).astype(BF16))
-        return attend_back_stage(factor, heads, projected[2] + marks, grad_attended)
+        inputs = projected[micro][2] + marks[micro]
+        return attend_back_stage(factor, heads, inputs, grad_attended)
 
     def latents_backward(grad_key_value, grad_rope):
         grad_rope = jnp.sum(grad_rope[:, : heads * ROPE].reshape(length, heads, ROPE), axis=1)
@@ -1076,10 +1078,8 @@
     shared = Flow(exchange(shared.astype(BF16).reshape(devices, piece, 3 * hidden), BOTH))
     parted, grad_key_value, one_part, grad_query_raw = slots.run(
         [grads[1], sums[1]],
-        lambda *given: projections_backward(*attend_backward(*given)),
+        lambda given: projections_backward(*attend_backward(0, given)),
         attn_out[0],
-        projected[0],
-        marks[0],
     )
     slots.finish(grads[1])
     homes[1], attn_out[1] = home_and_out(1)
@@ -1096,14 +1096,20 @@
         grad_query_raw,
         grad_key_value,
     )
-    scored = slots.run([sums[1]], attend_backward, attn_out[1], projected[1], marks[1])
+    scored = slots.run([sums[1]], functools.partial(attend_backward, 1), attn_out[1])
     parted, grad_key_value = slots.run([shared], latents_backward, *scored[2:])
     latent_sums = Flow(scatter_seq(parted, rows))
     one_part, grad_query_raw = slots.run([latent_sums], queries_backward, *scored[:2])
     one_part = lax.psum_scatter(one_part, "seq", scatter_dimension=0, tiled=True)
-    head_sums = slots.run(
+
+    def all_head_grads(before, *given):
+        query, out, up = added(head_grads)(before, *given)
+        packed = jnp.concatenate([query, out], axis=1).astype(BF16)
+        return packed.reshape(devices, piece, -1), line_blocks(up)
+
+    grad_heads, grad_up = slots.run(
         [latent_sums, sums[1]],
-        added(head_grads),
+        all_head_grads,
         head_sums,
         projected[1],
         attended[1][0],
@@ -1111,12 +1117,11 @@
         grad_query_raw,
         grad_key_value,
     )
-    grad_heads = jnp.concatenate(head_sums[:2], axis=1).astype(BF16)
-    grad_heads = Flow(exchange(grad_heads.reshape(devices, piece, -1), BOTH))
-    grad_up = Flow(exchange_line(line_blocks(head_sums[2])))
+    grad_heads = Flow(exchange(grad_heads, BOTH))
+    grad_up = Flow(exchange_line(grad_up))
     latents = [latent_backward(whole_part[:, width:], projected[0]), None]
     finals[0] = slots.run(
-        [latent_sums, grad_up],
+        [latent_sums],
         functools.partial(input_backward, 0),
         whole_part[:, :width],
         latents[0][0],
@@ -1152,7 +1157,7 @@
         for micro in micros
     )
     grad_kv_down = Flow(exchange_line(line_blocks(grad_kv_down)))
-    slots.run([grad_kv_down, tiny, grad_heads, sums[0], sums[1]])
+    slots.run([grad_kv_down, grad_up, tiny, grad_heads, sums[0], sums[1]])
     for flow in (sums[0], sums[1]):
         slots.finish(flow)
     outputs = [

time: 1290 us -> 1290 us (level)
    optimization_barrier x18 -> x2, local copies, waits for them, and re-layouts: 18.4 us -> 2.86 us  [tie(): return lax.optimization_barrier((values, self.token))[0]]
    all_to_all x8, waiting for transfers between devices: 24.8 us -> 10 us  [exchange(): arrived, = (yield [lax.all_to_all(value, axes, 0, 0, tiled=True)])]
    unnamed x436 -> x391, local copies, waits for them, and re-layouts: 41.1 us -> 42.7 us
  transfers between devices with their start and end apart: 104 -> 104, of which waited for: 32 -> 35; matrix products, arithmetic and copies ran while one was open for 43% -> 43% of each run, Pallas kernels for 22% -> 23%
where the time goes in v4:
time: 1290 us; the launch traced here: 1280 us
  Pallas kernels  289 us (22%)
  waiting for transfers between devices  243 us (19%)
  other arithmetic  221 us (17%)
  matrix products  184 us (14%)
  local copies, waits for them, and re-layouts  183 us (14%)
  starting transfers between devices  138 us (11%)
  between operations  17.5 us (1%)
    ppermute x64, waiting for transfers between devices, swap(): return lax.ppermute(value, 'seq', [(i, i ^ 1 << bit) for i in range(count)])  131 us
    dot_general x20, matrix products, left_product(): lax.dot_general(left, right, (((0,), (0,)), ((), ())), preferred_element_...  125 us
    pallas_call x4, Pallas kernels, combine_stage(): pl.pallas_call(functools.partial(combine_kernel, blocks, capacity, cuts,...  101 us
    pallas_call x2, Pallas kernels, forward_stage(): pl.pallas_call(functools.partial(forward_kernel, blocks, capacity, expert...  74.4 us
    ppermute x3, waiting for transfers between devices, line_gather(): lax.ppermute(down, 'fsdp', [(i, i - 1) for i in range(1, count - step + 1)])  67.2 us
    convert_element_type x26, other arithmetic, fold(): sent.append(swap(send.astype(BF16), order[step]))  59.9 us
    ppermute x64, starting transfers between devices, swap(): return lax.ppermute(value, 'seq', [(i, i ^ 1 << bit) for i in range(count)])  57.1 us
    pallas_call x2, Pallas kernels, backward_stage(): pl.pallas_call(functools.partial(backward_kernel, blocks, capacity), grid...  47.4 us
  transfers between devices with their start and end apart: 104, of which 35 were waited for; matrix products, arithmetic and copies ran while one was open for 43% of the time, Pallas kernels for 23%

profile of v4, /device:TPU:0, one launch (start us, length us, event | category | flops | bytes accessed | tf_op | source)
XLA Modules:
  0.0 1275.6 jit_solution(11899631782376947491)
XLA Ops:
  49.7 13.9 %collective-permute-done.3 = bf16[128,1024]{1,0:T(8,128)(2,1)} collective-permute-done((bf16[128,1024]{1,0:T(8,128)(2,1)}, bf16[128,1024]{1,0:T(8,128)(2,1)}, u32[]{:S(2)}, u32[]{:S(2)}) %collective-permute-start.3) | collective-permute-done | bytes 262176 | tf_op jit(solution)/shard_map/ppermute | solution.py:64
  95.1 12.8 %collective-permute-done.6 = bf16[2,128,1024]{2,1,0:T(8,128)(2,1)S(1)} collective-permute-done((bf16[2,128,1024]{2,1,0:T(8,128)(2,1)S(1)}, bf16[2,128,1024]{2,1,0:T(8,128)(2,1)S(1)}, u32[]{:S(2)}, u32[]{:S(2)}) %collective-permute-start.6) | collective-permute-done | bytes 524320 | tf_op jit(solution)/shard_map/ppermute | solution.py:64
  235.4 12.6 collective-permute-done.14
  251.8 11.0 collective-permute-done.16
  310.4 34.9 %collective-permute-done.23 = bf16[128,2048]{1,0:T(8,128)(2,1)} collective-permute-done((bf16[128,2048]{1,0:T(8,128)(2,1)}, bf16[128,2048]{1,0:T(8,128)(2,1)}, u32[]{:S(2)}, u32[]{:S(2)}) %collective-permute-start.23) | collective-permute-done | bytes 524320 | tf_op jit(solution)/shard_map/ppermute | solution.py:192
  352.3 32.0 %collective-permute-done.25 = bf16[128,2048]{1,0:T(8,128)(2,1)} collective-permute-done((bf16[128,2048]{1,0:T(8,128)(2,1)}, bf16[128,2048]{1,0:T(8,128)(2,1)}, u32[]{:S(2)}, u32[]{:S(2)}) %collective-permute-start.25) | collective-permute-done | bytes 524320 | tf_op jit(solution)/shard_map/ppermute | solution.py:192
  432.2 37.2 %forward_stage.2 = (bf16[2048,2048]{1,0:T(8,128)(2,1)}, bf16[2048,704]{1,0:T(8,128)(2,1)}, bf16[2048,704]{1,0:T(8,128)(2,1)}, bf16[2048,704]{1,0:T(8,128)(2,1)},...) custom-call(s32[3]{0:T(128)} %pad_add_fusion.place_ref, ...), custom_call_target="tpu_custom_call" | custom-call | flops 16106127360 | bytes 25165824 | tf_op jit(solution)/shard_map/forward_stage/pallas_call | solution.py:548
  469.4 24.2 %backward_stage.2 = (bf16[2048,2048]{1,0:T(8,128)(2,1)}, bf16[2048,704]{1,0:T(8,128)(2,1)}, bf16[2048,704]{1,0:T(8,128)(2,1)}, bf16[4096,256]{1,0:T(8,128)(2,1)}, f32[32,1,128]{2,1,0:T(1,128)}) custom-call(s32[32,1,128]{2,1,0:T(1,128)} %copy_select_fusion.1.slots_ref, bf16[4096,2048]{1,0:T(8,128)(2,1)} %all-gather.9.cloned.1.call-done.top_ref, ...), custom_call_target="tpu_custom_call" | custom-call | flops 8053063680 | bytes 33554432 | tf_op jit(solution)/shard_map/backward_stage/pallas_call | solution.py:582
  497.1 29.2 %combine_stage.4 = (bf16[2048,1024]{1,0:T(8,128)(2,1)}, bf16[2048,1024]{1,0:T(8,128)(2,1)}, bf16[2048,1024]{1,0:T(8,128)(2,1)}, bf16[2048,1024]{1,0:T(8,128)(2,1)}) custom-call(s32[3]{0:T(128)} %pad_add_fusion.place_ref, s32[32,1,128]{2,1,0:T(1,128)} %copy_select_fusion.1.slots_ref, bf16[2048,704]{1,0:T(8,128)(2,1)} %get-tuple-element.529.refs_0_, ...), custom_call_target="tpu_custom_call" | custom-call | flops 17179869184 | bytes 25165824 | tf_op jit(solution)/shard_map/combine_stage/pallas_call | solution.py:660
  549.1 12.0 assemble.1.top_ref
  561.1 21.5 %combine_stage.5 = (bf16[2048,1024]{1,0:T(8,128)(2,1)}, bf16[2048,1024]{1,0:T(8,128)(2,1)}, bf16[2048,1024]{1,0:T(8,128)(2,1)}, bf16[2048,1024]{1,0:T(8,128)(2,1)}) custom-call(s32[3]{0:T(128)} %pad_add_fusion.place_ref, s32[32,1,128]{2,1,0:T(1,128)} %copy_select_fusion.1.slots_ref, bf16[2048,704]{1,0:T(8,128)(2,1)} %get-tuple-element.532.refs_0_, ...), custom_call_target="tpu_custom_call" | custom-call | flops 9126805504 | bytes 25165824 | tf_op jit(solution)/shard_map/combine_stage/pallas_call | solution.py:660
  609.1 11.5 fusion.239
  663.1 37.2 %forward_stage.3 = (bf16[2048,2048]{1,0:T(8,128)(2,1)}, bf16[2048,704]{1,0:T(8,128)(2,1)}, bf16[2048,704]{1,0:T(8,128)(2,1)}, bf16[2048,704]{1,0:T(8,128)(2,1)},...) custom-call(s32[3]{0:T(128)} %pad_add_fusion.place_ref, ...), custom_call_target="tpu_custom_call" | custom-call | flops 16106127360 | bytes 25165824 | tf_op jit(solution)/shard_map/forward_stage/pallas_call | solution.py:548
  711.1 23.2 %backward_stage.3 = (bf16[2048,2048]{1,0:T(8,128)(2,1)}, bf16[2048,704]{1,0:T(8,128)(2,1)}, bf16[2048,704]{1,0:T(8,128)(2,1)}, bf16[4096,256]{1,0:T(8,128)(2,1)}, f32[32,1,128]{2,1,0:T(1,128)}) custom-call(s32[32,1,128]{2,1,0:T(1,128)} %copy_select_fusion.slots_ref, bf16[4096,2048]{1,0:T(8,128)(2,1)} %assemble.1.top_ref, ...), custom_call_target="tpu_custom_call" | custom-call | flops 8053063680 | bytes 33554432 | tf_op jit(solution)/shard_map/backward_stage/pallas_call | solution.py:582
  738.4 29.7 %combine_stage.6 = (bf16[2048,1024]{1,0:T(8,128)(2,1)}, bf16[2048,1024]{1,0:T(8,128)(2,1)}, bf16[2048,1024]{1,0:T(8,128)(2,1)}, bf16[2048,1024]{1,0:T(8,128)(2,1)}) custom-call(s32[3]{0:T(128)} %pad_add_fusion.place_ref, s32[32,1,128]{2,1,0:T(1,128)} %copy_select_fusion.slots_ref, bf16[2048,704]{1,0:T(8,128)(2,1)} %get-tuple-element.623.refs_0_, ...), custom_call_target="tpu_custom_call" | custom-call | flops 17179869184 | bytes 25165824 | tf_op jit(solution)/shard_map/combine_stage/pallas_call | solution.py:660
  784.0 21.1 %combine_stage.7 = (bf16[2048,1024]{1,0:T(8,128)(2,1)}, bf16[2048,1024]{1,0:T(8,128)(2,1)}, bf16[2048,1024]{1,0:T(8,128)(2,1)}, bf16[2048,1024]{1,0:T(8,128)(2,1)}) custom-call(s32[3]{0:T(128)} %pad_add_fusion.place_ref, s32[32,1,128]{2,1,0:T(1,128)} %copy_select_fusion.slots_ref, bf16[2048,704]{1,0:T(8,128)(2,1)} %get-tuple-element.628.refs_0_, ...), custom_call_target="tpu_custom_call" | custom-call | flops 9126805504 | bytes 25165824 | tf_op jit(solution)/shard_map/combine_stage/pallas_call | solution.py:660
  825.6 11.2 convolution_add_fusion.2
  836.8 12.1 convolution_add_fusion.1
  888.4 13.9 %convolution_add_fusion.3 = bf16[2048,256]{1,0:T(8,128)(2,1)} fusion(f32[2048,256]{1,0:T(8,128)} %fusion.240, bf16[4096,2048]{1,0:T(8,128)(2,1)} %all-gather.13.cloned.1.call-done.tokens_ref, bf16[4096,256]{1,0:T(8,128)(2,1)} %get-tuple-element.643.refs_4_), kind=kOutput, calls=%fused_computation.75 | convolution fusion | flops 4296015872 | bytes 22020096 | tf_op jit(solution)/shard_map/dot_general | solution.py:30
  910.2 14.4 %collective-permute-done.58 = bf16[4,128,1024]{2,1,0:T(8,128)(2,1)S(1)} collective-permute-done((bf16[4,128,1024]{2,1,0:T(8,128)(2,1)S(1)}, bf16[4,128,1024]{2,1,0:T(8,128)(2,1)S(1)}, u32[]{:S(2)}, u32[]{:S(2)}) %collective-permute-start.58) | collective-permute-done | bytes 1048608 | tf_op jit(solution)/shard_map/ppermute | solution.py:64
  949.2 16.0 %attend_back_stage.2 = (bf16[1024,256]{1,0:T(8,128)(2,1)}, f32[1024,128]{1,0:T(8,128)}, bf16[2,1024,256]{2,1,0:T(8,128)(2,1)}, f32[1024,128]{1,0:T(8,128)}) custom-call(bf16[1024,256]{1,0:T(8,128)(2,1)} %copy.505.qn_ref, bf16[1024,128]{1,0:T(8,128)(2,1)} %copy.408.qr_ref, bf16[1024,512]{1,0:T(8,128)(2,1)} %convolution_convert_fusion.7.kv_ref, ...), custom_call_target="tpu_custom_call" | custom-call | flops 4294967296 | bytes 4194304 | tf_op jit(solution)/shard_map/attend_back_stage/pallas_call | solution.py:502
  1040.8 15.2 %all-gather.17.cloned.1.call-done = bf16[1024,2048]{1,0:T(8,128)(2,1)} async-done(((bf16[128,2048]{1,0:T(8,128)(2,1)}), bf16[1024,2048]{1,0:T(8,128)(2,1)}) %all-gather.17.cloned.1.call-update) | async-done | bytes 4194320 | tf_op jit(solution)/shard_map/all_gather | solution.py:1012
  1061.2 16.4 %attend_back_stage.3 = (bf16[1024,256]{1,0:T(8,128)(2,1)}, f32[1024,128]{1,0:T(8,128)}, bf16[2,1024,256]{2,1,0:T(8,128)(2,1)}, f32[1024,128]{1,0:T(8,128)}) custom-call(bf16[1024,256]{1,0:T(8,128)(2,1)} %copy.506.qn_ref, bf16[1024,128]{1,0:T(8,128)(2,1)} %copy.416.qr_ref, bf16[1024,512]{1,0:T(8,128)(2,1)} %convolution_convert_fusion.6.kv_ref, ...), custom_call_target="tpu_custom_call" | custom-call | flops 4294967296 | bytes 4194304 | tf_op jit(solution)/shard_map/attend_back_stage/pallas_call | solution.py:502
  1138.8 10.9 collective-permute-done.73
  (951 shorter events, 784.0 us)
Async XLA Ops:
  30.7 80.6 %all-to-all-start = ((bf16[32,64,640]{2,1,0:T(8,128)(2,1)}), bf16[32,64,640]{2,1,0:T(8,128)(2,1)}, u32[]{:S(2)}, u32[]{:S(2)}) async-start(bf16[32,64,640]{2,1,0:T(8,128)(2,1)} %bitcast.3), calls=%async_computation | async-start | bytes 5242880 | tf_op jit(solution)/shard_map/all_to_all | solution.py:165
  34.5 93.6 %all-gather.7.cloned.1.call-start = ((), (), s32[]{:S(2)}) async-start(), calls=%async_computation.10 | async-start | bytes 2703360 | tf_op jit(solution)/shard_map/all_gather | solution.py:750
  36.1 239.1 %all-gather.9.cloned.1.call-start = ((), (), s32[]{:S(2)}) async-start(), calls=%async_computation.11 | async-start | bytes 17301504 | tf_op jit(solution)/shard_map/all_gather | solution.py:788
  123.5 75.1 %all-to-all-start.2 = ((bf16[32,64,264]{2,1,0:T(8,128)(2,1)}), bf16[32,64,264]{2,1,0:T(8,128)(2,1)}, u32[]{:S(2)}, u32[]{:S(2)}) async-start(bf16[32,64,264]{2,1,0:T(8,128)(2,1)} %pad_maximum_fusion.13), calls=%async_computation.2 | async-start | bytes 3145728 | tf_op jit(solution)/shard_map/all_to_all | solution.py:165
  127.9 304.3 %all-gather.11.cloned.1.call-start = ((), (), s32[]{:S(2)}) async-start(), calls=%async_computation.12 | async-start | bytes 17301504 | tf_op jit(solution)/shard_map/all_gather | solution.py:859
  275.2 371.1 %all-gather.13.cloned.1.call-start = ((), (), s32[]{:S(2)}) async-start(), calls=%async_computation.13 | async-start | bytes 17301504 | tf_op jit(solution)/shard_map/all_gather | solution.py:862
  422.8 70.7 %collective-permute-start.32 = (bf16[512,1024]{1,0:T(8,128)(2,1)}, bf16[512,1024]{1,0:T(8,128)(2,1)}, u32[]{:S(2)}, u32[]{:S(2)}) collective-permute-start(bf16[512,1024]{1,0:T(8,128)(2,1)} %collective-permute-done.26), channel_id=1, source_target_pairs={{0,4},{4,0},{8,12},{12,8},{16,20},{20,16},{24,28},{28,24},{1,5},{5... | collective-permute-start | bytes 3145736 | tf_op jit(solution)/shard_map/ppermute | solution.py:64
  422.8 70.7 %collective-permute-start.33 = (bf16[512,1024]{1,0:T(8,128)(2,1)}, bf16[512,1024]{1,0:T(8,128)(2,1)}, u32[]{:S(2)}, u32[]{:S(2)}) collective-permute-start(bf16[512,1024]{1,0:T(8,128)(2,1)} %collective-permute-done.27), channel_id=1, source_target_pairs={{0,4},{4,0},{8,12},{12,8},{16,20},{20,16},{24,28},{28,24},{1,5},{5... | collective-permute-start | bytes 3145736 | tf_op jit(solution)/shard_map/ppermute | solution.py:64
  426.9 66.8 %collective-permute-start.31 = (bf16[2,512,1024]{2,1,0:T(8,128)(2,1)}, bf16[2,512,1024]{2,1,0:T(8,128)(2,1)}, u32[]{:S(2)}, u32[]{:S(2)}) collective-permute-start(bf16[2,512,1024]{2,1,0:T(8,128)(2,1)} %get-tuple-element.902), channel_id=1, source_target_pairs={{0,8},{4,12},{8,0},{12,4},{16,24},{20,28},{24,16},{28,20},{1,9},{5... | collective-permute-start | bytes 6291464 | tf_op jit(solution)/shard_map/ppermute | solution.py:64
  432.1 61.5 %collective-permute-start.30 = (bf16[2,512,1024]{2,1,0:T(8,128)(2,1)}, bf16[2,512,1024]{2,1,0:T(8,128)(2,1)}, u32[]{:S(2)}, u32[]{:S(2)}) collective-permute-start(bf16[2,512,1024]{2,1,0:T(8,128)(2,1)} %get-tuple-element.904), channel_id=1, source_target_pairs={{0,16},{4,20},{8,24},{12,28},{16,0},{20,4},{24,8},{28,12},{1,17},{... | collective-permute-start | bytes 6291464 | tf_op jit(solution)/shard_map/ppermute | solution.py:64
  656.6 111.5 %collective-permute-start.48 = (bf16[2,4,128,1024]{3,2,1,0:T(8,128)(2,1)}, bf16[2,4,128,1024]{3,2,1,0:T(8,128)(2,1)}, u32[]{:S(2)}, u32[]{:S(2)}) collective-permute-start(bf16[2,4,128,1024]{3,2,1,0:T(8,128)(2,1)} %bitcast.137), channel_id=1, source_target_pairs={{0,16},{4,20},{8,24},{12,28},{16,0},{20,4},{24,8},{28,12},{1,17},{... | collective-permute-start | bytes 6291464 | tf_op jit(solution)/shard_map/ppermute | solution.py:64
  661.4 106.7 %collective-permute-start.47 = (bf16[2,4,128,1024]{3,2,1,0:T(8,128)(2,1)}, bf16[2,4,128,1024]{3,2,1,0:T(8,128)(2,1)}, u32[]{:S(2)}, u32[]{:S(2)}) collective-permute-start(bf16[2,4,128,1024]{3,2,1,0:T(8,128)(2,1)} %fusion.8), channel_id=1, source_target_pairs={{0,8},{4,12},{8,0},{12,4},{16,24},{20,28},{24,16},{28,20},{1,9},{5... | collective-permute-start | bytes 6291464 | tf_op jit(solution)/shard_map/ppermute | solution.py:64
  706.5 61.5 %collective-permute-start.46 = (bf16[128,2048]{1,0:T(8,128)(2,1)}, bf16[128,2048]{1,0:T(8,128)(2,1)S(1)}, u32[]{:S(2)}, u32[]{:S(2)}) collective-permute-start(bf16[128,2048]{1,0:T(8,128)(2,1)} %get-tuple-element.905), channel_id=1, source_target_pairs={{0,3},{1,0},{2,1},{3,2},{4,7},{5,4},{6,5},{7,6},{8,11},{9,8},{10,9... | collective-permute-start | bytes 1572872 | tf_op jit(solution)/shard_map/ppermute | solution.py:177
  709.9 58.2 %collective-permute-start.44 = (bf16[128,2048]{1,0:T(8,128)(2,1)}, bf16[128,2048]{1,0:T(8,128)(2,1)}, u32[]{:S(2)}, u32[]{:S(2)}) collective-permute-start(bf16[128,2048]{1,0:T(8,128)(2,1)} %get-tuple-element.906), channel_id=1, source_target_pairs={{0,1},{1,2},{2,3},{3,0},{4,5},{5,6},{6,7},{7,4},{8,9},{9,10},{10,1... | collective-permute-start | bytes 1572872 | tf_op jit(solution)/shard_map/ppermute | solution.py:177
  709.9 58.2 %collective-permute-start.45 = (bf16[128,2048]{1,0:T(8,128)(2,1)}, bf16[128,2048]{1,0:T(8,128)(2,1)}, u32[]{:S(2)}, u32[]{:S(2)}) collective-permute-start(bf16[128,2048]{1,0:T(8,128)(2,1)} %get-tuple-element.907), channel_id=1, source_target_pairs={{0,2},{1,3},{2,0},{3,1},{4,6},{5,7},{6,4},{7,5},{8,10},{9,11},{10,... | collective-permute-start | bytes 1572872 | tf_op jit(solution)/shard_map/ppermute | solution.py:177
  738.4 205.6 %all-gather.15.cloned.1.call-start = ((), (), s32[]{:S(2)}) async-start(), calls=%async_computation.14 | async-start | bytes 4718592 | tf_op jit(solution)/shard_map/all_gather | solution.py:1012
  875.5 180.5 %all-gather.17.cloned.1.call-start = ((), (), s32[]{:S(2)}) async-start(), calls=%async_computation.15 | async-start | bytes 4718592 | tf_op jit(solution)/shard_map/all_gather | solution.py:1012
  992.8 139.5 %reduce-scatter.3.cloned.1.call-start = ((), (), s32[]{:S(2)}) async-start(), calls=%async_computation.16 | async-start | bytes 6193152 | tf_op jit(solution)/shard_map/reduce_scatter | solution.py:1089
  1009.6 74.2 %all-to-all-start.5 = ((bf16[32,64,264]{2,1,0:T(8,128)(2,1)}), bf16[32,64,264]{2,1,0:T(8,128)(2,1)}, u32[]{:S(2)}, u32[]{:S(2)}) async-start(bf16[32,64,264]{2,1,0:T(8,128)(2,1)} %pad_maximum_fusion.14), calls=%async_computation.5 | async-start | bytes 3145728 | tf_op jit(solution)/shard_map/all_to_all | solution.py:165
  1015.1 200.6 %reduce-scatter.5.cloned.1.call-start = ((), (), s32[]{:S(2)}) async-start(), calls=%async_computation.17 | async-start | bytes 4718592 | tf_op jit(solution)/shard_map/reduce_scatter | solution.py:1103
  1149.8 73.1 %all-to-all-start.6 = ((bf16[32,64,640]{2,1,0:T(8,128)(2,1)}), bf16[32,64,640]{2,1,0:T(8,128)(2,1)}, u32[]{:S(2)}, u32[]{:S(2)}) async-start(bf16[32,64,640]{2,1,0:T(8,128)(2,1)} %pad_maximum_fusion.6), calls=%async_computation.7 | async-start | bytes 5242880 | tf_op jit(solution)/shard_map/all_to_all | solution.py:165
  1168.2 87.8 %collective-permute-start.85 = (bf16[128,512]{0,1:T(8,128)(2,1)}, bf16[128,512]{0,1:T(8,128)(2,1)}, u32[]{:S(2)}, u32[]{:S(2)}) collective-permute-start(bf16[128,512]{0,1:T(8,128)(2,1)} %bitcast.277), channel_id=1, source_target_pairs={{0,1},{1,2},{2,3},{3,0},{4,5},{5,6},{6,7},{7,4},{8,9},{9,10},{10,1... | collective-permute-start | bytes 393224 | tf_op jit(solution)/shard_map/ppermute | solution.py:177
  1169.5 90.6 %collective-permute-start.86 = (bf16[128,512]{0,1:T(8,128)(2,1)}, bf16[128,512]{0,1:T(8,128)(2,1)}, u32[]{:S(2)}, u32[]{:S(2)}) collective-permute-start(bf16[128,512]{0,1:T(8,128)(2,1)} %bitcast.743), channel_id=1, source_target_pairs={{0,2},{1,3},{2,0},{3,1},{4,6},{5,7},{6,4},{7,5},{8,10},{9,11},{10,... | collective-permute-start | bytes 393224 | tf_op jit(solution)/shard_map/ppermute | solution.py:177
  1172.0 88.2 %collective-permute-start.87 = (bf16[128,512]{0,1:T(8,128)(2,1)}, bf16[128,512]{0,1:T(8,128)(2,1)}, u32[]{:S(2)}, u32[]{:S(2)}) collective-permute-start(bf16[128,512]{0,1:T(8,128)(2,1)} %bitcast.742), channel_id=1, source_target_pairs={{0,3},{1,0},{2,1},{3,2},{4,7},{5,4},{6,5},{7,6},{8,11},{9,8},{10,9... | collective-permute-start | bytes 393224 | tf_op jit(solution)/shard_map/ppermute | solution.py:177
  (264 other events, 3970.5 us)
Sparse Core Ops, SparseCore 0:
  38.8 76.5 all-gather.6
  118.4 154.7 all-gather.8
  276.1 129.5 all-gather.10
  408.6 134.7 all-gather.12
  875.6 52.1 all-gather.14
  992.9 63.0 all-gather.16
  1059.4 57.4 reduce-scatter.2
  1120.6 66.7 reduce-scatter.4

commit v5 on v4

--- a/solution.py
+++ b/solution.py
@@ -765,7 +765,7 @@
         for_heads[:, None], (seqs, line, piece, query_width + out_width)
     ).reshape(devices, piece, query_width + out_width)
     ready, for_heads = lax.optimization_barrier((tokens_in, for_heads))
-    tokens = [Flow(gather_seq(ready[micro])) for micro in micros]
+    tokens = [Flow(gather_seq(ready[0])), None]
     for_heads = Flow(exchange(for_heads, BOTH))
     up_weight = Flow(
         exchange(jnp.broadcast_to(w_kv_up[None], (line,) + w_kv_up.shape), "fsdp")
@@ -782,12 +782,11 @@
             axis=2,
         )
 
-    for_shared = slots.run(tokens, pack_shared, w_shared_gate, w_shared_up, w_shared_down)
+    for_shared = slots.run(tokens[:1], pack_shared, w_shared_gate, w_shared_up, w_shared_down)
     for_shared = Flow(exchange(for_shared, BOTH))
-    slots.run([*tokens, for_heads, up_weight])
+    slots.run([tokens[0], for_heads, up_weight])
     tops = [lax.all_gather(slots.tie(cotangent[0]), BOTH, axis=0, tiled=True), None]
-    slots.finish(tokens[0], tokens[1])
-    slots.finish(tokens[1])
+    slots.finish(tokens[0])
     (small,) = slots.run([], lambda *given: given, small)
     for_heads, up_weight = for_heads.value, up_weight.value
     for_heads = for_heads.reshape(width, query_width + out_width)
@@ -847,9 +846,13 @@
     attended = [None, None]
     residuals = [None, None]
     normed_alls = [None, None]
-    projected[0] = slots.run([], projections, tokens[0].value)
-    attended[0] = slots.run([], functools.partial(attend, 0), projected[0][2][0])
+    tokens[1] = Flow(gather_seq(slots.tie(tokens_in[1])))
+    projected[0] = slots.run([tokens[1]], projections, tokens[0].value)
+    attended[0] = slots.run(
+        [tokens[1]], functools.partial(attend, 0), projected[0][2][0]
+    )
     summed = Flow(scatter_seq(attended[0][1], rows))
+    slots.finish(tokens[1], summed)
     projected[1] = slots.run([summed, for_shared], projections, tokens[1].value)
     attended[1] = slots.run([summed], functools.partial(attend, 1), projected[1][2][0])
     summed_two = Flow(scatter_seq(attended[1][1], rows))

time: 1290 us -> 1330 us (1.031)
  waiting for transfers between devices: 243 us -> 269 us
    all_to_all x8, waiting for transfers between devices: 10 us -> 51.7 us  [exchange(): arrived, = (yield [lax.all_to_all(value, axes, 0, 0, tiled=True)])]
    ppermute x64, waiting for transfers between devices: 131 us -> 112 us  [swap(): return lax.ppermute(value, 'seq', [(i, i ^ 1 << bit) for i in range(count)])]
    unnamed x391 -> x371, local copies, waits for them, and re-layouts: 42.7 us -> 42 us
  transfers between devices with their start and end apart: 104 -> 104, of which waited for: 35 -> 33; matrix products, arithmetic and copies ran while one was open for 43% -> 42% of each run, Pallas kernels for 23% -> 22%
where the time goes in v5:
time: 1330 us; the launch traced here: 1310 us
  Pallas kernels  289 us (22%)
  waiting for transfers between devices  269 us (20%)
  other arithmetic  225 us (17%)
  local copies, waits for them, and re-layouts  185 us (14%)
  matrix products  185 us (14%)
  starting transfers between devices  143 us (11%)
  between operations  17.4 us (1%)
    dot_general x20, matrix products, left_product(): lax.dot_general(left, right, (((0,), (0,)), ((), ())), preferred_element_...  124 us
    ppermute x64, waiting for transfers between devices, swap(): return lax.ppermute(value, 'seq', [(i, i ^ 1 << bit) for i in range(count)])  112 us
    pallas_call x4, Pallas kernels, combine_stage(): pl.pallas_call(functools.partial(combine_kernel, blocks, capacity, cuts,...  102 us
    pallas_call x2, Pallas kernels, forward_stage(): pl.pallas_call(functools.partial(forward_kernel, blocks, capacity, expert...  74.4 us
    ppermute x3, waiting for transfers between devices, line_gather(): lax.ppermute(down, 'fsdp', [(i, i - 1) for i in range(1, count - step + 1)])  66 us
    convert_element_type x26, other arithmetic, fold(): sent.append(swap(send.astype(BF16), order[step]))  60.9 us
    ppermute x64, starting transfers between devices, swap(): return lax.ppermute(value, 'seq', [(i, i ^ 1 << bit) for i in range(count)])  60.4 us
    all_to_all x8, waiting for transfers between devices, exchange(): arrived, = (yield [lax.all_to_all(value, axes, 0, 0, tiled=True)])  51.7 us
  transfers between devices with their start and end apart: 104, of which 33 were waited for; matrix products, arithmetic and copies ran while one was open for 42% of the time, Pallas kernels for 22%

profile of v5, /device:TPU:0, one launch (start us, length us, event | category | flops | bytes accessed | tf_op | source)
XLA Modules:
  0.0 1313.9 jit_solution(1712562534700523129)
XLA Ops:
  47.7 15.3 %collective-permute-done.1 = bf16[128,1024]{1,0:T(8,128)(2,1)} collective-permute-done((bf16[128,1024]{1,0:T(8,128)(2,1)}, bf16[128,1024]{1,0:T(8,128)(2,1)}, u32[]{:S(2)}, u32[]{:S(2)}) %collective-permute-start.1) | collective-permute-done | bytes 262176 | tf_op jit(solution)/shard_map/ppermute | solution.py:64
  67.4 14.9 %collective-permute-done.2 = bf16[2,128,1024]{2,1,0:T(8,128)(2,1)S(1)} collective-permute-done((bf16[2,128,1024]{2,1,0:T(8,128)(2,1)S(1)}, bf16[2,128,1024]{2,1,0:T(8,128)(2,1)S(1)}, u32[]{:S(2)}, u32[]{:S(2)}) %collective-permute-start.2) | collective-permute-done | bytes 524320 | tf_op jit(solution)/shard_map/ppermute | solution.py:64
  87.0 11.8 all-to-all-done
  225.9 29.9 %all-to-all-done.2 = bf16[32,64,264]{2,1,0:T(8,128)(2,1)} async-done(((bf16[32,64,264]{2,1,0:T(8,128)(2,1)}), bf16[32,64,264]{2,1,0:T(8,128)(2,1)}, u32[]{:S(2)}, u32[]{:S(2)}) %all-to-all-start.2) | async-done | bytes 1081376 | tf_op jit(solution)/shard_map/all_to_all | solution.py:165
  288.1 11.9 collective-permute-done.16
  350.5 34.0 %collective-permute-done.23 = bf16[128,2048]{1,0:T(8,128)(2,1)} collective-permute-done((bf16[128,2048]{1,0:T(8,128)(2,1)}, bf16[128,2048]{1,0:T(8,128)(2,1)}, u32[]{:S(2)}, u32[]{:S(2)}) %collective-permute-start.23) | collective-permute-done | bytes 524320 | tf_op jit(solution)/shard_map/ppermute | solution.py:192
  391.5 32.0 %collective-permute-done.25 = bf16[128,2048]{1,0:T(8,128)(2,1)} collective-permute-done((bf16[128,2048]{1,0:T(8,128)(2,1)}, bf16[128,2048]{1,0:T(8,128)(2,1)}, u32[]{:S(2)}, u32[]{:S(2)}) %collective-permute-start.25) | collective-permute-done | bytes 524320 | tf_op jit(solution)/shard_map/ppermute | solution.py:192
  471.2 37.2 %forward_stage.2 = (bf16[2048,2048]{1,0:T(8,128)(2,1)}, bf16[2048,704]{1,0:T(8,128)(2,1)}, bf16[2048,704]{1,0:T(8,128)(2,1)}, bf16[2048,704]{1,0:T(8,128)(2,1)},...) custom-call(s32[3]{0:T(128)} %pad_add_fusion.place_ref, ...), custom_call_target="tpu_custom_call" | custom-call | flops 16106127360 | bytes 25165824 | tf_op jit(solution)/shard_map/forward_stage/pallas_call | solution.py:548
  508.4 23.7 %backward_stage.2 = (bf16[2048,2048]{1,0:T(8,128)(2,1)}, bf16[2048,704]{1,0:T(8,128)(2,1)}, bf16[2048,704]{1,0:T(8,128)(2,1)}, bf16[4096,256]{1,0:T(8,128)(2,1)}, f32[32,1,128]{2,1,0:T(1,128)}) custom-call(s32[32,1,128]{2,1,0:T(1,128)} %copy_select_fusion.1.slots_ref, bf16[4096,2048]{1,0:T(8,128)(2,1)} %all-gather.9.cloned.1.call-done.top_ref, ...), custom_call_target="tpu_custom_call" | custom-call | flops 8053063680 | bytes 33554432 | tf_op jit(solution)/shard_map/backward_stage/pallas_call | solution.py:582
  535.6 29.2 %combine_stage.4 = (bf16[2048,1024]{1,0:T(8,128)(2,1)}, bf16[2048,1024]{1,0:T(8,128)(2,1)}, bf16[2048,1024]{1,0:T(8,128)(2,1)}, bf16[2048,1024]{1,0:T(8,128)(2,1)}) custom-call(s32[3]{0:T(128)} %pad_add_fusion.place_ref, s32[32,1,128]{2,1,0:T(1,128)} %copy_select_fusion.1.slots_ref, bf16[2048,704]{1,0:T(8,128)(2,1)} %get-tuple-element.533.refs_0_, ...), custom_call_target="tpu_custom_call" | custom-call | flops 17179869184 | bytes 25165824 | tf_op jit(solution)/shard_map/combine_stage/pallas_call | solution.py:660
  587.7 12.0 assemble.1.top_ref
  599.7 21.5 %combine_stage.5 = (bf16[2048,1024]{1,0:T(8,128)(2,1)}, bf16[2048,1024]{1,0:T(8,128)(2,1)}, bf16[2048,1024]{1,0:T(8,128)(2,1)}, bf16[2048,1024]{1,0:T(8,128)(2,1)}) custom-call(s32[3]{0:T(128)} %pad_add_fusion.place_ref, s32[32,1,128]{2,1,0:T(1,128)} %copy_select_fusion.1.slots_ref, bf16[2048,704]{1,0:T(8,128)(2,1)} %get-tuple-element.536.refs_0_, ...), custom_call_target="tpu_custom_call" | custom-call | flops 9126805504 | bytes 25165824 | tf_op jit(solution)/shard_map/combine_stage/pallas_call | solution.py:660
  647.5 11.4 fusion.239
  701.6 37.2 %forward_stage.3 = (bf16[2048,2048]{1,0:T(8,128)(2,1)}, bf16[2048,704]{1,0:T(8,128)(2,1)}, bf16[2048,704]{1,0:T(8,128)(2,1)}, bf16[2048,704]{1,0:T(8,128)(2,1)},...) custom-call(s32[3]{0:T(128)} %pad_add_fusion.place_ref, ...), custom_call_target="tpu_custom_call" | custom-call | flops 16106127360 | bytes 25165824 | tf_op jit(solution)/shard_map/forward_stage/pallas_call | solution.py:548
  749.4 23.3 %backward_stage.3 = (bf16[2048,2048]{1,0:T(8,128)(2,1)}, bf16[2048,704]{1,0:T(8,128)(2,1)}, bf16[2048,704]{1,0:T(8,128)(2,1)}, bf16[4096,256]{1,0:T(8,128)(2,1)}, f32[32,1,128]{2,1,0:T(1,128)}) custom-call(s32[32,1,128]{2,1,0:T(1,128)} %copy_select_fusion.slots_ref, bf16[4096,2048]{1,0:T(8,128)(2,1)} %assemble.1.top_ref, ...), custom_call_target="tpu_custom_call" | custom-call | flops 8053063680 | bytes 33554432 | tf_op jit(solution)/shard_map/backward_stage/pallas_call | solution.py:582
  776.9 29.7 %combine_stage.6 = (bf16[2048,1024]{1,0:T(8,128)(2,1)}, bf16[2048,1024]{1,0:T(8,128)(2,1)}, bf16[2048,1024]{1,0:T(8,128)(2,1)}, bf16[2048,1024]{1,0:T(8,128)(2,1)}) custom-call(s32[3]{0:T(128)} %pad_add_fusion.place_ref, s32[32,1,128]{2,1,0:T(1,128)} %copy_select_fusion.slots_ref, bf16[2048,704]{1,0:T(8,128)(2,1)} %get-tuple-element.627.refs_0_, ...), custom_call_target="tpu_custom_call" | custom-call | flops 17179869184 | bytes 25165824 | tf_op jit(solution)/shard_map/combine_stage/pallas_call | solution.py:660
  822.6 21.2 %combine_stage.7 = (bf16[2048,1024]{1,0:T(8,128)(2,1)}, bf16[2048,1024]{1,0:T(8,128)(2,1)}, bf16[2048,1024]{1,0:T(8,128)(2,1)}, bf16[2048,1024]{1,0:T(8,128)(2,1)}) custom-call(s32[3]{0:T(128)} %pad_add_fusion.place_ref, s32[32,1,128]{2,1,0:T(1,128)} %copy_select_fusion.slots_ref, bf16[2048,704]{1,0:T(8,128)(2,1)} %get-tuple-element.632.refs_0_, ...), custom_call_target="tpu_custom_call" | custom-call | flops 9126805504 | bytes 25165824 | tf_op jit(solution)/shard_map/combine_stage/pallas_call | solution.py:660
  864.1 11.2 convolution_add_fusion.2
  875.4 12.1 convolution_add_fusion.1
  927.0 13.8 %convolution_add_fusion.3 = bf16[2048,256]{1,0:T(8,128)(2,1)} fusion(f32[2048,256]{1,0:T(8,128)} %fusion.240, bf16[4096,2048]{1,0:T(8,128)(2,1)} %all-gather.13.cloned.1.call-done.tokens_ref, bf16[4096,256]{1,0:T(8,128)(2,1)} %get-tuple-element.647.refs_4_), kind=kOutput, calls=%fused_computation.75 | convolution fusion | flops 4296015872 | bytes 22020096 | tf_op jit(solution)/shard_map/dot_general | solution.py:30
  948.7 14.4 %collective-permute-done.58 = bf16[4,128,1024]{2,1,0:T(8,128)(2,1)S(1)} collective-permute-done((bf16[4,128,1024]{2,1,0:T(8,128)(2,1)S(1)}, bf16[4,128,1024]{2,1,0:T(8,128)(2,1)S(1)}, u32[]{:S(2)}, u32[]{:S(2)}) %collective-permute-start.58) | collective-permute-done | bytes 1048608 | tf_op jit(solution)/shard_map/ppermute | solution.py:64
  987.8 16.0 %attend_back_stage.2 = (bf16[1024,256]{1,0:T(8,128)(2,1)}, f32[1024,128]{1,0:T(8,128)}, bf16[2,1024,256]{2,1,0:T(8,128)(2,1)}, f32[1024,128]{1,0:T(8,128)}) custom-call(bf16[1024,256]{1,0:T(8,128)(2,1)} %copy.505.qn_ref, bf16[1024,128]{1,0:T(8,128)(2,1)} %copy.407.qr_ref, bf16[1024,512]{1,0:T(8,128)(2,1)} %convolution_convert_fusion.7.kv_ref, ...), custom_call_target="tpu_custom_call" | custom-call | flops 4294967296 | bytes 4194304 | tf_op jit(solution)/shard_map/attend_back_stage/pallas_call | solution.py:502
  1079.4 15.1 %all-gather.17.cloned.1.call-done = bf16[1024,2048]{1,0:T(8,128)(2,1)} async-done(((bf16[128,2048]{1,0:T(8,128)(2,1)}), bf16[1024,2048]{1,0:T(8,128)(2,1)}) %all-gather.17.cloned.1.call-update) | async-done | bytes 4194320 | tf_op jit(solution)/shard_map/all_gather | solution.py:1015
  1099.7 16.3 %attend_back_stage.3 = (bf16[1024,256]{1,0:T(8,128)(2,1)}, f32[1024,128]{1,0:T(8,128)}, bf16[2,1024,256]{2,1,0:T(8,128)(2,1)}, f32[1024,128]{1,0:T(8,128)}) custom-call(bf16[1024,256]{1,0:T(8,128)(2,1)} %copy.506.qn_ref, bf16[1024,128]{1,0:T(8,128)(2,1)} %copy.416.qr_ref, bf16[1024,512]{1,0:T(8,128)(2,1)} %convolution_convert_fusion.6.kv_ref, ...), custom_call_target="tpu_custom_call" | custom-call | flops 4294967296 | bytes 4194304 | tf_op jit(solution)/shard_map/attend_back_stage/pallas_call | solution.py:502
  (934 shorter events, 801.4 us)
Async XLA Ops:
  30.7 68.1 %all-to-all-start = ((bf16[32,64,640]{2,1,0:T(8,128)(2,1)}), bf16[32,64,640]{2,1,0:T(8,128)(2,1)}, u32[]{:S(2)}, u32[]{:S(2)}) async-start(bf16[32,64,640]{2,1,0:T(8,128)(2,1)} %bitcast.7), calls=%async_computation | async-start | bytes 5242880 | tf_op jit(solution)/shard_map/all_to_all | solution.py:165
  34.5 77.4 %all-gather.7.cloned.1.call-start = ((), (), s32[]{:S(2)}) async-start(), calls=%async_computation.10 | async-start | bytes 2703360 | tf_op jit(solution)/shard_map/all_gather | solution.py:750
  36.1 277.1 %all-gather.9.cloned.1.call-start = ((), (), s32[]{:S(2)}) async-start(), calls=%async_computation.11 | async-start | bytes 17301504 | tf_op jit(solution)/shard_map/all_gather | solution.py:788
  183.3 72.4 %all-to-all-start.2 = ((bf16[32,64,264]{2,1,0:T(8,128)(2,1)}), bf16[32,64,264]{2,1,0:T(8,128)(2,1)}, u32[]{:S(2)}, u32[]{:S(2)}) async-start(bf16[32,64,264]{2,1,0:T(8,128)(2,1)} %pad_maximum_fusion.13), calls=%async_computation.2 | async-start | bytes 3145728 | tf_op jit(solution)/shard_map/all_to_all | solution.py:165
  188.0 283.2 %all-gather.11.cloned.1.call-start = ((), (), s32[]{:S(2)}) async-start(), calls=%async_computation.12 | async-start | bytes 17301504 | tf_op jit(solution)/shard_map/all_gather | solution.py:862
  313.3 371.3 %all-gather.13.cloned.1.call-start = ((), (), s32[]{:S(2)}) async-start(), calls=%async_computation.13 | async-start | bytes 17301504 | tf_op jit(solution)/shard_map/all_gather | solution.py:865
  461.9 70.3 %collective-permute-start.32 = (bf16[512,1024]{1,0:T(8,128)(2,1)}, bf16[512,1024]{1,0:T(8,128)(2,1)}, u32[]{:S(2)}, u32[]{:S(2)}) collective-permute-start(bf16[512,1024]{1,0:T(8,128)(2,1)} %collective-permute-done.26), channel_id=1, source_target_pairs={{0,4},{4,0},{8,12},{12,8},{16,20},{20,16},{24,28},{28,24},{1,5},{5... | collective-permute-start | bytes 3145736 | tf_op jit(solution)/shard_map/ppermute | solution.py:64
  461.9 70.3 %collective-permute-start.33 = (bf16[512,1024]{1,0:T(8,128)(2,1)}, bf16[512,1024]{1,0:T(8,128)(2,1)}, u32[]{:S(2)}, u32[]{:S(2)}) collective-permute-start(bf16[512,1024]{1,0:T(8,128)(2,1)} %collective-permute-done.27), channel_id=1, source_target_pairs={{0,4},{4,0},{8,12},{12,8},{16,20},{20,16},{24,28},{28,24},{1,5},{5... | collective-permute-start | bytes 3145736 | tf_op jit(solution)/shard_map/ppermute | solution.py:64
  465.9 66.4 %collective-permute-start.31 = (bf16[2,512,1024]{2,1,0:T(8,128)(2,1)}, bf16[2,512,1024]{2,1,0:T(8,128)(2,1)}, u32[]{:S(2)}, u32[]{:S(2)}) collective-permute-start(bf16[2,512,1024]{2,1,0:T(8,128)(2,1)} %get-tuple-element.906), channel_id=1, source_target_pairs={{0,8},{4,12},{8,0},{12,4},{16,24},{20,28},{24,16},{28,20},{1,9},{5... | collective-permute-start | bytes 6291464 | tf_op jit(solution)/shard_map/ppermute | solution.py:64
  471.2 61.1 %collective-permute-start.30 = (bf16[2,512,1024]{2,1,0:T(8,128)(2,1)}, bf16[2,512,1024]{2,1,0:T(8,128)(2,1)}, u32[]{:S(2)}, u32[]{:S(2)}) collective-permute-start(bf16[2,512,1024]{2,1,0:T(8,128)(2,1)} %get-tuple-element.908), channel_id=1, source_target_pairs={{0,16},{4,20},{8,24},{12,28},{16,0},{20,4},{24,8},{28,12},{1,17},{... | collective-permute-start | bytes 6291464 | tf_op jit(solution)/shard_map/ppermute | solution.py:64
  694.7 111.9 %collective-permute-start.48 = (bf16[2,4,128,1024]{3,2,1,0:T(8,128)(2,1)}, bf16[2,4,128,1024]{3,2,1,0:T(8,128)(2,1)}, u32[]{:S(2)}, u32[]{:S(2)}) collective-permute-start(bf16[2,4,128,1024]{3,2,1,0:T(8,128)(2,1)} %bitcast.135), channel_id=1, source_target_pairs={{0,16},{4,20},{8,24},{12,28},{16,0},{20,4},{24,8},{28,12},{1,17},{... | collective-permute-start | bytes 6291464 | tf_op jit(solution)/shard_map/ppermute | solution.py:64
  700.7 106.0 %collective-permute-start.47 = (bf16[2,4,128,1024]{3,2,1,0:T(8,128)(2,1)}, bf16[2,4,128,1024]{3,2,1,0:T(8,128)(2,1)}, u32[]{:S(2)}, u32[]{:S(2)}) collective-permute-start(bf16[2,4,128,1024]{3,2,1,0:T(8,128)(2,1)} %fusion.8), channel_id=1, source_target_pairs={{0,8},{4,12},{8,0},{12,4},{16,24},{20,28},{24,16},{28,20},{1,9},{5... | collective-permute-start | bytes 6291464 | tf_op jit(solution)/shard_map/ppermute | solution.py:64
  745.0 61.6 %collective-permute-start.46 = (bf16[128,2048]{1,0:T(8,128)(2,1)}, bf16[128,2048]{1,0:T(8,128)(2,1)S(1)}, u32[]{:S(2)}, u32[]{:S(2)}) collective-permute-start(bf16[128,2048]{1,0:T(8,128)(2,1)} %get-tuple-element.909), channel_id=1, source_target_pairs={{0,3},{1,0},{2,1},{3,2},{4,7},{5,4},{6,5},{7,6},{8,11},{9,8},{10,9... | collective-permute-start | bytes 1572872 | tf_op jit(solution)/shard_map/ppermute | solution.py:177
  748.5 58.1 %collective-permute-start.44 = (bf16[128,2048]{1,0:T(8,128)(2,1)}, bf16[128,2048]{1,0:T(8,128)(2,1)}, u32[]{:S(2)}, u32[]{:S(2)}) collective-permute-start(bf16[128,2048]{1,0:T(8,128)(2,1)} %get-tuple-element.910), channel_id=1, source_target_pairs={{0,1},{1,2},{2,3},{3,0},{4,5},{5,6},{6,7},{7,4},{8,9},{9,10},{10,1... | collective-permute-start | bytes 1572872 | tf_op jit(solution)/shard_map/ppermute | solution.py:177
  748.5 58.1 %collective-permute-start.45 = (bf16[128,2048]{1,0:T(8,128)(2,1)}, bf16[128,2048]{1,0:T(8,128)(2,1)}, u32[]{:S(2)}, u32[]{:S(2)}) collective-permute-start(bf16[128,2048]{1,0:T(8,128)(2,1)} %get-tuple-element.911), channel_id=1, source_target_pairs={{0,2},{1,3},{2,0},{3,1},{4,6},{5,7},{6,4},{7,5},{8,10},{9,11},{10,... | collective-permute-start | bytes 1572872 | tf_op jit(solution)/shard_map/ppermute | solution.py:177
  776.9 205.7 %all-gather.15.cloned.1.call-start = ((), (), s32[]{:S(2)}) async-start(), calls=%async_computation.14 | async-start | bytes 4718592 | tf_op jit(solution)/shard_map/all_gather | solution.py:1015
  914.1 180.4 %all-gather.17.cloned.1.call-start = ((), (), s32[]{:S(2)}) async-start(), calls=%async_computation.15 | async-start | bytes 4718592 | tf_op jit(solution)/shard_map/all_gather | solution.py:1015
  1031.4 139.4 %reduce-scatter.3.cloned.1.call-start = ((), (), s32[]{:S(2)}) async-start(), calls=%async_computation.16 | async-start | bytes 6193152 | tf_op jit(solution)/shard_map/reduce_scatter | solution.py:1092
  1048.3 74.0 %all-to-all-start.5 = ((bf16[32,64,264]{2,1,0:T(8,128)(2,1)}), bf16[32,64,264]{2,1,0:T(8,128)(2,1)}, u32[]{:S(2)}, u32[]{:S(2)}) async-start(bf16[32,64,264]{2,1,0:T(8,128)(2,1)} %pad_maximum_fusion.14), calls=%async_computation.5 | async-start | bytes 3145728 | tf_op jit(solution)/shard_map/all_to_all | solution.py:165
  1053.7 200.4 %reduce-scatter.5.cloned.1.call-start = ((), (), s32[]{:S(2)}) async-start(), calls=%async_computation.17 | async-start | bytes 4718592 | tf_op jit(solution)/shard_map/reduce_scatter | solution.py:1106
  1188.3 72.9 %all-to-all-start.6 = ((bf16[32,64,640]{2,1,0:T(8,128)(2,1)}), bf16[32,64,640]{2,1,0:T(8,128)(2,1)}, u32[]{:S(2)}, u32[]{:S(2)}) async-start(bf16[32,64,640]{2,1,0:T(8,128)(2,1)} %pad_maximum_fusion.6), calls=%async_computation.7 | async-start | bytes 5242880 | tf_op jit(solution)/shard_map/all_to_all | solution.py:165
  1206.6 87.7 %collective-permute-start.85 = (bf16[128,512]{0,1:T(8,128)(2,1)}, bf16[128,512]{0,1:T(8,128)(2,1)}, u32[]{:S(2)}, u32[]{:S(2)}) collective-permute-start(bf16[128,512]{0,1:T(8,128)(2,1)} %bitcast.274), channel_id=1, source_target_pairs={{0,1},{1,2},{2,3},{3,0},{4,5},{5,6},{6,7},{7,4},{8,9},{9,10},{10,1... | collective-permute-start | bytes 393224 | tf_op jit(solution)/shard_map/ppermute | solution.py:177
  1207.9 90.6 %collective-permute-start.86 = (bf16[128,512]{0,1:T(8,128)(2,1)}, bf16[128,512]{0,1:T(8,128)(2,1)}, u32[]{:S(2)}, u32[]{:S(2)}) collective-permute-start(bf16[128,512]{0,1:T(8,128)(2,1)} %bitcast.744), channel_id=1, source_target_pairs={{0,2},{1,3},{2,0},{3,1},{4,6},{5,7},{6,4},{7,5},{8,10},{9,11},{10,... | collective-permute-start | bytes 393224 | tf_op jit(solution)/shard_map/ppermute | solution.py:177
  1210.4 88.1 %collective-permute-start.87 = (bf16[128,512]{0,1:T(8,128)(2,1)}, bf16[128,512]{0,1:T(8,128)(2,1)}, u32[]{:S(2)}, u32[]{:S(2)}) collective-permute-start(bf16[128,512]{0,1:T(8,128)(2,1)} %bitcast.743), channel_id=1, source_target_pairs={{0,3},{1,0},{2,1},{3,2},{4,7},{5,4},{6,5},{7,6},{8,11},{9,8},{10,9... | collective-permute-start | bytes 393224 | tf_op jit(solution)/shard_map/ppermute | solution.py:177
  (255 other events, 4182.1 us)
Sparse Core Ops, SparseCore 0:
  38.8 73.1 all-gather.6
  114.9 158.0 all-gather.8
  313.4 131.4 all-gather.10
  447.7 134.2 all-gather.12
  914.2 52.0 all-gather.14
  1031.5 62.9 all-gather.16
  1097.9 57.4 reduce-scatter.2
  1159.2 66.6 reduce-scatter.4
